TPU v7x, 512 devices: a whole 4x4x16 slice. The times are simulated.
512 devices in a mesh: tm: 64 (over z, y), rows: 8 (over x, core).
Axes of the slice: x: 4, y: 4, z: 16, core: 2. Of those that a mesh axis runs over, the one named last changes fastest.
Arguments:
- features: bfloat16 [256, 224, 16, 256], P('tm', 'rows'), as said below
- clip_ids: int32 [256], P('tm'), may hold values from 0 to 63, as said below
- frame_valid: int32 [256], P('tm'), may hold values from 0 to 1, as said below
- norm_gain: float32 [256], replicated, may hold values from 0.1 to 1.9
- norm_bias: float32 [256], replicated, may hold values from -3 to 3
- conv_weight: bfloat16 [3, 3, 3, 256, 256], P(None, None, None, 'rows'), may hold values from -0.078125 to 0.078125
- down_weight: bfloat16 [3, 3, 256, 256], P(None, None, 'rows'), may hold values from -0.125 to 0.125
Outputs:
- reduced: bfloat16 [256, 112, 8, 256], P('tm', 'rows')
Inputs may be any that keep to these rules, and one draw needn't show every extreme that they name: `clip_ids`: each of the 64 clips holds 2 to 6 consecutive frames, one exactly 6; the index never falls along time. `frame_valid`: a padding frame is the last frame of its clip, never its first. `features`: activations.
All inputs are finite; a program needn't handle non-finite values.
Results may differ from a plain program's by a relative error of at most 0.0051.
Values may be sent and summed in bfloat16 or wider, within the bound.
No kernel may reach another device: no remote copies, remote signals or barrier semaphores. Data moves between devices by JAX's collectives and lax.ppermute only.
A program may use at most 64 MiB of HBM per device.

v0:
```python
import jax
import jax.numpy as jnp
from jax import lax
from jax.sharding import PartitionSpec as P

GROUPS = 32


def carried_in(value, axis, join, neutral, backward):
    count, mine = (lax.axis_size(axis), lax.axis_index(axis))
    pieces = jax.tree.map(lambda part: lax.all_gather(part, axis), value)
    if backward:
        pieces = jax.tree.map(lambda part: part[::-1], pieces)
        mine = count - 1 - mine
    running = jax.tree.map(
        lambda part, zero: jnp.full_like(part, 0) + jnp.asarray(zero, part.dtype), value, neutral
    )

    def turn(position, running):
        longer = join(running, jax.tree.map(lambda part: part[position], pieces))
        return jax.tree.map(lambda new, old: jnp.where(position < mine, new, old), longer, running)

    return lax.fori_loop(0, count - 1, turn, running)


def shifted(value, axis, steps):
    count = lax.axis_size(axis)
    first, last = (max(0, -steps), min(count, count - steps))
    return lax.ppermute(value, axis, [(source, source + steps) for source in range(first, last)])


def padded_2(block, sides, width):
    for axis, dim in sides:
        count = lax.axis_size(axis)
        forward = [(i, i + 1) for i in range(count - 1)]
        backward = [(target, source) for source, target in forward]
        low = lax.ppermute(
            lax.slice_in_dim(block, block.shape[dim] - width, None, axis=dim), axis, forward
        )
        high = lax.ppermute(lax.slice_in_dim(block, 0, width, axis=dim), axis, backward)
        block = jnp.concatenate([low, block, high], axis=dim)
    return block


def activate(block, mean_val, inv_std, frame_weight, gain_vec, bias_vec):
    frames, height, across, channels = block.shape
    groups = mean_val.shape[1]
    grouped = block.astype(jnp.float32).reshape(frames, height, across, groups, channels // groups)
    scaled = (grouped - mean_val[:, None, None, :, None]) * inv_std[:, None, None, :, None]
    scaled = scaled.reshape(frames, height, across, channels) * gain_vec + bias_vec
    return (jax.nn.silu(scaled) * frame_weight[:, None, None, None]).astype(jnp.bfloat16)


def local_stats(block, valid_f, groups):
    frames, height, across, channels = block.shape
    grouped = block.astype(jnp.float32).reshape(frames, height * across, groups, channels // groups)
    first_sum = jnp.sum(grouped, axis=(1, 3))
    square_sum = jnp.sum(grouped * grouped, axis=(1, 3))
    sums = jnp.stack([first_sum, square_sum], axis=-1) * valid_f[:, None, None]
    counts = valid_f * float(height * across * (channels // groups))
    return (sums, counts)


def finish_stats(sums_fg, counts_f):
    safe = jnp.maximum(counts_f, 1.0)[:, None]
    mean_val = sums_fg[..., 0] / safe
    spread = jnp.maximum(sums_fg[..., 1] / safe - mean_val * mean_val, 0.0)
    return (mean_val, lax.rsqrt(spread + 1e-05))


def conv_part(columns, masks, weight_piece):
    frames = masks.shape[1]
    height = columns.shape[1] - 2
    channels = weight_piece.shape[3]
    width_out = weight_piece.shape[4]
    total = jnp.zeros((frames, height, columns.shape[2], width_out), jnp.float32)
    for tap_time in range(3):
        partial_sum = jnp.zeros_like(total)
        for tap_row in range(3):
            patch = columns[tap_time : tap_time + frames, tap_row : tap_row + height]
            kernel = weight_piece[tap_time, tap_row].reshape(3 * channels, width_out)
            partial_sum = partial_sum + jnp.einsum(
                "frwc,cn->frwn", patch, kernel, preferred_element_type=jnp.float32
            )
        total = total + masks[tap_time][:, None, None, None] * partial_sum
    return total


def down_part(dcolumns, weight_piece):
    height_out = (dcolumns.shape[1] - 1) // 2
    channels = weight_piece.shape[2]
    width_out = weight_piece.shape[3]
    total = jnp.zeros((dcolumns.shape[0], height_out, dcolumns.shape[2], width_out), jnp.float32)
    for tap_row in range(3):
        patch = dcolumns[:, tap_row : tap_row + 2 * height_out - 1 : 2]
        kernel = weight_piece[tap_row].reshape(3 * channels, width_out)
        total = total + jnp.einsum(
            "frwc,cn->frwn", patch, kernel, preferred_element_type=jnp.float32
        )
    return total


def conv_columns_of(padded, across):
    return jnp.concatenate([padded[:, :, tap : tap + across] for tap in range(3)], axis=-1)


def down_columns_of(extended, across):
    return jnp.concatenate(
        [extended[:, :, tap : tap + across - 1 : 2] for tap in range(3)], axis=-1
    )


def join_spans(earlier_span, later_span):
    early_first, early_last, early_heads, early_headn, early_tails, early_tailn = earlier_span
    late_first, late_last, late_heads, late_headn, late_tails, late_tailn = later_span
    early_empty = early_first < 0.0
    late_empty = late_first < 0.0
    head_more = jnp.logical_and(early_first == early_last, late_first == early_last)
    tail_more = jnp.logical_and(late_first == late_last, early_last == late_first)
    joined_first = jnp.where(early_empty, late_first, early_first)
    joined_last = jnp.where(late_empty, early_last, late_last)
    head_sums = jnp.where(
        early_empty, late_heads, early_heads + jnp.where(head_more, late_heads, 0.0)
    )
    head_count = jnp.where(
        early_empty, late_headn, early_headn + jnp.where(head_more, late_headn, 0.0)
    )
    tail_sums = jnp.where(
        late_empty, early_tails, late_tails + jnp.where(tail_more, early_tails, 0.0)
    )
    tail_count = jnp.where(
        late_empty, early_tailn, late_tailn + jnp.where(tail_more, early_tailn, 0.0)
    )
    return (joined_first, joined_last, head_sums, head_count, tail_sums, tail_count)


def join_reversed(earlier_span, later_span):
    return join_spans(later_span, earlier_span)


def body(features, clip_ids, frame_valid, norm_gain, norm_bias, conv_weight, down_weight):
    frames, height, across, channels = features.shape
    highest = lax.Precision.HIGHEST
    valid_f = frame_valid.astype(jnp.float32)
    ids_f = clip_ids.astype(jnp.float32)
    ids_wire = (ids_f + 1.0).astype(jnp.bfloat16)
    sums, counts = local_stats(features, valid_f, GROUPS)
    band = lax.psum(sums, "rows")
    counts_full = counts * float(lax.axis_size("rows"))
    first_id = ids_f[0]
    last_id = ids_f[-1]
    at_first = (ids_f == first_id).astype(jnp.float32)
    at_last = (ids_f == last_id).astype(jnp.float32)
    element = (
        first_id,
        last_id,
        jnp.einsum("f,fgk->gk", at_first, band, precision=highest),
        jnp.sum(at_first * counts_full),
        jnp.einsum("f,fgk->gk", at_last, band, precision=highest),
        jnp.sum(at_last * counts_full),
    )
    zero_sums = jnp.zeros(band.shape[1:], jnp.float32)
    identity = (
        jnp.float32(-1.0),
        jnp.float32(-1.0),
        zero_sums,
        jnp.float32(0.0),
        zero_sums,
        jnp.float32(0.0),
    )
    before = carried_in(element, "tm", join_spans, identity, False)
    after = carried_in(element, "tm", join_reversed, identity, True)
    same_clip = (ids_f[:, None] == ids_f[None, :]).astype(jnp.float32)
    from_before = (ids_f == before[1]).astype(jnp.float32)
    from_after = (ids_f == after[0]).astype(jnp.float32)
    frame_s = jnp.einsum("fh,hgk->fgk", same_clip, band, precision=highest)
    frame_s = (
        frame_s + from_before[:, None, None] * before[4] + from_after[:, None, None] * after[2]
    )
    frame_n = (
        jnp.dot(same_clip, counts_full, precision=highest)
        + from_before * before[5]
        + from_after * after[3]
    )
    mean_val, inv_std = finish_stats(frame_s, frame_n)
    normed = activate(features, mean_val, inv_std, valid_f, norm_gain, norm_bias)
    prev_h, prev_ids = shifted((normed[-2:], ids_wire[-2:]), "tm", 1)
    all_ids = jnp.concatenate([prev_ids.astype(jnp.float32), ids_wire.astype(jnp.float32)])
    masks = jnp.stack(
        [
            (all_ids[tap : tap + frames] == all_ids[2 : 2 + frames]).astype(jnp.float32)
            for tap in range(3)
        ]
    )
    six_frames = jnp.concatenate([prev_h, normed], axis=0)
    haloed = padded_2(six_frames, (("rows", 1),), 1)
    padded = jnp.pad(haloed, ((0, 0), (0, 0), (1, 1), (0, 0)))
    conv_full, down_full = (
        lax.all_gather(conv_weight, "rows", axis=3, tiled=True),
        lax.all_gather(down_weight, "rows", axis=2, tiled=True),
    )
    conv = conv_part(conv_columns_of(padded, across), masks, conv_full)
    mixed = (valid_f[:, None, None, None] * (features.astype(jnp.float32) + conv)).astype(
        jnp.bfloat16
    )
    below_row = shifted(mixed[:, :1], "rows", -1)
    extended = jnp.pad(
        jnp.concatenate([mixed, below_row], axis=1), ((0, 0), (0, 0), (0, 1), (0, 0))
    )
    reduced = down_part(down_columns_of(extended, across), down_full)
    return reduced.astype(jnp.bfloat16)


def solution(mesh):
    return jax.shard_map(
        body,
        mesh=mesh,
        in_specs=(
            P("tm", "rows", None, None),
            P("tm"),
            P("tm"),
            P(),
            P(),
            P(None, None, None, "rows", None),
            P(None, None, "rows", None),
        ),
        out_specs=P("tm", "rows", None, None),
        check_vma=False,
    )
```

profile of v0, /device:TPU:1, one launch (start us, length us, event | category | flops | bytes accessed | tf_op | source)
XLA Modules:
  0.0 1119.5 jit_solution(11368167877779802042)
XLA Ops:
  6.6 0.7 convert_element_type.53
  7.3 1.3 dynamic-slice
  8.7 1.3 fusion.55
  9.9 2.6 fusion.41
  12.6 4.0 collective-permute-start
  17.4 1.4 convert_reduce_fusion
  19.3 15.9 %psum.7 = f32[4,32,2]{1,0,2:T(4,128)S(1)} all-reduce(f32[4,32,2]{1,0,2:T(4,128)S(1)} %maximum_multiply_fusion), channel_id=1, replica_groups=mesh['tm'=64,'rows'=8] {'rows'}, use_global_device_ids=true, to_apply=%region_4.0 | all-reduce | flops 256 | bytes 2048 | tf_op jit(solution)/shard_map/psum | solution.py:148
  35.2 1.5 fusion.31
  36.6 1.4 fusion.33
  38.0 0.8 slice_dynamic-update-slice_fusion
  38.8 1.3 dynamic-update-slice.2
  40.1 1.4 dynamic-update-slice.3
  41.5 117.1 %all-reduce.6 = (f32[64]{0:T(128)S(1)}, f32[64]{0:T(128)S(1)}, f32[64]{0:T(128)S(1)}, f32[64]{0:T(128)S(1)}) all-reduce(f32[64]{0:T(128)S(1)} %get-tuple-element.453, f32[64]{0:T(128)S(1)} %slice_dynamic-update-slice_fusion, f32[64]{0:T(128)S(1)} %dynamic-update-slice.3, ...), channel_id=1, replica_groups=mesh['tm'=64,'rows'=8] {'tm'}, use_global_device_ids=true, to_apply=%add.2 | all-reduce | flops 256 | bytes 2048
  158.9 61.4 %all-gather.3 = f32[64,32,2]{1,2,0:T(2,128)S(1)} all-gather(f32[1,32,2]{1,2,0:T(2,128)S(1)} %bitcast.171), channel_id=3, replica_groups=mesh['tm'=64,'rows'=8] {'tm'}, dimensions={0}, use_global_device_ids=true | all-gather | bytes 16640 | tf_op jit(solution)/shard_map/all_gather | solution.py:11
  220.3 356.4 %while.37 = (s32[]{:T(128)}, f32[]{:T(128)}, f32[32,2]{0,1:T(2,128)S(1)}, f32[]{:T(128)}, s32[]{:T(128)}, /*index=5*/f32[64]{0:T(128)S(1)}, f32[64,32,2]{1,2,0:T...) while((s32[]{:T(128)}, f32[]{:T(128)}, ...), condition=%wide.region_10.11_spmd.clone, body=%wide.region_9.10_spmd.clone.sunk | while | flops 334 | bytes 1054 | solution.py:23
  223.5 0.7 dynamic_slice.81
  240.4 0.7 dynamic_slice.81
  246.1 0.7 dynamic_slice.81
  576.7 62.2 %all-gather.2 = f32[64,32,2]{1,2,0:T(2,128)S(1)} all-gather(f32[1,32,2]{1,2,0:T(2,128)S(1)} %bitcast.170), channel_id=2, replica_groups=mesh['tm'=64,'rows'=8] {'tm'}, dimensions={0}, use_global_device_ids=true | all-gather | bytes 16640 | tf_op jit(solution)/shard_map/all_gather | solution.py:11
  638.9 350.6 %while.36 = (s32[]{:T(128)}, f32[]{:T(128)}, f32[32,2]{0,1:T(2,128)S(1)}, f32[]{:T(128)}, s32[]{:T(128)}, /*index=5*/f32[64]{0:T(128)S(1)}, f32[64]{0:T(128)S(1)...) while((s32[]{:T(128)}, f32[]{:T(128)}, ...), condition=%wide.region_7.8_spmd.clone, body=%wide.region_6.7_spmd.clone.sunk | while | flops 334 | bytes 1054 | solution.py:23
  990.5 0.7 fusion.16
  991.3 1.3 collective-permute-start.1
  992.6 5.4 collective-permute-done.1
  998.0 67.1 %collective-permute-start.2 = (bf16[6,1,16,256]{3,2,1,0:T(8,128)(2,1)S(1)}, bf16[6,1,16,256]{3,2,1,0:T(8,128)(2,1)S(1)}, u32[]{:S(2)}, u32[]{:S(2)}) collective-permute-start(bf16[6,1,16,256]{3,2,1,0:T(8,128)(2,1)S(1)} %get-tuple-element.440), channel_id=1, source_target_pairs={{0,1},{1,2},{2,3},{3,4},{4,5},{5,6},{6,7},{8,9},{9,10},{10,11},{11... | collective-permute-start | bytes 147464 | tf_op jit(solution)/shard_map/ppermute | solution.py:37
  1065.1 3.4 collective-permute-start.3
  1068.5 2.0 collective-permute-done.3
  1070.6 1.2 select_maximum_fusion
  1071.8 0.8 fusion.53
  1072.6 2.3 pad_maximum_fusion
  1074.9 2.4 fusion.52
  1077.3 0.9 copy-done
  1078.2 0.9 fusion.56
  1079.1 0.9 fusion.57
  1080.0 0.9 fusion.58
  1080.9 0.9 fusion.59
  1081.8 0.9 fusion.60
  1082.7 0.9 fusion.61
  1083.5 0.9 fusion.62
  1084.4 0.9 fusion.63
  1085.3 1.7 fusion.18
  1087.0 1.9 collective-permute-start.4
  1088.9 11.2 %all-gather.9.cloned.1.call-done = bf16[3,3,256,256]{3,2,1,0:T(8,128)(2,1)} async-done(((bf16[3,3,32,256]{3,2,1,0:T(8,128)(2,1)}), bf16[3,3,256,256]{3,2,1,0:T(8,128)(2,1)}) %all-gather.9.cloned.1.call-update) | async-done | bytes 1179664 | tf_op jit(solution)/shard_map/all_gather | solution.py:200
  1100.1 2.3 fusion.54
  1102.5 1.3 slice.152
  1103.8 1.3 slice.153
  1105.1 4.4 slice.154
  1109.5 1.2 pad_maximum_fusion.1
  1111.6 1.0 fusion.20
  (559 shorter events, 239.5 us)
Async XLA Ops:
  6.5 983.2 %copy-start.5 = (s32[4]{0:T(128)S(1)}, s32[4]{0:T(128)}, u32[]{:S(2)}) copy-start(s32[4]{0:T(128)} %param.12) | copy-start | bytes 52
  6.5 982.9 %copy-start.8 = (s32[4]{0:T(128)S(1)}, s32[4]{0:T(128)}, u32[]{:S(2)}) copy-start(s32[4]{0:T(128)} %param.13) | copy-start | bytes 52
  6.5 984.0 %copy-start.1 = (bf16[4,28,16,256]{3,2,1,0:T(8,128)(2,1)S(1)}, bf16[4,28,16,256]{3,2,1,0:T(8,128)(2,1)}, u32[]{:S(2)}) copy-start(bf16[4,28,16,256]{3,2,1,0:T(8,128)(2,1)} %param.11) | copy-start | bytes 2752516
  6.5 984.0 %copy-start.7 = (f32[256]{0:T(256)S(1)}, f32[256]{0:T(256)}, u32[]{:S(2)}) copy-start(f32[256]{0:T(256)} %param.14) | copy-start | bytes 3076
  6.5 984.0 %copy-start.6 = (f32[256]{0:T(256)S(1)}, f32[256]{0:T(256)}, u32[]{:S(2)}) copy-start(f32[256]{0:T(256)} %param.15) | copy-start | bytes 3076
  6.5 1068.3 %all-gather.7.cloned.1.call-start = ((), (), s32[]{:S(2)}) async-start(), calls=%async_computation | async-start | bytes 3981312 | tf_op jit(solution)/shard_map/all_gather | solution.py:199
  12.6 977.1 %collective-permute-start = (bf16[2]{0:T(256)(128)(2,1)S(1)}, bf16[2]{0:T(256)(128)(2,1)S(1)}, u32[]{:S(2)}, u32[]{:S(2)}) collective-permute-start(bf16[2]{0:T(256)(128)(2,1)S(1)} %slice.121), channel_id=1, source_target_pairs={{0,8},{8,16},{16,24},{24,32},{32,40},{40,48},{48,56},{56,64},{64,7... | collective-permute-start | bytes 20 | tf_op jit(solution)/shard_map/ppermute | solution.py:29
  16.7 1083.5 %all-gather.9.cloned.1.call-start = ((), (), s32[]{:S(2)}) async-start(), calls=%async_computation.1 | async-start | bytes 1327104 | tf_op jit(solution)/shard_map/all_gather | solution.py:200
  991.3 6.7 collective-permute-start.1
  998.0 70.5 %collective-permute-start.2 = (bf16[6,1,16,256]{3,2,1,0:T(8,128)(2,1)S(1)}, bf16[6,1,16,256]{3,2,1,0:T(8,128)(2,1)S(1)}, u32[]{:S(2)}, u32[]{:S(2)}) collective-permute-start(bf16[6,1,16,256]{3,2,1,0:T(8,128)(2,1)S(1)} %get-tuple-element.440), channel_id=1, source_target_pairs={{0,1},{1,2},{2,3},{3,4},{4,5},{5,6},{6,7},{8,9},{9,10},{10,11},{11... | collective-permute-start | bytes 147464 | tf_op jit(solution)/shard_map/ppermute | solution.py:37
  1065.1 5.4 collective-permute-start.3
  1074.9 3.3 copy-start
  1087.0 15.4 %collective-permute-start.4 = (bf16[4,1,16,256]{3,2,1,0:T(8,128)(2,1)S(1)}, bf16[4,1,16,256]{3,2,1,0:T(8,128)(2,1)S(1)}, u32[]{:S(2)}, u32[]{:S(2)}) collective-permute-start(bf16[4,1,16,256]{3,2,1,0:T(8,128)(2,1)S(1)} %slice.175), channel_id=1, source_target_pairs={{1,0},{2,1},{3,2},{4,3},{5,4},{6,5},{7,6},{9,8},{10,9},{11,10},{12... | collective-permute-start | bytes 98312 | tf_op jit(solution)/shard_map/ppermute | solution.py:29
  1105.1 5.6 copy-start.3
  1109.5 1.5 copy-start.4
  1110.6 1.0 copy-start.2
Sparse Core Ops, SparseCore 0:
  16.8 41.9 all-gather.6
  1068.7 31.4 all-gather.8
where the time goes:
time: 1130 us; the launch traced here: 1120 us
  loops' own time  469 us (42%)
  blocking collectives  257 us (23%)
  local copies, waits for them, and re-layouts  256 us (23%)
  starting transfers between devices  77.8 us (7%)
  waiting for transfers between devices  18.6 us (2%)
  other arithmetic  13.8 us (1%)
  between operations  13.8 us (1%)
  matrix products  13.7 us (1%)
    another operation x2, loops' own time, carried_in(): return lax.fori_loop(0, count - 1, turn, running)  469 us
    dynamic_slice x378, local copies, waits for them, and re-layouts, turn(): longer = join(running, jax.tree.map(lambda part: part[position], pieces))  235 us
    all_gather x2, blocking collectives, carried_in(): pieces = jax.tree.map(lambda part: lax.all_gather(part, axis), value)  124 us
    unnamed x1, blocking collectives  117 us
    ppermute x1, starting transfers between devices, padded_2(): lax.ppermute(lax.slice_in_dim(block, block.shape[dim] - width, None, axis...  67.1 us
  transfers between devices with their start and end apart: 7, of which 3 were waited for; matrix products, arithmetic and copies ran while one was open for 24% of the time, Pallas kernels for 0%

commit v1 on v0

v1 whole, which is shorter than its diff:
```python
import jax
import jax.numpy as jnp
from jax import lax
from jax.experimental import pallas as pl
from jax.experimental.pallas import tpu as pltpu
from jax.sharding import PartitionSpec as P

GROUPS = 32
ID_LANE = 64
VALID_LANE = 65
BLOCK = 4
F32 = jnp.float32
BF16 = jnp.bfloat16


def shifted(value, axis, steps):
    count = lax.axis_size(axis)
    first, last = (max(0, -steps), min(count, count - steps))
    return lax.ppermute(value, axis, [(source, source + steps) for source in range(first, last)])


def swapped(value, axis, bits):
    return lax.ppermute(value, axis, [(i, i ^ bits) for i in range(lax.axis_size(axis))])


def ring_move(value, axis, cross):
    chips = lax.axis_size(axis) // 2
    pairs = []
    for chip in range(chips):
        for core in range(2):
            source_chip = (chip + (-1 if core == 0 else 1)) % chips
            pairs.append((2 * source_chip + (core ^ cross), 2 * chip + core))
    return lax.ppermute(value, axis, pairs)


def group_lanes(channels, first):
    lane = lax.broadcasted_iota(jnp.int32, (channels, 128), 1)
    group = lax.broadcasted_iota(jnp.int32, (channels, 128), 0) // (channels // GROUPS) + first
    return (lane == group).astype(F32)


def exact_dot(lhs, rhs):
    return lax.dot_general(
        lhs,
        rhs,
        (((1,), (0,)), ((), ())),
        precision=lax.Precision.HIGHEST,
        preferred_element_type=F32,
    )


def pack_kernel(
    place, ids, valid, feat, plain, gain, bias, cross, swap, table, params, kept
):
    frames, height, across, channels = feat.shape
    taps, slice_in, _ = plain.shape
    for message in (cross, swap):
        message[0:taps] = plain[...]
    for core in range(2):

        @pl.when(place[0] % 2 == core)
        def _(core=core):
            first_rows = feat[:, 0:2].reshape(frames, slice_in, channels)
            last_rows = feat[:, height - 2 :].reshape(frames, slice_in, channels)
            cross[taps:] = last_rows if core else first_rows
            swap[taps:] = first_rows if core else last_rows

    kept[...] = feat[...]
    params[0:1, :] = gain[...]
    params[1:2, :] = bias[...]

    first, second = [], []
    for f in range(frames):
        block = feat[f].astype(F32).reshape(height * across, channels)
        first.append(jnp.sum(block, axis=0, keepdims=True))
        second.append(jnp.sum(block * block, axis=0, keepdims=True))
    rows = exact_dot(
        jnp.concatenate(first + first, axis=0), group_lanes(channels, 0)
    ) + exact_dot(jnp.concatenate(second + second, axis=0), group_lanes(channels, GROUPS))
    lane = lax.broadcasted_iota(jnp.int32, (1, 128), 1)
    for at in range(2 * frames):
        weight = valid[at % frames].astype(F32)
        row = rows[at : at + 1, :] * weight
        row = jnp.where(lane == ID_LANE, ids[at % frames].astype(F32) + 1.0, row)
        table[at : at + 1, :] = jnp.where(lane == VALID_LANE, weight, row)


def pack_call(place, clip_ids, frame_valid, features, plain, gain, bias):
    frames, channels = features.shape[0], features.shape[-1]
    taps, slice_in, _ = plain.shape
    vmem = pl.BlockSpec(memory_space=pltpu.VMEM)
    return pl.pallas_call(
        pack_kernel,
        out_shape=(
            jax.ShapeDtypeStruct((taps + frames, slice_in, channels), BF16),
            jax.ShapeDtypeStruct((taps + frames, slice_in, channels), BF16),
            jax.ShapeDtypeStruct((2 * frames, 128), F32),
            jax.ShapeDtypeStruct((8, channels), F32),
            jax.ShapeDtypeStruct(features.shape, BF16),
        ),
        in_specs=[pl.BlockSpec(memory_space=pltpu.SMEM)] * 3 + [vmem] * 4,
        out_specs=(vmem,) * 5,
        compiler_params=pltpu.CompilerParams(vmem_limit_bytes=24 << 20),
        name="pack_and_sum",
    )(place, clip_ids, frame_valid, features, plain, gain, bias)


def halo_kernel(place, cross, swap, feat, out):
    frames, height, across, channels = feat.shape
    taps = cross.shape[0] - frames
    out[:, 1 : height + 1] = feat[frames - 2 :]
    for core in range(2):

        @pl.when(place[0] % 2 == core)
        def _(core=core):
            above, below = (swap, cross) if core else (cross, swap)
            rows = above[taps + frames - 2 :].reshape(2, 2, across, channels)
            out[:, 0:1] = rows[:, 1:2]
            out[:, height + 1 :] = below[taps + frames - 2 :].reshape(2, 2, across, channels)


def halo_call(place, cross, swap, feat):
    frames, height, across, channels = feat.shape
    vmem = pl.BlockSpec(memory_space=pltpu.VMEM)
    return pl.pallas_call(
        halo_kernel,
        out_shape=jax.ShapeDtypeStruct((2, height + 3, across, channels), BF16),
        in_specs=[pl.BlockSpec(memory_space=pltpu.SMEM)] + [vmem] * 3,
        out_specs=vmem,
        compiler_params=pltpu.CompilerParams(vmem_limit_bytes=16 << 20),
        name="halo",
    )(place, cross, swap, feat)


def held_places(band):
    chip, core = band // 2, band % 2
    near_chip = (chip + 3 + 2 * core) % 4
    far_chip = (chip + 2) % 4
    return [band, 2 * near_chip + core, 2 * near_chip + 1 - core, 2 * far_chip + core]


def main_kernel(place, block, params, feat, prev, *rest):
    pieces, (out, w_all, hcol, mixed_all, top, bottom, sems) = rest[:8], rest[8:]
    frames, height, across, channels = feat.shape
    taps, slice_in = pieces[0].shape[:2]
    taps_conv = 27

    band = place[0]
    places = held_places(band) + held_places(band + 1 - 2 * (band % 2))
    copies = []
    for at in range(8):
        start = pl.multiple_of(places[at] * slice_in, slice_in)
        source, target = pieces[at].at[0:taps], w_all.at[:, pl.ds(start, slice_in), :]
        copies.append(pltpu.make_async_copy(source, target, sems.at[at]))
    for copy in copies:
        copy.start()

    cross, swap = pieces[2], pieces[4]
    for core in range(2):

        @pl.when(band % 2 == core)
        def _(core=core):
            above, below = (swap, cross) if core else (cross, swap)
            top[...] = above[taps:].reshape(frames, 2, across, channels)[:, 1:2]
            bottom[...] = below[taps:].reshape(frames, 2, across, channels)

    bands = block.shape[1]
    here = place[1] % BLOCK

    def lane_of(rows, at):
        lane = lax.broadcasted_iota(jnp.int32, rows.shape, 1)
        return jnp.sum(jnp.where(lane == at, rows, 0.0), axis=1, keepdims=True)

    own_rows = block[here, 0]
    own_ids = lane_of(own_rows, ID_LANE)
    own_valid = lane_of(own_rows, VALID_LANE)
    total = jnp.zeros((8, 128), F32)
    for device in range(BLOCK):
        table = block[device, 0]
        table_ids = lane_of(table, ID_LANE)
        for sender in range(1, bands):
            table = table + block[device, sender]
        for f in range(2 * frames):
            same = table_ids[f : f + 1] == own_ids
            total = total + jnp.where(same, table[f : f + 1, :], 0.0)
    group = channels // GROUPS
    count = lane_of(total, VALID_LANE) * float(height * across * group)
    safe = jnp.maximum(count, 1.0)
    both = total / safe
    lane_at = lax.broadcasted_iota(jnp.int32, (128, channels), 0)
    group_at = lax.broadcasted_iota(jnp.int32, (128, channels), 1) // group
    mean = exact_dot(both, (lane_at == group_at).astype(F32))
    square = exact_dot(both, (lane_at == group_at + GROUPS).astype(F32))
    variance = jnp.maximum(square - mean * mean, 0.0)
    half_scale = 0.5 * (lax.rsqrt(variance + 1e-05) * params[0:1, :])
    half_bias = 0.5 * params[1:2, :]

    before_own = block[jnp.maximum(here - 1, 0), 0][frames - 2 : frames]
    before_sent = block[BLOCK - 1, 0][2 * frames - 2 : 2 * frames]
    before_rows = jnp.where(here > 0, before_own, before_sent)
    before_ids = lane_of(before_rows, ID_LANE)
    before_valid = lane_of(before_rows, VALID_LANE)

    top_ok = (band > 0).astype(F32)
    bottom_ok = (band < bands - 1).astype(F32)

    def normalise(x, at, weight, j, first, inside=None):
        rows = x.shape[0]
        x = x.astype(F32).reshape(rows * across, channels)
        u = (x - mean[at : at + 1]) * half_scale[at : at + 1] + half_bias
        h = (u + u * jnp.tanh(u)) * weight
        if inside is not None:
            h = jnp.where(jnp.full(h.shape, inside) > 0.0, h, 0.0)
        column = lax.broadcasted_iota(jnp.int32, h.shape, 0) % across
        left = jnp.where(column == 0, 0.0, pltpu.roll(h, 1, 0))
        right = jnp.where(column == across - 1, 0.0, pltpu.roll(h, rows * across - 1, 0))
        shape = (rows, across, channels)
        hcol[j, pl.ds(first, rows), :, 0:channels] = left.astype(BF16).reshape(shape)
        hcol[j, pl.ds(first, rows), :, channels : 2 * channels] = h.astype(BF16).reshape(shape)
        hcol[j, pl.ds(first, rows), :, 2 * channels :] = right.astype(BF16).reshape(shape)

    rows_step = 4
    for j in range(frames + 2):
        at = max(j - 2, 0)
        if j < 2:
            weight = before_valid[j : j + 1]
            source, source_at, shift = prev, j, 1
            normalise(prev[j, 0:1], at, weight, j, 0, top_ok)
            normalise(prev[j, height + 1 :], at, weight, j, height + 1, bottom_ok)
        else:
            weight = own_valid[at : at + 1]
            source, source_at, shift = feat, at, 0
            normalise(top[at], at, weight, j, 0, top_ok)
            normalise(bottom[at], at, weight, j, height + 1, bottom_ok)

        @pl.loop(0, height // rows_step)
        def _(step):
            first = step * rows_step
            x = source[source_at, pl.ds(first + shift, rows_step)]
            normalise(x, at, weight, j, first + 1)

    for copy in copies:
        copy.wait()

    out_rows = height + 1
    lane_parts = channels // 128
    ids_all = [before_ids[f : f + 1] for f in range(2)]
    ids_all = ids_all + [own_ids[f : f + 1] for f in range(frames)]
    for t in range(frames):
        total = None
        for dt in (2, 1, 0):
            part = None
            for dr in range(3):
                lhs = hcol[t + dt, dr : dr + out_rows].reshape(out_rows * across, 3 * channels)
                tap = (dt * 3 + dr) * 3
                rhs = w_all[tap : tap + 3].reshape(3 * channels, channels)
                product = jnp.dot(lhs, rhs, preferred_element_type=F32)
                part = product if part is None else part + product
            if dt == 2:
                total = part
            else:
                total = total + jnp.where(ids_all[t + dt] == ids_all[t + 2], part, 0.0)
        weight = own_valid[t : t + 1]
        body_rows = height * across
        main_rows = feat[t].astype(F32).reshape(body_rows, channels) + total[:body_rows]
        main_rows = (weight * main_rows).astype(BF16).astype(F32)
        main_rows = main_rows.reshape(height // 2, 2, across, channels)
        last_row = bottom[t, 0].astype(F32) + total[body_rows:]
        last_row = (weight * last_row * bottom_ok).astype(BF16).astype(F32)
        for part_at in range(lane_parts):
            lanes = slice(part_at * 128, (part_at + 1) * 128)
            mixed_all[part_at, t, 0 : height // 2] = main_rows[..., lanes]
            mixed_all[part_at, t, height // 2, 0] = last_row[:, lanes]

    half_rows, half_across = height // 2, across // 2
    points = frames * half_rows * half_across
    reduced = None
    for dr in range(3):
        rows_at, parity = (1 if dr == 2 else 0), dr % 2

        def every_second(first):
            columns = pl.ds(first, half_across, 2)
            return jnp.concatenate(
                [
                    mixed_all[at, :, rows_at : rows_at + half_rows, parity, columns, :].reshape(
                        points, 128
                    )
                    for at in range(lane_parts)
                ],
                axis=-1,
            )

        even, odd = every_second(0), every_second(1)
        column = lax.broadcasted_iota(jnp.int32, even.shape, 0) % half_across
        following = jnp.where(column == half_across - 1, 0.0, pltpu.roll(even, points - 1, 0))
        lhs = jnp.concatenate([even, odd, following], axis=-1).astype(BF16)
        tap = taps_conv + dr * 3
        rhs = w_all[tap : tap + 3].reshape(3 * channels, channels)
        product = jnp.dot(lhs, rhs, preferred_element_type=F32)
        reduced = product if reduced is None else reduced + product
    out[...] = reduced.astype(BF16)


def main_call(place, block, params, feat, prev, pieces):
    frames, height, across, channels = feat.shape
    taps = pieces[0].shape[0]
    points = frames * (height // 2) * (across // 2)
    vmem = pl.BlockSpec(memory_space=pltpu.VMEM)
    return pl.pallas_call(
        main_kernel,
        out_shape=jax.ShapeDtypeStruct((points, channels), BF16),
        in_specs=[pl.BlockSpec(memory_space=pltpu.SMEM)]
        + [vmem] * 12,
        out_specs=vmem,
        scratch_shapes=[
            pltpu.VMEM((taps, channels, channels), BF16),
            pltpu.VMEM((frames + 2, height + 3, across, 3 * channels), BF16),
            pltpu.VMEM((channels // 128, frames, height // 2 + 1, 2, across, 128), F32),
            pltpu.VMEM((frames, 1, across, channels), BF16),
            pltpu.VMEM((frames, 2, across, channels), BF16),
            pltpu.SemaphoreType.DMA((8,)),
        ],
        compiler_params=pltpu.CompilerParams(vmem_limit_bytes=28 << 20),
        name="norm_conv_down",
    )(place, block, params, feat, prev, *pieces)


def body(features, clip_ids, frame_valid, norm_gain, norm_bias, conv_weight, down_weight):
    frames, height, across, channels = features.shape
    slice_in = conv_weight.shape[3]
    place = jnp.stack([lax.axis_index("rows"), lax.axis_index("tm")]).astype(jnp.int32)

    bands, times = lax.axis_size("rows"), lax.axis_size("tm")

    plain = jnp.concatenate(
        [
            conv_weight.reshape(27, slice_in, channels),
            down_weight.reshape(9, slice_in, channels),
        ],
        axis=0,
    )
    cross, swap, table, params, feat = pack_call(
        place,
        clip_ids,
        frame_valid,
        features,
        plain,
        norm_gain.reshape(1, channels),
        norm_bias.reshape(1, channels),
    )

    near = ring_move(plain, "rows", 0)
    near_cross = ring_move(cross, "rows", 1)
    other = swapped(swap, "rows", 1)

    half = BLOCK // 2
    pairs = [(at, at + (BLOCK if at % BLOCK >= half else -BLOCK)) for at in range(times)]
    sent = lax.ppermute(table, "tm", [pair for pair in pairs if 0 <= pair[1] < times])
    row = lax.broadcasted_iota(jnp.int32, table.shape, 0)
    rows = jnp.where(row < frames, table, sent)
    size = BLOCK * bands
    groups = [[first + at for at in range(size)] for first in range(0, bands * times, size)]
    block = lax.all_to_all(
        jnp.broadcast_to(rows[None], (size, *rows.shape)),
        ("tm", "rows"),
        0,
        0,
        axis_index_groups=groups,
        tiled=True,
    ).reshape(BLOCK, bands, *rows.shape)

    near, near_cross, other, block = lax.optimization_barrier((near, near_cross, other, block))
    far = ring_move(near, "rows", 0)
    prev = shifted(halo_call(place, near_cross, other, feat), "tm", 1)
    far, prev = lax.optimization_barrier((far, prev))
    pieces = [plain, near, near_cross, far, other]
    pieces = pieces + [swapped(piece, "rows", 1) for piece in (near, near_cross, far)]

    out = main_call(place, block, params, feat, prev, pieces)
    return out.reshape(frames, height // 2, across // 2, channels)


def solution(mesh):
    return jax.shard_map(
        body,
        mesh=mesh,
        in_specs=(
            P("tm", "rows", None, None),
            P("tm"),
            P("tm"),
            P(),
            P(),
            P(None, None, None, "rows", None),
            P(None, None, "rows", None),
        ),
        out_specs=P("tm", "rows", None, None),
        check_vma=False,
    )
```

time: 1130 us -> 72.4 us (0.06)
  the two profiles are of different devices: /device:TPU:1 before, /device:TPU:257 now
where the time goes in v1:
time: 72.4 us; the launch traced here: 72 us
  starting transfers between devices  23.2 us (32%)
  blocking collectives  16.3 us (23%)
  waiting for transfers between devices  16.1 us (22%)
  Pallas kernels  14.1 us (19%)
  other arithmetic  1.35 us (2%)
    all_to_all x1, blocking collectives, body(): lax.all_to_all(jnp.broadcast_to(rows[None], (size, *rows.shape)), ('tm',...  16.3 us
    pallas_call x1, Pallas kernels, main_call(): pl.pallas_call(main_kernel, out_shape=jax.ShapeDtypeStruct((points, chann...  12.5 us
    ppermute x1, waiting for transfers between devices, shifted(): lax.ppermute(value, axis, [(source, source + steps) for source in range(f...  11.8 us
    ppermute x4, starting transfers between devices, swapped(): lax.ppermute(value, axis, [(i, i ^ bits) for i in range(lax.axis_size(axi...  10 us
    ppermute x3, starting transfers between devices, ring_move(): return lax.ppermute(value, axis, pairs)  9.06 us
    ppermute x1, waiting for transfers between devices, body(): lax.ppermute(table, 'tm', [pair for pair in pairs if 0 <= pair[1] < times])  2.71 us
    ppermute x1, starting transfers between devices, shifted(): lax.ppermute(value, axis, [(source, source + steps) for source in range(f...  2.24 us
    ppermute x1, starting transfers between devices, body(): lax.ppermute(table, 'tm', [pair for pair in pairs if 0 <= pair[1] < times])  1.92 us
  transfers between devices with their start and end apart: 9, of which 3 were waited for; matrix products, arithmetic and copies ran while one was open for 0% of the time, Pallas kernels for 1%

profile of v1, /device:TPU:257, one launch (start us, length us, event | category | flops | bytes accessed | tf_op | source)
XLA Modules:
  0.0 72.0 jit_solution(9439471390459417983)
XLA Ops:
  0.0 0.0 copy-start
  0.0 0.1 pad_add_fusion.place
  0.1 0.0 copy-start.2
  0.1 0.0 copy-start.4
  0.1 1.2 %pad_maximum_fusion.plain.rest_0_ = bf16[36,32,256]{2,1,0:T(8,128)(2,1)S(1)} fusion(bf16[9,32,256]{2,1,0:T(8,128)(2,1)} %bitcast.12, bf16[27,32,256]{2,1,0:T(8,128)(2,1)} %bitcast.11), kind=kLoop, calls=%fused_computation | loop fusion | flops 294912 | bytes 1179648 | tf_op jit(solution)/shard_map/concatenate | solution.py:335
  1.3 0.0 copy-start.1
  1.3 0.0 copy-start.3
  1.3 0.1 copy-done
  1.4 0.0 copy-done.2
  1.4 0.0 copy-done.4
  1.4 0.6 copy-done.1
  2.0 0.0 copy-done.3
  2.0 1.1 %pack_and_sum.1 = (bf16[40,32,256]{2,1,0:T(8,128)(2,1)S(1)}, bf16[40,32,256]{2,1,0:T(8,128)(2,1)S(1)}, f32[8,128]{1,0:T(8,128)S(1)}, f32[8,256]{1,0:T(8,128)S(1)}, bf16[4,28,16,256]{3,2,1,0:T(8,128)(2,1)S(1)}) custom-call(s32[2]{0:T(128)S(1)} %pad_add_fusion.place, s32[4]{0:T(128)S(1)} %copy-done.3, s32[4]{0:T(128)S(1)} %copy-done.4, ...), custom_call_target="tpu_custom_call" | custom-call | tf_op jit(solution)/shard_map/pack_and_sum/pallas_call | solution.py:92
  3.1 3.7 %collective-permute-start.1 = (bf16[40,32,256]{2,1,0:T(8,128)(2,1)S(1)}, bf16[40,32,256]{2,1,0:T(8,128)(2,1)S(1)}, u32[]{:S(2)}, u32[]{:S(2)}) collective-permute-start(bf16[40,32,256]{2,1,0:T(8,128)(2,1)S(1)} %get-tuple-element.16), channel_id=1, source_target_pairs={{7,0},{2,1},{1,2},{4,3},{3,4},{6,5},{5,6},{0,7},{15,8},{10,9},{9,1... | collective-permute-start | bytes 1966088 | tf_op jit(solution)/shard_map/ppermute | solution.py:33
  6.8 3.0 %collective-permute-start.2 = (bf16[40,32,256]{2,1,0:T(8,128)(2,1)S(1)}, bf16[40,32,256]{2,1,0:T(8,128)(2,1)S(1)}, u32[]{:S(2)}, u32[]{:S(2)}) collective-permute-start(bf16[40,32,256]{2,1,0:T(8,128)(2,1)S(1)} %get-tuple-element.17), channel_id=1, source_target_pairs={{0,1},{1,0},{2,3},{3,2},{4,5},{5,4},{6,7},{7,6},{8,9},{9,8},{10,11... | collective-permute-start | bytes 1966088 | tf_op jit(solution)/shard_map/ppermute | solution.py:23
  9.8 2.5 %collective-permute-start = (bf16[36,32,256]{2,1,0:T(8,128)(2,1)S(1)}, bf16[36,32,256]{2,1,0:T(8,128)(2,1)S(1)}, u32[]{:S(2)}, u32[]{:S(2)}) collective-permute-start(bf16[36,32,256]{2,1,0:T(8,128)(2,1)S(1)} %pad_maximum_fusion.plain.rest_0_), channel_id=1, source_target_pairs={{6,0},{3,1},{0,2},{5,3},{2,4},{7,5},{4,6},{1,7},{14,8},{11,9},{8,1... | collective-permute-start | bytes 1769480 | tf_op jit(solution)/shard_map/ppermute | solution.py:33
  12.3 1.9 %collective-permute-start.3 = (f32[8,128]{1,0:T(8,128)S(1)}, f32[8,128]{1,0:T(8,128)S(1)}, u32[]{:S(2)}, u32[]{:S(2)}) collective-permute-start(f32[8,128]{1,0:T(8,128)S(1)} %get-tuple-element.18), channel_id=1, source_target_pairs={{16,48},{24,56},{32,0},{40,8},{48,80},{56,88},{64,32},{72,40},{80,... | collective-permute-start | bytes 12296 | tf_op jit(solution)/shard_map/ppermute | solution.py:358
  14.2 2.7 %collective-permute-done.3 = f32[8,128]{1,0:T(8,128)S(1)} collective-permute-done((f32[8,128]{1,0:T(8,128)S(1)}, f32[8,128]{1,0:T(8,128)S(1)}, u32[]{:S(2)}, u32[]{:S(2)}) %collective-permute-start.3) | collective-permute-done | bytes 4128 | tf_op jit(solution)/shard_map/ppermute | solution.py:358
  16.9 0.1 broadcast_select_fusion
  17.0 16.3 %all_to_all.5 = f32[32,8,128]{2,1,0:T(8,128)S(1)} all-to-all(f32[32,8,128]{2,1,0:T(8,128)S(1)} %broadcast_in_dim.2), channel_id=1, replica_groups={{0,1,2,3,4,5,6,7,8,9,10,11,12,13,14,15,16,17,18,19,20,21,22,23,24,25,26..., dimensions={0} | all-to-all | bytes 262144 | tf_op jit(solution)/shard_map/all_to_all | solution.py:363
  33.3 0.0 collective-permute-done.rest_1_
  33.3 0.0 collective-permute-done.1.cross.rest_2_
  33.3 0.0 collective-permute-done.2.swap.rest_4_
  33.3 2.9 %collective-permute-start.4 = (bf16[36,32,256]{2,1,0:T(8,128)(2,1)S(1)}, bf16[36,32,256]{2,1,0:T(8,128)(2,1)S(1)}, u32[]{:S(2)}, u32[]{:S(2)}) collective-permute-start(bf16[36,32,256]{2,1,0:T(8,128)(2,1)S(1)} %collective-permute-done.rest_1_), channel_id=1, source_target_pairs={{6,0},{3,1},{0,2},{5,3},{2,4},{7,5},{4,6},{1,7},{14,8},{11,9},{8,1... | collective-permute-start | bytes 1769480 | tf_op jit(solution)/shard_map/ppermute | solution.py:33
  36.2 0.6 halo.1
  36.8 2.2 %collective-permute-start.5 = (bf16[2,31,16,256]{3,2,1,0:T(8,128)(2,1)S(1)}, bf16[2,31,16,256]{3,2,1,0:T(8,128)(2,1)S(1)}, u32[]{:S(2)}, u32[]{:S(2)}) collective-permute-start(bf16[2,31,16,256]{3,2,1,0:T(8,128)(2,1)S(1)} %halo.1), channel_id=1, source_target_pairs={{0,8},{8,16},{16,24},{24,32},{32,40},{40,48},{48,56},{56,64},{64,7... | collective-permute-start | bytes 1523720 | tf_op jit(solution)/shard_map/ppermute | solution.py:19
  39.0 2.2 %collective-permute-start.7 = (bf16[40,32,256]{2,1,0:T(8,128)(2,1)S(1)}, bf16[40,32,256]{2,1,0:T(8,128)(2,1)S(1)}, u32[]{:S(2)}, u32[]{:S(2)}) collective-permute-start(bf16[40,32,256]{2,1,0:T(8,128)(2,1)S(1)} %collective-permute-done.1.cross.rest_2_), channel_id=1, source_target_pairs={{0,1},{1,0},{2,3},{3,2},{4,5},{5,4},{6,7},{7,6},{8,9},{9,8},{10,11... | collective-permute-start | bytes 1966088 | tf_op jit(solution)/shard_map/ppermute | solution.py:23
  41.2 2.1 %collective-permute-start.6 = (bf16[36,32,256]{2,1,0:T(8,128)(2,1)S(1)}, bf16[36,32,256]{2,1,0:T(8,128)(2,1)S(1)}, u32[]{:S(2)}, u32[]{:S(2)}) collective-permute-start(bf16[36,32,256]{2,1,0:T(8,128)(2,1)S(1)} %collective-permute-done.rest_1_), channel_id=1, source_target_pairs={{0,1},{1,0},{2,3},{3,2},{4,5},{5,4},{6,7},{7,6},{8,9},{9,8},{10,11... | collective-permute-start | bytes 1769480 | tf_op jit(solution)/shard_map/ppermute | solution.py:23
  43.4 11.8 %collective-permute-done.5.prev = bf16[2,31,16,256]{3,2,1,0:T(8,128)(2,1)S(1)} collective-permute-done((bf16[2,31,16,256]{3,2,1,0:T(8,128)(2,1)S(1)}, bf16[2,31,16,256]{3,2,1,0:T(8,128)(2,1)S(1)}, u32[]{:S(2)}, u32[]{:S(2)}) %collective-permute-start.5) | collective-permute-done | bytes 507936 | tf_op jit(solution)/shard_map/ppermute | solution.py:19
  55.2 0.0 collective-permute-done.4.rest_3_
  55.2 2.7 %collective-permute-start.8 = (bf16[36,32,256]{2,1,0:T(8,128)(2,1)S(1)}, bf16[36,32,256]{2,1,0:T(8,128)(2,1)S(1)}, u32[]{:S(2)}, u32[]{:S(2)}) collective-permute-start(bf16[36,32,256]{2,1,0:T(8,128)(2,1)S(1)} %collective-permute-done.4.rest_3_), channel_id=1, source_target_pairs={{0,1},{1,0},{2,3},{3,2},{4,5},{5,4},{6,7},{7,6},{8,9},{9,8},{10,11... | collective-permute-start | bytes 1769480 | tf_op jit(solution)/shard_map/ppermute | solution.py:23
  57.9 0.0 collective-permute-done.6.rest_5_
  57.9 0.0 collective-permute-done.7.rest_6_
  57.9 1.6 %collective-permute-done.8.rest_7_ = bf16[36,32,256]{2,1,0:T(8,128)(2,1)S(1)} collective-permute-done((bf16[36,32,256]{2,1,0:T(8,128)(2,1)S(1)}, bf16[36,32,256]{2,1,0:T(8,128)(2,1)S(1)}, u32[]{:S(2)}, u32[]{:S(2)}) %collective-permute-start.8) | collective-permute-done | bytes 589856 | tf_op jit(solution)/shard_map/ppermute | solution.py:23
  59.5 12.5 %norm_conv_down.1 = bf16[448,256]{1,0:T(8,128)(2,1)} custom-call(s32[2]{0:T(128)S(1)} %pad_add_fusion.place, f32[4,8,8,128]{3,2,1,0:T(8,128)S(1)} %bitcast.8, f32[8,256]{1,0:T(8,128)S(1)} %get-tuple-element.20.params, bf16[4,28,16,256]{3,2,1,0:T(8,128)(2,1)S(1)} %get-tuple-element.21.feat, bf16[2,31,16,256]{3,2,1,0:T(8,128)(2,1)S(1)} %collective-permute-done.5.prev, ...), custom_call_target="tpu_custom_call" | custom-call | tf_op jit(solution)/shard_map/norm_conv_down/pallas_call | solution.py:309
  (2 shorter events, 0.0 us)
Async XLA Ops:
  0.0 1.4 %copy-start = (bf16[4,28,16,256]{3,2,1,0:T(8,128)(2,1)S(1)}, bf16[4,28,16,256]{3,2,1,0:T(8,128)(2,1)}, u32[]{:S(2)}) copy-start(bf16[4,28,16,256]{3,2,1,0:T(8,128)(2,1)} %feat.1) | copy-start | bytes 2752516
  0.1 1.3 %copy-start.2 = (f32[256]{0:T(256)S(1)}, f32[256]{0:T(256)}, u32[]{:S(2)}) copy-start(f32[256]{0:T(256)} %param.11) | copy-start | bytes 3076
  0.1 1.3 %copy-start.4 = (s32[4]{0:T(128)S(1)}, s32[4]{0:T(128)}, u32[]{:S(2)}) copy-start(s32[4]{0:T(128)} %valid.1) | copy-start | bytes 52
  1.3 0.7 copy-start.1
  1.3 0.7 copy-start.3
  3.1 30.2 %collective-permute-start.1 = (bf16[40,32,256]{2,1,0:T(8,128)(2,1)S(1)}, bf16[40,32,256]{2,1,0:T(8,128)(2,1)S(1)}, u32[]{:S(2)}, u32[]{:S(2)}) collective-permute-start(bf16[40,32,256]{2,1,0:T(8,128)(2,1)S(1)} %get-tuple-element.16), channel_id=1, source_target_pairs={{7,0},{2,1},{1,2},{4,3},{3,4},{6,5},{5,6},{0,7},{15,8},{10,9},{9,1... | collective-permute-start | bytes 1966088 | tf_op jit(solution)/shard_map/ppermute | solution.py:33
  6.8 26.5 %collective-permute-start.2 = (bf16[40,32,256]{2,1,0:T(8,128)(2,1)S(1)}, bf16[40,32,256]{2,1,0:T(8,128)(2,1)S(1)}, u32[]{:S(2)}, u32[]{:S(2)}) collective-permute-start(bf16[40,32,256]{2,1,0:T(8,128)(2,1)S(1)} %get-tuple-element.17), channel_id=1, source_target_pairs={{0,1},{1,0},{2,3},{3,2},{4,5},{5,4},{6,7},{7,6},{8,9},{9,8},{10,11... | collective-permute-start | bytes 1966088 | tf_op jit(solution)/shard_map/ppermute | solution.py:23
  9.8 23.5 %collective-permute-start = (bf16[36,32,256]{2,1,0:T(8,128)(2,1)S(1)}, bf16[36,32,256]{2,1,0:T(8,128)(2,1)S(1)}, u32[]{:S(2)}, u32[]{:S(2)}) collective-permute-start(bf16[36,32,256]{2,1,0:T(8,128)(2,1)S(1)} %pad_maximum_fusion.plain.rest_0_), channel_id=1, source_target_pairs={{6,0},{3,1},{0,2},{5,3},{2,4},{7,5},{4,6},{1,7},{14,8},{11,9},{8,1... | collective-permute-start | bytes 1769480 | tf_op jit(solution)/shard_map/ppermute | solution.py:33
  12.3 4.6 %collective-permute-start.3 = (f32[8,128]{1,0:T(8,128)S(1)}, f32[8,128]{1,0:T(8,128)S(1)}, u32[]{:S(2)}, u32[]{:S(2)}) collective-permute-start(f32[8,128]{1,0:T(8,128)S(1)} %get-tuple-element.18), channel_id=1, source_target_pairs={{16,48},{24,56},{32,0},{40,8},{48,80},{56,88},{64,32},{72,40},{80,... | collective-permute-start | bytes 12296 | tf_op jit(solution)/shard_map/ppermute | solution.py:358
  33.3 21.9 %collective-permute-start.4 = (bf16[36,32,256]{2,1,0:T(8,128)(2,1)S(1)}, bf16[36,32,256]{2,1,0:T(8,128)(2,1)S(1)}, u32[]{:S(2)}, u32[]{:S(2)}) collective-permute-start(bf16[36,32,256]{2,1,0:T(8,128)(2,1)S(1)} %collective-permute-done.rest_1_), channel_id=1, source_target_pairs={{6,0},{3,1},{0,2},{5,3},{2,4},{7,5},{4,6},{1,7},{14,8},{11,9},{8,1... | collective-permute-start | bytes 1769480 | tf_op jit(solution)/shard_map/ppermute | solution.py:33
  36.8 18.4 %collective-permute-start.5 = (bf16[2,31,16,256]{3,2,1,0:T(8,128)(2,1)S(1)}, bf16[2,31,16,256]{3,2,1,0:T(8,128)(2,1)S(1)}, u32[]{:S(2)}, u32[]{:S(2)}) collective-permute-start(bf16[2,31,16,256]{3,2,1,0:T(8,128)(2,1)S(1)} %halo.1), channel_id=1, source_target_pairs={{0,8},{8,16},{16,24},{24,32},{32,40},{40,48},{48,56},{56,64},{64,7... | collective-permute-start | bytes 1523720 | tf_op jit(solution)/shard_map/ppermute | solution.py:19
  39.0 18.9 %collective-permute-start.7 = (bf16[40,32,256]{2,1,0:T(8,128)(2,1)S(1)}, bf16[40,32,256]{2,1,0:T(8,128)(2,1)S(1)}, u32[]{:S(2)}, u32[]{:S(2)}) collective-permute-start(bf16[40,32,256]{2,1,0:T(8,128)(2,1)S(1)} %collective-permute-done.1.cross.rest_2_), channel_id=1, source_target_pairs={{0,1},{1,0},{2,3},{3,2},{4,5},{5,4},{6,7},{7,6},{8,9},{9,8},{10,11... | collective-permute-start | bytes 1966088 | tf_op jit(solution)/shard_map/ppermute | solution.py:23
  41.2 16.7 %collective-permute-start.6 = (bf16[36,32,256]{2,1,0:T(8,128)(2,1)S(1)}, bf16[36,32,256]{2,1,0:T(8,128)(2,1)S(1)}, u32[]{:S(2)}, u32[]{:S(2)}) collective-permute-start(bf16[36,32,256]{2,1,0:T(8,128)(2,1)S(1)} %collective-permute-done.rest_1_), channel_id=1, source_target_pairs={{0,1},{1,0},{2,3},{3,2},{4,5},{5,4},{6,7},{7,6},{8,9},{9,8},{10,11... | collective-permute-start | bytes 1769480 | tf_op jit(solution)/shard_map/ppermute | solution.py:23
  55.2 4.3 %collective-permute-start.8 = (bf16[36,32,256]{2,1,0:T(8,128)(2,1)S(1)}, bf16[36,32,256]{2,1,0:T(8,128)(2,1)S(1)}, u32[]{:S(2)}, u32[]{:S(2)}) collective-permute-start(bf16[36,32,256]{2,1,0:T(8,128)(2,1)S(1)} %collective-permute-done.4.rest_3_), channel_id=1, source_target_pairs={{0,1},{1,0},{2,3},{3,2},{4,5},{5,4},{6,7},{7,6},{8,9},{9,8},{10,11... | collective-permute-start | bytes 1769480 | tf_op jit(solution)/shard_map/ppermute | solution.py:23

commit v2 on v1

--- a/solution.py
+++ b/solution.py
@@ -49,22 +49,8 @@
     )
 
 
-def pack_kernel(
-    place, ids, valid, feat, plain, gain, bias, cross, swap, table, params, kept
-):
-    frames, height, across, channels = feat.shape
-    taps, slice_in, _ = plain.shape
-    for message in (cross, swap):
-        message[0:taps] = plain[...]
-    for core in range(2):
-
-        @pl.when(place[0] % 2 == core)
-        def _(core=core):
-            first_rows = feat[:, 0:2].reshape(frames, slice_in, channels)
-            last_rows = feat[:, height - 2 :].reshape(frames, slice_in, channels)
-            cross[taps:] = last_rows if core else first_rows
-            swap[taps:] = first_rows if core else last_rows
-
+def pack_kernel(ids, valid, feat, gain, bias, table, params, kept):
+    frames, height, across, channels = feat.shape
     kept[...] = feat[...]
     params[0:1, :] = gain[...]
     params[1:2, :] = bias[...]
@@ -85,51 +71,53 @@
         table[at : at + 1, :] = jnp.where(lane == VALID_LANE, weight, row)
 
 
-def pack_call(place, clip_ids, frame_valid, features, plain, gain, bias):
+def pack_call(clip_ids, frame_valid, features, gain, bias):
     frames, channels = features.shape[0], features.shape[-1]
-    taps, slice_in, _ = plain.shape
     vmem = pl.BlockSpec(memory_space=pltpu.VMEM)
     return pl.pallas_call(
         pack_kernel,
         out_shape=(
-            jax.ShapeDtypeStruct((taps + frames, slice_in, channels), BF16),
-            jax.ShapeDtypeStruct((taps + frames, slice_in, channels), BF16),
             jax.ShapeDtypeStruct((2 * frames, 128), F32),
             jax.ShapeDtypeStruct((8, channels), F32),
             jax.ShapeDtypeStruct(features.shape, BF16),
         ),
-        in_specs=[pl.BlockSpec(memory_space=pltpu.SMEM)] * 3 + [vmem] * 4,
-        out_specs=(vmem,) * 5,
+        in_specs=[pl.BlockSpec(memory_space=pltpu.SMEM)] * 2 + [vmem] * 3,
+        out_specs=(vmem,) * 3,
         compiler_params=pltpu.CompilerParams(vmem_limit_bytes=24 << 20),
-        name="pack_and_sum",
-    )(place, clip_ids, frame_valid, features, plain, gain, bias)
-
-
-def halo_kernel(place, cross, swap, feat, out):
-    frames, height, across, channels = feat.shape
-    taps = cross.shape[0] - frames
-    out[:, 1 : height + 1] = feat[frames - 2 :]
+        name="frame_sums",
+    )(clip_ids, frame_valid, features, gain, bias)
+
+
+def edges_kernel(place, feat, prev, plain, swap, edge):
+    frames, height, across, channels = feat.shape
+    taps, slice_in, _ = plain.shape
+    swap[0:taps] = plain[...]
     for core in range(2):
 
         @pl.when(place[0] % 2 == core)
         def _(core=core):
-            above, below = (swap, cross) if core else (cross, swap)
-            rows = above[taps + frames - 2 :].reshape(2, 2, across, channels)
-            out[:, 0:1] = rows[:, 1:2]
-            out[:, height + 1 :] = below[taps + frames - 2 :].reshape(2, 2, across, channels)
-
-
-def halo_call(place, cross, swap, feat):
-    frames, height, across, channels = feat.shape
+            for source, first, count in ((prev, 0, 2), (feat, 2, frames)):
+                first_rows = source[:, 0:2].reshape(count, slice_in, channels)
+                last_rows = source[:, height - 2 :].reshape(count, slice_in, channels)
+                edge[first : first + count] = last_rows if core else first_rows
+                swap[taps + first : taps + first + count] = first_rows if core else last_rows
+
+
+def edges_call(place, feat, prev, plain):
+    frames, height, across, channels = feat.shape
+    taps, slice_in, _ = plain.shape
     vmem = pl.BlockSpec(memory_space=pltpu.VMEM)
     return pl.pallas_call(
-        halo_kernel,
-        out_shape=jax.ShapeDtypeStruct((2, height + 3, across, channels), BF16),
+        edges_kernel,
+        out_shape=(
+            jax.ShapeDtypeStruct((taps + frames + 2, slice_in, channels), BF16),
+            jax.ShapeDtypeStruct((frames + 2, slice_in, channels), BF16),
+        ),
         in_specs=[pl.BlockSpec(memory_space=pltpu.SMEM)] + [vmem] * 3,
-        out_specs=vmem,
+        out_specs=(vmem,) * 2,
         compiler_params=pltpu.CompilerParams(vmem_limit_bytes=16 << 20),
-        name="halo",
-    )(place, cross, swap, feat)
+        name="edge_rows",
+    )(place, feat, prev, plain)
 
 
 def held_places(band):
@@ -139,7 +127,7 @@
     return [band, 2 * near_chip + core, 2 * near_chip + 1 - core, 2 * far_chip + core]
 
 
-def main_kernel(place, block, params, feat, prev, *rest):
+def main_kernel(place, block, params, feat, prev, edge, *rest):
     pieces, (out, w_all, hcol, mixed_all, top, bottom, sems) = rest[:8], rest[8:]
     frames, height, across, channels = feat.shape
     taps, slice_in = pieces[0].shape[:2]
@@ -155,14 +143,15 @@
     for copy in copies:
         copy.start()
 
-    cross, swap = pieces[2], pieces[4]
+    swap = pieces[4]
     for core in range(2):
 
         @pl.when(band % 2 == core)
         def _(core=core):
-            above, below = (swap, cross) if core else (cross, swap)
-            top[...] = above[taps:].reshape(frames, 2, across, channels)[:, 1:2]
-            bottom[...] = below[taps:].reshape(frames, 2, across, channels)
+            swap_rows = swap[taps:].reshape(frames + 2, 2, across, channels)
+            edge_rows = edge[...].reshape(frames + 2, 2, across, channels)
+            top[...] = (swap_rows if core else edge_rows)[:, 1:2]
+            bottom[...] = edge_rows if core else swap_rows
 
     bands = block.shape[1]
     here = place[1] % BLOCK
@@ -224,19 +213,17 @@
         at = max(j - 2, 0)
         if j < 2:
             weight = before_valid[j : j + 1]
-            source, source_at, shift = prev, j, 1
-            normalise(prev[j, 0:1], at, weight, j, 0, top_ok)
-            normalise(prev[j, height + 1 :], at, weight, j, height + 1, bottom_ok)
+            source, source_at = prev, j
         else:
             weight = own_valid[at : at + 1]
-            source, source_at, shift = feat, at, 0
-            normalise(top[at], at, weight, j, 0, top_ok)
-            normalise(bottom[at], at, weight, j, height + 1, bottom_ok)
+            source, source_at = feat, at
+        normalise(top[j], at, weight, j, 0, top_ok)
+        normalise(bottom[j], at, weight, j, height + 1, bottom_ok)
 
         @pl.loop(0, height // rows_step)
         def _(step):
             first = step * rows_step
-            x = source[source_at, pl.ds(first + shift, rows_step)]
+            x = source[source_at, pl.ds(first, rows_step)]
             normalise(x, at, weight, j, first + 1)
 
     for copy in copies:
@@ -265,7 +252,7 @@
         main_rows = feat[t].astype(F32).reshape(body_rows, channels) + total[:body_rows]
         main_rows = (weight * main_rows).astype(BF16).astype(F32)
         main_rows = main_rows.reshape(height // 2, 2, across, channels)
-        last_row = bottom[t, 0].astype(F32) + total[body_rows:]
+        last_row = bottom[2 + t, 0].astype(F32) + total[body_rows:]
         last_row = (weight * last_row * bottom_ok).astype(BF16).astype(F32)
         for part_at in range(lane_parts):
             lanes = slice(part_at * 128, (part_at + 1) * 128)
@@ -301,7 +288,7 @@
     out[...] = reduced.astype(BF16)
 
 
-def main_call(place, block, params, feat, prev, pieces):
+def main_call(place, block, params, feat, prev, edge, pieces):
     frames, height, across, channels = feat.shape
     taps = pieces[0].shape[0]
     points = frames * (height // 2) * (across // 2)
@@ -310,19 +297,19 @@
         main_kernel,
         out_shape=jax.ShapeDtypeStruct((points, channels), BF16),
         in_specs=[pl.BlockSpec(memory_space=pltpu.SMEM)]
-        + [vmem] * 12,
+        + [vmem] * 13,
         out_specs=vmem,
         scratch_shapes=[
             pltpu.VMEM((taps, channels, channels), BF16),
             pltpu.VMEM((frames + 2, height + 3, across, 3 * channels), BF16),
             pltpu.VMEM((channels // 128, frames, height // 2 + 1, 2, across, 128), F32),
-            pltpu.VMEM((frames, 1, across, channels), BF16),
-            pltpu.VMEM((frames, 2, across, channels), BF16),
+            pltpu.VMEM((frames + 2, 1, across, channels), BF16),
+            pltpu.VMEM((frames + 2, 2, across, channels), BF16),
             pltpu.SemaphoreType.DMA((8,)),
         ],
         compiler_params=pltpu.CompilerParams(vmem_limit_bytes=28 << 20),
         name="norm_conv_down",
-    )(place, block, params, feat, prev, *pieces)
+    )(place, block, params, feat, prev, edge, *pieces)
 
 
 def body(features, clip_ids, frame_valid, norm_gain, norm_bias, conv_weight, down_weight):
@@ -332,6 +319,7 @@
 
     bands, times = lax.axis_size("rows"), lax.axis_size("tm")
 
+    prev = shifted(features[frames - 2 :], "tm", 1)
     plain = jnp.concatenate(
         [
             conv_weight.reshape(27, slice_in, channels),
@@ -339,25 +327,31 @@
         ],
         axis=0,
     )
-    cross, swap, table, params, feat = pack_call(
-        place,
+    near = ring_move(plain, "rows", 0)
+    table, params, feat = pack_call(
         clip_ids,
         frame_valid,
         features,
-        plain,
         norm_gain.reshape(1, channels),
         norm_bias.reshape(1, channels),
     )
-
-    near = ring_move(plain, "rows", 0)
-    near_cross = ring_move(cross, "rows", 1)
-    other = swapped(swap, "rows", 1)
+    near_cross = ring_move(plain, "rows", 1)
 
     half = BLOCK // 2
     pairs = [(at, at + (BLOCK if at % BLOCK >= half else -BLOCK)) for at in range(times)]
     sent = lax.ppermute(table, "tm", [pair for pair in pairs if 0 <= pair[1] < times])
     row = lax.broadcasted_iota(jnp.int32, table.shape, 0)
     rows = jnp.where(row < frames, table, sent)
+
+    near, prev, rows = lax.optimization_barrier((near, prev, rows))
+    far = ring_move(near, "rows", 0)
+    near_swapped = swapped(near, "rows", 1)
+    swap, edge = edges_call(place, feat, prev, plain)
+    other = swapped(swap, "rows", 1)
+    edge = ring_move(edge, "rows", 1)
+    near_cross, rows = lax.optimization_barrier((near_cross, rows))
+    cross_swapped = swapped(near_cross, "rows", 1)
+
     size = BLOCK * bands
     groups = [[first + at for at in range(size)] for first in range(0, bands * times, size)]
     block = lax.all_to_all(
@@ -369,14 +363,11 @@
         tiled=True,
     ).reshape(BLOCK, bands, *rows.shape)
 
-    near, near_cross, other, block = lax.optimization_barrier((near, near_cross, other, block))
-    far = ring_move(near, "rows", 0)
-    prev = shifted(halo_call(place, near_cross, other, feat), "tm", 1)
-    far, prev = lax.optimization_barrier((far, prev))
-    pieces = [plain, near, near_cross, far, other]
-    pieces = pieces + [swapped(piece, "rows", 1) for piece in (near, near_cross, far)]
-
-    out = main_call(place, block, params, feat, prev, pieces)
+    far, block = lax.optimization_barrier((far, block))
+    far_swapped = swapped(far, "rows", 1)
+    pieces = [plain, near, near_cross, far, other, near_swapped, cross_swapped, far_swapped]
+
+    out = main_call(place, block, params, feat, prev, edge, pieces)
     return out.reshape(frames, height // 2, across // 2, channels)
 
 

time: 72.4 us -> 63.8 us (0.88)
  the two profiles are of different devices: /device:TPU:257 before, /device:TPU:1 now
where the time goes in v2:
time: 63.8 us; the launch traced here: 62.8 us
  starting transfers between devices  36.7 us (58%)
  Pallas kernels  15.8 us (25%)
  waiting for transfers between devices  6.2 us (10%)
  local copies, waits for them, and re-layouts  2.48 us (4%)
  other arithmetic  1.37 us (2%)
    ppermute x4, starting transfers between devices, ring_move(): return lax.ppermute(value, axis, pairs)  16.6 us
    pallas_call x1, Pallas kernels, main_call(): pl.pallas_call(main_kernel, out_shape=jax.ShapeDtypeStruct((points, chann...  13.3 us
    ppermute x4, starting transfers between devices, swapped(): lax.ppermute(value, axis, [(i, i ^ bits) for i in range(lax.axis_size(axi...  8.64 us
    all_to_all x1, starting transfers between devices, body(): lax.all_to_all(jnp.broadcast_to(rows[None], (size, *rows.shape)), ('tm',...  6.94 us
    ppermute x1, waiting for transfers between devices, body(): lax.ppermute(table, 'tm', [pair for pair in pairs if 0 <= pair[1] < times])  3.49 us
    ppermute x1, starting transfers between devices, shifted(): lax.ppermute(value, axis, [(source, source + steps) for source in range(f...  3.23 us
    ppermute x4, waiting for transfers between devices, ring_move(): return lax.ppermute(value, axis, pairs)  2.69 us
    unnamed x14, local copies, waits for them, and re-layouts  1.73 us
  transfers between devices with their start and end apart: 11, of which 2 were waited for; matrix products, arithmetic and copies ran while one was open for 1% of the time, Pallas kernels for 4%

profile of v2, /device:TPU:1, one launch (start us, length us, event | category | flops | bytes accessed | tf_op | source)
XLA Modules:
  0.0 62.8 jit_solution(1716403842734260556)
XLA Ops:
  0.0 0.0 copy-start
  0.0 1.2 %pad_maximum_fusion.plain.rest_0_ = bf16[36,32,256]{2,1,0:T(8,128)(2,1)S(1)} fusion(bf16[9,32,256]{2,1,0:T(8,128)(2,1)} %bitcast.12, bf16[27,32,256]{2,1,0:T(8,128)(2,1)} %bitcast.11), kind=kLoop, calls=%fused_computation | loop fusion | flops 294912 | bytes 1179648 | tf_op jit(solution)/shard_map/concatenate | solution.py:323
  1.2 5.2 %collective-permute-start = (bf16[36,32,256]{2,1,0:T(8,128)(2,1)S(1)}, bf16[36,32,256]{2,1,0:T(8,128)(2,1)S(1)}, u32[]{:S(2)}, u32[]{:S(2)}) collective-permute-start(bf16[36,32,256]{2,1,0:T(8,128)(2,1)S(1)} %pad_maximum_fusion.plain.rest_0_), channel_id=1, source_target_pairs={{6,0},{3,1},{0,2},{5,3},{2,4},{7,5},{4,6},{1,7},{14,8},{11,9},{8,1... | collective-permute-start | bytes 1769480 | tf_op jit(solution)/shard_map/ppermute | solution.py:33
  6.4 0.0 copy-done
  6.5 0.0 copy-start.4
  6.5 0.0 copy-start.6
  6.5 3.2 %collective-permute-start.1 = (bf16[2,28,16,256]{3,2,1,0:T(8,128)(2,1)S(1)}, bf16[2,28,16,256]{3,2,1,0:T(8,128)(2,1)S(1)}, u32[]{:S(2)}, u32[]{:S(2)}) collective-permute-start(bf16[2,28,16,256]{3,2,1,0:T(8,128)(2,1)S(1)} %slice.3), channel_id=1, source_target_pairs={{0,8},{8,16},{16,24},{24,32},{32,40},{40,48},{48,56},{56,64},{64,7... | collective-permute-start | bytes 1376264 | tf_op jit(solution)/shard_map/ppermute | solution.py:19
  9.8 3.0 %collective-permute-start.4 = (bf16[36,32,256]{2,1,0:T(8,128)(2,1)S(1)}, bf16[36,32,256]{2,1,0:T(8,128)(2,1)S(1)}, u32[]{:S(2)}, u32[]{:S(2)}) collective-permute-start(bf16[36,32,256]{2,1,0:T(8,128)(2,1)S(1)} %pad_maximum_fusion.plain.rest_0_), channel_id=1, source_target_pairs={{7,0},{2,1},{1,2},{4,3},{3,4},{6,5},{5,6},{0,7},{15,8},{10,9},{9,1... | collective-permute-start | bytes 1769480 | tf_op jit(solution)/shard_map/ppermute | solution.py:33
  12.7 0.0 copy-start.3
  12.8 0.0 copy-start.5
  12.8 0.0 copy-done.4
  12.8 0.0 copy-done.6
  12.8 0.6 %copy-done.3 = f32[256]{0:T(256)S(1)} copy-done((f32[256]{0:T(256)S(1)}, f32[256]{0:T(256)}, u32[]{:S(2)}) %copy-start.3) | copy-done | bytes 1048
  13.4 0.0 copy-done.5
  13.4 1.0 %frame_sums.1 = (f32[8,128]{1,0:T(8,128)S(1)}, f32[8,256]{1,0:T(8,128)S(1)}, bf16[4,28,16,256]{3,2,1,0:T(8,128)(2,1)S(1)}) custom-call(s32[4]{0:T(128)S(1)} %copy-done.5, s32[4]{0:T(128)S(1)} %copy-done.6, bf16[4,28,16,256]{3,2,1,0:T(8,128)(2,1)S(1)} %copy-done, f32[1,256]{1,0:T(1,128)S(1)} %bitcast.9, f32[1,256]{1,0:T(1,128)S(1)} %bitcast.10), custom_call_target="tpu_custom_call" | custom-call | tf_op jit(solution)/shard_map/frame_sums/pallas_call | solution.py:77
  14.4 1.3 %collective-permute-start.2 = (f32[8,128]{1,0:T(8,128)S(1)}, f32[8,128]{1,0:T(8,128)S(1)}, u32[]{:S(2)}, u32[]{:S(2)}) collective-permute-start(f32[8,128]{1,0:T(8,128)S(1)} %get-tuple-element.17), channel_id=1, source_target_pairs={{16,48},{24,56},{32,0},{40,8},{48,80},{56,88},{64,32},{72,40},{80,... | collective-permute-start | bytes 12296 | tf_op jit(solution)/shard_map/ppermute | solution.py:342
  15.7 3.5 %collective-permute-done.2 = f32[8,128]{1,0:T(8,128)S(1)} collective-permute-done((f32[8,128]{1,0:T(8,128)S(1)}, f32[8,128]{1,0:T(8,128)S(1)}, u32[]{:S(2)}, u32[]{:S(2)}) %collective-permute-start.2) | collective-permute-done | bytes 4128 | tf_op jit(solution)/shard_map/ppermute | solution.py:342
  19.2 0.1 broadcast_select_fusion
  19.3 0.0 collective-permute-done.1.prev
  19.3 0.0 collective-permute-done.rest_1_
  19.3 4.9 %collective-permute-start.3 = (bf16[36,32,256]{2,1,0:T(8,128)(2,1)S(1)}, bf16[36,32,256]{2,1,0:T(8,128)(2,1)}, u32[]{:S(2)}, u32[]{:S(2)}) collective-permute-start(bf16[36,32,256]{2,1,0:T(8,128)(2,1)S(1)} %collective-permute-done.rest_1_), channel_id=1, source_target_pairs={{6,0},{3,1},{0,2},{5,3},{2,4},{7,5},{4,6},{1,7},{14,8},{11,9},{8,1... | collective-permute-start | bytes 1769480 | tf_op jit(solution)/shard_map/ppermute | solution.py:33
  24.2 0.0 collective-permute-done.4.rest_2_
  24.2 0.0 copy-start.1
  24.3 0.7 %broadcast_in_dim.2 = f32[32,8,128]{2,1,0:T(8,128)} broadcast(f32[8,128]{1,0:T(8,128)S(1)} %broadcast_select_fusion), dimensions={1,2} | broadcast | bytes 135168 | tf_op jit(solution)/shard_map/broadcast_in_dim | solution.py:358
  25.0 6.9 %all-to-all-start = ((f32[32,8,128]{2,1,0:T(8,128)}), f32[32,8,128]{2,1,0:T(8,128)S(1)}, u32[]{:S(2)}, u32[]{:S(2)}) async-start(f32[32,8,128]{2,1,0:T(8,128)} %broadcast_in_dim.2), calls=%async_computation | async-start | bytes 262144 | tf_op jit(solution)/shard_map/all_to_all | solution.py:357
  31.9 0.1 pad_add_fusion.place
  32.0 1.5 %edge_rows.1 = (bf16[42,32,256]{2,1,0:T(8,128)(2,1)}, bf16[6,32,256]{2,1,0:T(8,128)(2,1)S(1)}) custom-call(s32[2]{0:T(128)S(1)} %pad_add_fusion.place, bf16[4,28,16,256]{3,2,1,0:T(8,128)(2,1)S(1)} %get-tuple-element.23.feat, bf16[2,28,16,256]{3,2,1,0:T(8,128)(2,1)S(1)} %collective-permute-done.1.prev, bf16[36,32,256]{2,1,0:T(8,128)(2,1)S(1)} %pad_maximum_fusion.plain.rest_0_), custom_call_target="tpu_custom_call" | custom-call | tf_op jit(solution)/shard_map/edge_rows/pallas_call | solution.py:110
  33.5 0.0 copy-done.1
  33.5 2.1 %collective-permute-start.6 = (bf16[42,32,256]{2,1,0:T(8,128)(2,1)}, bf16[42,32,256]{2,1,0:T(8,128)(2,1)S(1)}, u32[]{:S(2)}, u32[]{:S(2)}) collective-permute-start(bf16[42,32,256]{2,1,0:T(8,128)(2,1)} %get-tuple-element.28), channel_id=1, source_target_pairs={{0,1},{1,0},{2,3},{3,2},{4,5},{5,4},{6,7},{7,6},{8,9},{9,8},{10,11... | collective-permute-start | bytes 2064392 | tf_op jit(solution)/shard_map/ppermute | solution.py:23
  35.6 2.2 %collective-permute-start.7 = (bf16[36,32,256]{2,1,0:T(8,128)(2,1)S(1)}, bf16[36,32,256]{2,1,0:T(8,128)(2,1)}, u32[]{:S(2)}, u32[]{:S(2)}) collective-permute-start(bf16[36,32,256]{2,1,0:T(8,128)(2,1)S(1)} %collective-permute-done.rest_1_), channel_id=1, source_target_pairs={{0,1},{1,0},{2,3},{3,2},{4,5},{5,4},{6,7},{7,6},{8,9},{9,8},{10,11... | collective-permute-start | bytes 1769480 | tf_op jit(solution)/shard_map/ppermute | solution.py:23
  37.8 2.1 %collective-permute-start.8 = (bf16[36,32,256]{2,1,0:T(8,128)(2,1)}, bf16[36,32,256]{2,1,0:T(8,128)(2,1)}, u32[]{:S(2)}, u32[]{:S(2)}) collective-permute-start(bf16[36,32,256]{2,1,0:T(8,128)(2,1)} %copy-done.1), channel_id=1, source_target_pairs={{0,1},{1,0},{2,3},{3,2},{4,5},{5,4},{6,7},{7,6},{8,9},{9,8},{10,11... | collective-permute-start | bytes 1769480 | tf_op jit(solution)/shard_map/ppermute | solution.py:23
  40.0 0.0 all-to-all-done
  40.0 0.0 collective-permute-done.3.rest_3_
  40.0 2.2 %collective-permute-start.9 = (bf16[36,32,256]{2,1,0:T(8,128)(2,1)}, bf16[36,32,256]{2,1,0:T(8,128)(2,1)S(1)}, u32[]{:S(2)}, u32[]{:S(2)}) collective-permute-start(bf16[36,32,256]{2,1,0:T(8,128)(2,1)} %collective-permute-done.3.rest_3_), channel_id=1, source_target_pairs={{0,1},{1,0},{2,3},{3,2},{4,5},{5,4},{6,7},{7,6},{8,9},{9,8},{10,11... | collective-permute-start | bytes 1769480 | tf_op jit(solution)/shard_map/ppermute | solution.py:23
  42.2 3.5 %collective-permute-start.5 = (bf16[6,32,256]{2,1,0:T(8,128)(2,1)S(1)}, bf16[6,32,256]{2,1,0:T(8,128)(2,1)S(1)}, u32[]{:S(2)}, u32[]{:S(2)}) collective-permute-start(bf16[6,32,256]{2,1,0:T(8,128)(2,1)S(1)} %get-tuple-element.25), channel_id=1, source_target_pairs={{7,0},{2,1},{1,2},{4,3},{3,4},{6,5},{5,6},{0,7},{15,8},{10,9},{9,1... | collective-permute-start | bytes 294920 | tf_op jit(solution)/shard_map/ppermute | solution.py:33
  45.7 2.7 %collective-permute-done.5.edge = bf16[6,32,256]{2,1,0:T(8,128)(2,1)S(1)} collective-permute-done((bf16[6,32,256]{2,1,0:T(8,128)(2,1)S(1)}, bf16[6,32,256]{2,1,0:T(8,128)(2,1)S(1)}, u32[]{:S(2)}, u32[]{:S(2)}) %collective-permute-start.5) | collective-permute-done | bytes 98336 | tf_op jit(solution)/shard_map/ppermute | solution.py:33
  48.4 0.0 collective-permute-done.8.rest_6_
  48.4 0.0 collective-permute-done.7.rest_5_
  48.4 0.0 collective-permute-done.6.rest_4_
  48.4 0.0 collective-permute-done.9.rest_7_
  48.4 0.0 copy-start.2
  48.4 1.1 %copy-done.2 = bf16[36,32,256]{2,1,0:T(8,128)(2,1)S(1)} copy-done((bf16[36,32,256]{2,1,0:T(8,128)(2,1)S(1)}, bf16[36,32,256]{2,1,0:T(8,128)(2,1)}, u32[]{:S(2)}) %copy-start.2) | copy-done | bytes 589848
  49.5 13.3 %norm_conv_down.1 = bf16[448,256]{1,0:T(8,128)(2,1)} custom-call(s32[2]{0:T(128)S(1)} %pad_add_fusion.place, f32[4,8,8,128]{3,2,1,0:T(8,128)S(1)} %bitcast.8, f32[8,256]{1,0:T(8,128)S(1)} %get-tuple-element.22.params, bf16[4,28,16,256]{3,2,1,0:T(8,128)(2,1)S(1)} %get-tuple-element.23.feat, bf16[2,28,16,256]{3,2,1,0:T(8,128)(2,1)S(1)} %collective-permute-done.1.prev, ...), custom_call_target="tpu_custom_call" | custom-call | tf_op jit(solution)/shard_map/norm_conv_down/pallas_call | solution.py:296
  (2 shorter events, 0.0 us)
Async XLA Ops:
  0.0 6.4 %copy-start = (bf16[4,28,16,256]{3,2,1,0:T(8,128)(2,1)S(1)}, bf16[4,28,16,256]{3,2,1,0:T(8,128)(2,1)}, u32[]{:S(2)}) copy-start(bf16[4,28,16,256]{3,2,1,0:T(8,128)(2,1)} %feat.1) | copy-start | bytes 2752516
  1.2 18.1 %collective-permute-start = (bf16[36,32,256]{2,1,0:T(8,128)(2,1)S(1)}, bf16[36,32,256]{2,1,0:T(8,128)(2,1)S(1)}, u32[]{:S(2)}, u32[]{:S(2)}) collective-permute-start(bf16[36,32,256]{2,1,0:T(8,128)(2,1)S(1)} %pad_maximum_fusion.plain.rest_0_), channel_id=1, source_target_pairs={{6,0},{3,1},{0,2},{5,3},{2,4},{7,5},{4,6},{1,7},{14,8},{11,9},{8,1... | collective-permute-start | bytes 1769480 | tf_op jit(solution)/shard_map/ppermute | solution.py:33
  6.5 6.3 %copy-start.4 = (f32[256]{0:T(256)S(1)}, f32[256]{0:T(256)}, u32[]{:S(2)}) copy-start(f32[256]{0:T(256)} %param.11) | copy-start | bytes 3076
  6.5 6.3 %copy-start.6 = (s32[4]{0:T(128)S(1)}, s32[4]{0:T(128)}, u32[]{:S(2)}) copy-start(s32[4]{0:T(128)} %valid.1) | copy-start | bytes 52
  6.5 12.8 %collective-permute-start.1 = (bf16[2,28,16,256]{3,2,1,0:T(8,128)(2,1)S(1)}, bf16[2,28,16,256]{3,2,1,0:T(8,128)(2,1)S(1)}, u32[]{:S(2)}, u32[]{:S(2)}) collective-permute-start(bf16[2,28,16,256]{3,2,1,0:T(8,128)(2,1)S(1)} %slice.3), channel_id=1, source_target_pairs={{0,8},{8,16},{16,24},{24,32},{32,40},{40,48},{48,56},{56,64},{64,7... | collective-permute-start | bytes 1376264 | tf_op jit(solution)/shard_map/ppermute | solution.py:19
  9.8 14.5 %collective-permute-start.4 = (bf16[36,32,256]{2,1,0:T(8,128)(2,1)S(1)}, bf16[36,32,256]{2,1,0:T(8,128)(2,1)S(1)}, u32[]{:S(2)}, u32[]{:S(2)}) collective-permute-start(bf16[36,32,256]{2,1,0:T(8,128)(2,1)S(1)} %pad_maximum_fusion.plain.rest_0_), channel_id=1, source_target_pairs={{7,0},{2,1},{1,2},{4,3},{3,4},{6,5},{5,6},{0,7},{15,8},{10,9},{9,1... | collective-permute-start | bytes 1769480 | tf_op jit(solution)/shard_map/ppermute | solution.py:33
  12.7 0.7 %copy-start.3 = (f32[256]{0:T(256)S(1)}, f32[256]{0:T(256)}, u32[]{:S(2)}) copy-start(f32[256]{0:T(256)} %param.10) | copy-start | bytes 3076
  12.8 0.7 %copy-start.5 = (s32[4]{0:T(128)S(1)}, s32[4]{0:T(128)}, u32[]{:S(2)}) copy-start(s32[4]{0:T(128)} %ids.1) | copy-start | bytes 52
  14.4 4.8 %collective-permute-start.2 = (f32[8,128]{1,0:T(8,128)S(1)}, f32[8,128]{1,0:T(8,128)S(1)}, u32[]{:S(2)}, u32[]{:S(2)}) collective-permute-start(f32[8,128]{1,0:T(8,128)S(1)} %get-tuple-element.17), channel_id=1, source_target_pairs={{16,48},{24,56},{32,0},{40,8},{48,80},{56,88},{64,32},{72,40},{80,... | collective-permute-start | bytes 12296 | tf_op jit(solution)/shard_map/ppermute | solution.py:342
  19.3 20.7 %collective-permute-start.3 = (bf16[36,32,256]{2,1,0:T(8,128)(2,1)S(1)}, bf16[36,32,256]{2,1,0:T(8,128)(2,1)}, u32[]{:S(2)}, u32[]{:S(2)}) collective-permute-start(bf16[36,32,256]{2,1,0:T(8,128)(2,1)S(1)} %collective-permute-done.rest_1_), channel_id=1, source_target_pairs={{6,0},{3,1},{0,2},{5,3},{2,4},{7,5},{4,6},{1,7},{14,8},{11,9},{8,1... | collective-permute-start | bytes 1769480 | tf_op jit(solution)/shard_map/ppermute | solution.py:33
  24.2 9.2 %copy-start.1 = (bf16[36,32,256]{2,1,0:T(8,128)(2,1)}, bf16[36,32,256]{2,1,0:T(8,128)(2,1)S(1)}, u32[]{:S(2)}) copy-start(bf16[36,32,256]{2,1,0:T(8,128)(2,1)S(1)} %collective-permute-done.4.rest_2_) | copy-start | bytes 1769476
  25.0 15.0 %all-to-all-start = ((f32[32,8,128]{2,1,0:T(8,128)}), f32[32,8,128]{2,1,0:T(8,128)S(1)}, u32[]{:S(2)}, u32[]{:S(2)}) async-start(f32[32,8,128]{2,1,0:T(8,128)} %broadcast_in_dim.2), calls=%async_computation | async-start | bytes 262144 | tf_op jit(solution)/shard_map/all_to_all | solution.py:357
  33.5 14.9 %collective-permute-start.6 = (bf16[42,32,256]{2,1,0:T(8,128)(2,1)}, bf16[42,32,256]{2,1,0:T(8,128)(2,1)S(1)}, u32[]{:S(2)}, u32[]{:S(2)}) collective-permute-start(bf16[42,32,256]{2,1,0:T(8,128)(2,1)} %get-tuple-element.28), channel_id=1, source_target_pairs={{0,1},{1,0},{2,3},{3,2},{4,5},{5,4},{6,7},{7,6},{8,9},{9,8},{10,11... | collective-permute-start | bytes 2064392 | tf_op jit(solution)/shard_map/ppermute | solution.py:23
  35.6 12.8 %collective-permute-start.7 = (bf16[36,32,256]{2,1,0:T(8,128)(2,1)S(1)}, bf16[36,32,256]{2,1,0:T(8,128)(2,1)}, u32[]{:S(2)}, u32[]{:S(2)}) collective-permute-start(bf16[36,32,256]{2,1,0:T(8,128)(2,1)S(1)} %collective-permute-done.rest_1_), channel_id=1, source_target_pairs={{0,1},{1,0},{2,3},{3,2},{4,5},{5,4},{6,7},{7,6},{8,9},{9,8},{10,11... | collective-permute-start | bytes 1769480 | tf_op jit(solution)/shard_map/ppermute | solution.py:23
  37.8 10.6 %collective-permute-start.8 = (bf16[36,32,256]{2,1,0:T(8,128)(2,1)}, bf16[36,32,256]{2,1,0:T(8,128)(2,1)}, u32[]{:S(2)}, u32[]{:S(2)}) collective-permute-start(bf16[36,32,256]{2,1,0:T(8,128)(2,1)} %copy-done.1), channel_id=1, source_target_pairs={{0,1},{1,0},{2,3},{3,2},{4,5},{5,4},{6,7},{7,6},{8,9},{9,8},{10,11... | collective-permute-start | bytes 1769480 | tf_op jit(solution)/shard_map/ppermute | solution.py:23
  40.0 8.4 %collective-permute-start.9 = (bf16[36,32,256]{2,1,0:T(8,128)(2,1)}, bf16[36,32,256]{2,1,0:T(8,128)(2,1)S(1)}, u32[]{:S(2)}, u32[]{:S(2)}) collective-permute-start(bf16[36,32,256]{2,1,0:T(8,128)(2,1)} %collective-permute-done.3.rest_3_), channel_id=1, source_target_pairs={{0,1},{1,0},{2,3},{3,2},{4,5},{5,4},{6,7},{7,6},{8,9},{9,8},{10,11... | collective-permute-start | bytes 1769480 | tf_op jit(solution)/shard_map/ppermute | solution.py:23
  42.2 6.2 %collective-permute-start.5 = (bf16[6,32,256]{2,1,0:T(8,128)(2,1)S(1)}, bf16[6,32,256]{2,1,0:T(8,128)(2,1)S(1)}, u32[]{:S(2)}, u32[]{:S(2)}) collective-permute-start(bf16[6,32,256]{2,1,0:T(8,128)(2,1)S(1)} %get-tuple-element.25), channel_id=1, source_target_pairs={{7,0},{2,1},{1,2},{4,3},{3,4},{6,5},{5,6},{0,7},{15,8},{10,9},{9,1... | collective-permute-start | bytes 294920 | tf_op jit(solution)/shard_map/ppermute | solution.py:33
  48.4 1.1 %copy-start.2 = (bf16[36,32,256]{2,1,0:T(8,128)(2,1)S(1)}, bf16[36,32,256]{2,1,0:T(8,128)(2,1)}, u32[]{:S(2)}) copy-start(bf16[36,32,256]{2,1,0:T(8,128)(2,1)} %copy-done.1) | copy-start | bytes 1769476

commit v3 on v2

--- a/solution.py
+++ b/solution.py
@@ -83,15 +83,16 @@
         ),
         in_specs=[pl.BlockSpec(memory_space=pltpu.SMEM)] * 2 + [vmem] * 3,
         out_specs=(vmem,) * 3,
-        compiler_params=pltpu.CompilerParams(vmem_limit_bytes=24 << 20),
+        compiler_params=pltpu.CompilerParams(vmem_limit_bytes=10 << 20),
         name="frame_sums",
     )(clip_ids, frame_valid, features, gain, bias)
 
 
-def edges_kernel(place, feat, prev, plain, swap, edge):
+def swap_kernel(place, feat, prev, plain, near, near_cross, swap, edge):
     frames, height, across, channels = feat.shape
     taps, slice_in, _ = plain.shape
-    swap[0:taps] = plain[...]
+    for at, piece in enumerate((plain, near, near_cross)):
+        swap[at * taps : (at + 1) * taps] = piece[...]
     for core in range(2):
 
         @pl.when(place[0] % 2 == core)
@@ -100,24 +101,25 @@
                 first_rows = source[:, 0:2].reshape(count, slice_in, channels)
                 last_rows = source[:, height - 2 :].reshape(count, slice_in, channels)
                 edge[first : first + count] = last_rows if core else first_rows
-                swap[taps + first : taps + first + count] = first_rows if core else last_rows
-
-
-def edges_call(place, feat, prev, plain):
+                to_core = first_rows if core else last_rows
+                swap[3 * taps + first : 3 * taps + first + count] = to_core
+
+
+def swap_call(place, feat, prev, plain, near, near_cross):
     frames, height, across, channels = feat.shape
     taps, slice_in, _ = plain.shape
     vmem = pl.BlockSpec(memory_space=pltpu.VMEM)
     return pl.pallas_call(
-        edges_kernel,
+        swap_kernel,
         out_shape=(
-            jax.ShapeDtypeStruct((taps + frames + 2, slice_in, channels), BF16),
+            jax.ShapeDtypeStruct((3 * taps + frames + 2, slice_in, channels), BF16),
             jax.ShapeDtypeStruct((frames + 2, slice_in, channels), BF16),
         ),
-        in_specs=[pl.BlockSpec(memory_space=pltpu.SMEM)] + [vmem] * 3,
+        in_specs=[pl.BlockSpec(memory_space=pltpu.SMEM)] + [vmem] * 5,
         out_specs=(vmem,) * 2,
-        compiler_params=pltpu.CompilerParams(vmem_limit_bytes=16 << 20),
-        name="edge_rows",
-    )(place, feat, prev, plain)
+        compiler_params=pltpu.CompilerParams(vmem_limit_bytes=10 << 20),
+        name="swap_message",
+    )(place, feat, prev, plain, near, near_cross)
 
 
 def held_places(band):
@@ -128,27 +130,29 @@
 
 
 def main_kernel(place, block, params, feat, prev, edge, *rest):
-    pieces, (out, w_all, hcol, mixed_all, top, bottom, sems) = rest[:8], rest[8:]
+    swap, pieces = rest[0], rest[1:6]
+    out, w_all, hcol, mixed_all, top, bottom, sems = rest[6:]
     frames, height, across, channels = feat.shape
     taps, slice_in = pieces[0].shape[:2]
     taps_conv = 27
 
     band = place[0]
     places = held_places(band) + held_places(band + 1 - 2 * (band % 2))
+    sources = list(pieces[:4])
+    sources += [swap.at[at * taps : (at + 1) * taps] for at in range(3)] + [pieces[4]]
     copies = []
     for at in range(8):
         start = pl.multiple_of(places[at] * slice_in, slice_in)
-        source, target = pieces[at].at[0:taps], w_all.at[:, pl.ds(start, slice_in), :]
+        source, target = sources[at], w_all.at[:, pl.ds(start, slice_in), :]
         copies.append(pltpu.make_async_copy(source, target, sems.at[at]))
     for copy in copies:
         copy.start()
 
-    swap = pieces[4]
     for core in range(2):
 
         @pl.when(band % 2 == core)
         def _(core=core):
-            swap_rows = swap[taps:].reshape(frames + 2, 2, across, channels)
+            swap_rows = swap[3 * taps :].reshape(frames + 2, 2, across, channels)
             edge_rows = edge[...].reshape(frames + 2, 2, across, channels)
             top[...] = (swap_rows if core else edge_rows)[:, 1:2]
             bottom[...] = edge_rows if core else swap_rows
@@ -236,13 +240,15 @@
     for t in range(frames):
         total = None
         for dt in (2, 1, 0):
-            part = None
-            for dr in range(3):
-                lhs = hcol[t + dt, dr : dr + out_rows].reshape(out_rows * across, 3 * channels)
-                tap = (dt * 3 + dr) * 3
-                rhs = w_all[tap : tap + 3].reshape(3 * channels, channels)
-                product = jnp.dot(lhs, rhs, preferred_element_type=F32)
-                part = product if part is None else part + product
+            lhs = jnp.concatenate(
+                [
+                    hcol[t + dt, dr : dr + out_rows].reshape(out_rows * across, 3 * channels)
+                    for dr in range(3)
+                ],
+                axis=1,
+            )
+            rhs = w_all[dt * 9 : dt * 9 + 9].reshape(9 * channels, channels)
+            part = jnp.dot(lhs, rhs, preferred_element_type=F32)
             if dt == 2:
                 total = part
             else:
@@ -288,7 +294,7 @@
     out[...] = reduced.astype(BF16)
 
 
-def main_call(place, block, params, feat, prev, edge, pieces):
+def main_call(place, block, params, feat, prev, edge, swap, pieces):
     frames, height, across, channels = feat.shape
     taps = pieces[0].shape[0]
     points = frames * (height // 2) * (across // 2)
@@ -297,7 +303,7 @@
         main_kernel,
         out_shape=jax.ShapeDtypeStruct((points, channels), BF16),
         in_specs=[pl.BlockSpec(memory_space=pltpu.SMEM)]
-        + [vmem] * 13,
+        + [vmem] * 11,
         out_specs=vmem,
         scratch_shapes=[
             pltpu.VMEM((taps, channels, channels), BF16),
@@ -307,9 +313,9 @@
             pltpu.VMEM((frames + 2, 2, across, channels), BF16),
             pltpu.SemaphoreType.DMA((8,)),
         ],
-        compiler_params=pltpu.CompilerParams(vmem_limit_bytes=28 << 20),
+        compiler_params=pltpu.CompilerParams(vmem_limit_bytes=24 << 20),
         name="norm_conv_down",
-    )(place, block, params, feat, prev, edge, *pieces)
+    )(place, block, params, feat, prev, edge, swap, *pieces)
 
 
 def body(features, clip_ids, frame_valid, norm_gain, norm_bias, conv_weight, down_weight):
@@ -345,12 +351,9 @@
 
     near, prev, rows = lax.optimization_barrier((near, prev, rows))
     far = ring_move(near, "rows", 0)
-    near_swapped = swapped(near, "rows", 1)
-    swap, edge = edges_call(place, feat, prev, plain)
-    other = swapped(swap, "rows", 1)
+    swap, edge = swap_call(place, feat, prev, plain, near, near_cross)
+    swap = swapped(swap, "rows", 1)
     edge = ring_move(edge, "rows", 1)
-    near_cross, rows = lax.optimization_barrier((near_cross, rows))
-    cross_swapped = swapped(near_cross, "rows", 1)
 
     size = BLOCK * bands
     groups = [[first + at for at in range(size)] for first in range(0, bands * times, size)]
@@ -363,11 +366,10 @@
         tiled=True,
     ).reshape(BLOCK, bands, *rows.shape)
 
-    far, block = lax.optimization_barrier((far, block))
-    far_swapped = swapped(far, "rows", 1)
-    pieces = [plain, near, near_cross, far, other, near_swapped, cross_swapped, far_swapped]
-
-    out = main_call(place, block, params, feat, prev, edge, pieces)
+    far, block, edge = lax.optimization_barrier((far, block, edge))
+    pieces = [plain, near, near_cross, far, swapped(far, "rows", 1)]
+
+    out = main_call(place, block, params, feat, prev, edge, swap, pieces)
     return out.reshape(frames, height // 2, across // 2, channels)
 
 

time: 63.8 us -> 65.9 us (1.033)
  waiting for transfers between devices: 6.2 us -> 12.9 us
  starting transfers between devices: 36.7 us -> 32 us
  Pallas kernels: 15.8 us -> 16.5 us
    ppermute x1, waiting for transfers between devices: 0.01 us -> 3.6 us  [shifted(): lax.ppermute(value, axis, [(source, source + steps) for source in range(f...]
    ppermute x4, starting transfers between devices: 16.6 us -> 14.6 us  [ring_move(): return lax.ppermute(value, axis, pairs)]
    all_to_all x1, starting transfers between devices: 6.94 us -> 5 us  [body(): lax.all_to_all(jnp.broadcast_to(rows[None], (size, *rows.shape)), ('tm',...]
    ppermute x4 -> x2, waiting for transfers between devices: 0.01 us -> 1.82 us  [swapped(): lax.ppermute(value, axis, [(i, i ^ bits) for i in range(lax.axis_size(axi...]
    slice x1, local copies, waits for them, and re-layouts: 0.03 us -> 1.83 us  [body(): prev = shifted(features[frames - 2:], 'tm', 1)]
    unnamed x14 -> x10, local copies, waits for them, and re-layouts: 1.73 us -> 0.02 us
    all_to_all x1, waiting for transfers between devices: 0.01 us -> 1.4 us  [body(): lax.all_to_all(jnp.broadcast_to(rows[None], (size, *rows.shape)), ('tm',...]
    ppermute x4 -> x2, starting transfers between devices: 8.64 us -> 7.86 us  [swapped(): lax.ppermute(value, axis, [(i, i ^ bits) for i in range(lax.axis_size(axi...]
  transfers between devices with their start and end apart: 11 -> 9, of which waited for: 2 -> 5; matrix products, arithmetic and copies ran while one was open for 1% -> 4% of each run, Pallas kernels for 4% -> 2%
where the time goes in v3:
time: 65.9 us; the launch traced here: 65.4 us
  starting transfers between devices  32 us (49%)
  Pallas kernels  16.5 us (25%)
  waiting for transfers between devices  12.9 us (20%)
  local copies, waits for them, and re-layouts  2.51 us (4%)
  other arithmetic  1.37 us (2%)
    ppermute x4, starting transfers between devices, ring_move(): return lax.ppermute(value, axis, pairs)  14.6 us
    pallas_call x1, Pallas kernels, main_call(): pl.pallas_call(main_kernel, out_shape=jax.ShapeDtypeStruct((points, chann...  13.6 us
    ppermute x2, starting transfers between devices, swapped(): lax.ppermute(value, axis, [(i, i ^ bits) for i in range(lax.axis_size(axi...  7.86 us
    all_to_all x1, starting transfers between devices, body(): lax.all_to_all(jnp.broadcast_to(rows[None], (size, *rows.shape)), ('tm',...  5 us
    ppermute x1, waiting for transfers between devices, shifted(): lax.ppermute(value, axis, [(source, source + steps) for source in range(f...  3.6 us
    ppermute x1, waiting for transfers between devices, body(): lax.ppermute(table, 'tm', [pair for pair in pairs if 0 <= pair[1] < times])  3.41 us
    ppermute x1, starting transfers between devices, shifted(): lax.ppermute(value, axis, [(source, source + steps) for source in range(f...  3.22 us
    ppermute x4, waiting for transfers between devices, ring_move(): return lax.ppermute(value, axis, pairs)  2.69 us
  transfers between devices with their start and end apart: 9, of which 5 were waited for; matrix products, arithmetic and copies ran while one was open for 4% of the time, Pallas kernels for 2%

profile of v3, /device:TPU:1, one launch (start us, length us, event | category | flops | bytes accessed | tf_op | source)
XLA Modules:
  0.0 65.4 jit_solution(12516821214402925524)
XLA Ops:
  0.0 0.0 copy-start
  0.0 0.0 copy-start.3
  0.0 0.0 copy-start.4
  0.0 0.0 copy-start.1
  0.0 0.0 copy-start.2
  0.0 1.2 %pad_maximum_fusion.plain.rest_1_ = bf16[36,32,256]{2,1,0:T(8,128)(2,1)S(1)} fusion(bf16[9,32,256]{2,1,0:T(8,128)(2,1)} %bitcast.12, bf16[27,32,256]{2,1,0:T(8,128)(2,1)} %bitcast.11), kind=kLoop, calls=%fused_computation | loop fusion | flops 294912 | bytes 1179648 | tf_op jit(solution)/shard_map/concatenate | solution.py:329
  1.2 5.2 %collective-permute-start = (bf16[36,32,256]{2,1,0:T(8,128)(2,1)S(1)}, bf16[36,32,256]{2,1,0:T(8,128)(2,1)S(1)}, u32[]{:S(2)}, u32[]{:S(2)}) collective-permute-start(bf16[36,32,256]{2,1,0:T(8,128)(2,1)S(1)} %pad_maximum_fusion.plain.rest_1_), channel_id=1, source_target_pairs={{6,0},{3,1},{0,2},{5,3},{2,4},{7,5},{4,6},{1,7},{14,8},{11,9},{8,1... | collective-permute-start | bytes 1769480 | tf_op jit(solution)/shard_map/ppermute | solution.py:33
  6.5 2.7 %collective-permute-start.4 = (bf16[36,32,256]{2,1,0:T(8,128)(2,1)S(1)}, bf16[36,32,256]{2,1,0:T(8,128)(2,1)S(1)}, u32[]{:S(2)}, u32[]{:S(2)}) collective-permute-start(bf16[36,32,256]{2,1,0:T(8,128)(2,1)S(1)} %pad_maximum_fusion.plain.rest_1_), channel_id=1, source_target_pairs={{7,0},{2,1},{1,2},{4,3},{3,4},{6,5},{5,6},{0,7},{15,8},{10,9},{9,1... | collective-permute-start | bytes 1769480 | tf_op jit(solution)/shard_map/ppermute | solution.py:33
  9.2 1.8 %slice.3 = bf16[2,28,16,256]{3,2,1,0:T(8,128)(2,1)} slice(bf16[4,28,16,256]{3,2,1,0:T(8,128)(2,1)} %feat.1), slice={[2:4], [0:28], [0:16], [0:256]} | slice | bytes 917504 | tf_op jit(solution)/shard_map/slice | solution.py:328
  11.0 3.2 %collective-permute-start.1 = (bf16[2,28,16,256]{3,2,1,0:T(8,128)(2,1)}, bf16[2,28,16,256]{3,2,1,0:T(8,128)(2,1)S(1)}, u32[]{:S(2)}, u32[]{:S(2)}) collective-permute-start(bf16[2,28,16,256]{3,2,1,0:T(8,128)(2,1)} %slice.3), channel_id=1, source_target_pairs={{0,8},{8,16},{16,24},{24,32},{32,40},{40,48},{48,56},{56,64},{64,7... | collective-permute-start | bytes 1376264 | tf_op jit(solution)/shard_map/ppermute | solution.py:19
  14.2 0.0 copy-done
  14.2 0.0 copy-done.3
  14.2 0.0 copy-done.4
  14.3 0.0 copy-done.1
  14.3 0.0 copy-done.2
  14.3 1.0 %frame_sums.1 = (f32[8,128]{1,0:T(8,128)S(1)}, f32[8,256]{1,0:T(8,128)S(1)}, bf16[4,28,16,256]{3,2,1,0:T(8,128)(2,1)S(1)}) custom-call(s32[4]{0:T(128)S(1)} %copy-done.3, s32[4]{0:T(128)S(1)} %copy-done.4, bf16[4,28,16,256]{3,2,1,0:T(8,128)(2,1)S(1)} %copy-done, f32[1,256]{1,0:T(1,128)S(1)} %bitcast.9, f32[1,256]{1,0:T(1,128)S(1)} %bitcast.10), custom_call_target="tpu_custom_call" | custom-call | tf_op jit(solution)/shard_map/frame_sums/pallas_call | solution.py:77
  15.3 1.3 %collective-permute-start.2 = (f32[8,128]{1,0:T(8,128)S(1)}, f32[8,128]{1,0:T(8,128)S(1)}, u32[]{:S(2)}, u32[]{:S(2)}) collective-permute-start(f32[8,128]{1,0:T(8,128)S(1)} %get-tuple-element.16), channel_id=1, source_target_pairs={{16,48},{24,56},{32,0},{40,8},{48,80},{56,88},{64,32},{72,40},{80,... | collective-permute-start | bytes 12296 | tf_op jit(solution)/shard_map/ppermute | solution.py:348
  16.6 0.1 pad_add_fusion.place
  16.7 3.4 %collective-permute-done.2 = f32[8,128]{1,0:T(8,128)S(1)} collective-permute-done((f32[8,128]{1,0:T(8,128)S(1)}, f32[8,128]{1,0:T(8,128)S(1)}, u32[]{:S(2)}, u32[]{:S(2)}) %collective-permute-start.2) | collective-permute-done | bytes 4128 | tf_op jit(solution)/shard_map/ppermute | solution.py:348
  20.1 0.1 broadcast_select_fusion
  20.2 3.6 %collective-permute-done.1.prev = bf16[2,28,16,256]{3,2,1,0:T(8,128)(2,1)S(1)} collective-permute-done((bf16[2,28,16,256]{3,2,1,0:T(8,128)(2,1)}, bf16[2,28,16,256]{3,2,1,0:T(8,128)(2,1)S(1)}, u32[]{:S(2)}, u32[]{:S(2)}) %collective-permute-start.1) | collective-permute-done | bytes 458784 | tf_op jit(solution)/shard_map/ppermute | solution.py:19
  23.8 0.0 collective-permute-done.near.rest_2_
  23.8 0.0 collective-permute-done.4.near_cross.rest_3_
  23.8 1.9 %swap_message.1 = (bf16[114,32,256]{2,1,0:T(8,128)(2,1)}, bf16[6,32,256]{2,1,0:T(8,128)(2,1)S(1)}) custom-call(s32[2]{0:T(128)S(1)} %pad_add_fusion.place, bf16[4,28,16,256]{3,2,1,0:T(8,128)(2,1)S(1)} %get-tuple-element.19.feat, bf16[2,28,16,256]{3,2,1,0:T(8,128)(2,1)S(1)} %collective-permute-done.1.prev, ...), custom_call_target="tpu_custom_call" | custom-call | tf_op jit(solution)/shard_map/swap_message/pallas_call | solution.py:112
  25.7 5.6 %collective-permute-start.6 = (bf16[114,32,256]{2,1,0:T(8,128)(2,1)}, bf16[114,32,256]{2,1,0:T(8,128)(2,1)}, u32[]{:S(2)}, u32[]{:S(2)}) collective-permute-start(bf16[114,32,256]{2,1,0:T(8,128)(2,1)} %get-tuple-element.25), channel_id=1, source_target_pairs={{0,1},{1,0},{2,3},{3,2},{4,5},{5,4},{6,7},{7,6},{8,9},{9,8},{10,11... | collective-permute-start | bytes 5603336 | tf_op jit(solution)/shard_map/ppermute | solution.py:23
  31.3 3.2 %collective-permute-start.3 = (bf16[36,32,256]{2,1,0:T(8,128)(2,1)S(1)}, bf16[36,32,256]{2,1,0:T(8,128)(2,1)}, u32[]{:S(2)}, u32[]{:S(2)}) collective-permute-start(bf16[36,32,256]{2,1,0:T(8,128)(2,1)S(1)} %collective-permute-done.near.rest_2_), channel_id=1, source_target_pairs={{6,0},{3,1},{0,2},{5,3},{2,4},{7,5},{4,6},{1,7},{14,8},{11,9},{8,1... | collective-permute-start | bytes 1769480 | tf_op jit(solution)/shard_map/ppermute | solution.py:33
  34.4 0.7 %broadcast_in_dim.2 = f32[32,8,128]{2,1,0:T(8,128)} broadcast(f32[8,128]{1,0:T(8,128)S(1)} %broadcast_select_fusion), dimensions={1,2} | broadcast | bytes 135168 | tf_op jit(solution)/shard_map/broadcast_in_dim | solution.py:361
  35.1 5.0 %all-to-all-start = ((f32[32,8,128]{2,1,0:T(8,128)}), f32[32,8,128]{2,1,0:T(8,128)S(1)}, u32[]{:S(2)}, u32[]{:S(2)}) async-start(f32[32,8,128]{2,1,0:T(8,128)} %broadcast_in_dim.2), calls=%async_computation | async-start | bytes 262144 | tf_op jit(solution)/shard_map/all_to_all | solution.py:360
  40.1 3.5 %collective-permute-start.5 = (bf16[6,32,256]{2,1,0:T(8,128)(2,1)S(1)}, bf16[6,32,256]{2,1,0:T(8,128)(2,1)S(1)}, u32[]{:S(2)}, u32[]{:S(2)}) collective-permute-start(bf16[6,32,256]{2,1,0:T(8,128)(2,1)S(1)} %get-tuple-element.21), channel_id=1, source_target_pairs={{7,0},{2,1},{1,2},{4,3},{3,4},{6,5},{5,6},{0,7},{15,8},{10,9},{9,1... | collective-permute-start | bytes 294920 | tf_op jit(solution)/shard_map/ppermute | solution.py:33
  43.7 2.7 %collective-permute-done.5.edge = bf16[6,32,256]{2,1,0:T(8,128)(2,1)S(1)} collective-permute-done((bf16[6,32,256]{2,1,0:T(8,128)(2,1)S(1)}, bf16[6,32,256]{2,1,0:T(8,128)(2,1)S(1)}, u32[]{:S(2)}, u32[]{:S(2)}) %collective-permute-start.5) | collective-permute-done | bytes 98336 | tf_op jit(solution)/shard_map/ppermute | solution.py:33
  46.3 1.4 %all-to-all-done = f32[32,8,128]{2,1,0:T(8,128)S(1)} async-done(((f32[32,8,128]{2,1,0:T(8,128)}), f32[32,8,128]{2,1,0:T(8,128)S(1)}, u32[]{:S(2)}, u32[]{:S(2)}) %all-to-all-start) | async-done | bytes 131104 | tf_op jit(solution)/shard_map/all_to_all | solution.py:360
  47.7 0.0 collective-permute-done.3.rest_4_
  47.7 2.3 %collective-permute-start.7 = (bf16[36,32,256]{2,1,0:T(8,128)(2,1)}, bf16[36,32,256]{2,1,0:T(8,128)(2,1)S(1)}, u32[]{:S(2)}, u32[]{:S(2)}) collective-permute-start(bf16[36,32,256]{2,1,0:T(8,128)(2,1)} %collective-permute-done.3.rest_4_), channel_id=1, source_target_pairs={{0,1},{1,0},{2,3},{3,2},{4,5},{5,4},{6,7},{7,6},{8,9},{9,8},{10,11... | collective-permute-start | bytes 1769480 | tf_op jit(solution)/shard_map/ppermute | solution.py:23
  50.1 1.8 %collective-permute-done.7.rest_5_ = bf16[36,32,256]{2,1,0:T(8,128)(2,1)S(1)} collective-permute-done((bf16[36,32,256]{2,1,0:T(8,128)(2,1)}, bf16[36,32,256]{2,1,0:T(8,128)(2,1)S(1)}, u32[]{:S(2)}, u32[]{:S(2)}) %collective-permute-start.7) | collective-permute-done | bytes 589856 | tf_op jit(solution)/shard_map/ppermute | solution.py:23
  51.9 0.0 collective-permute-done.6.rest_0_
  51.9 13.6 %norm_conv_down.1 = bf16[448,256]{1,0:T(8,128)(2,1)} custom-call(s32[2]{0:T(128)S(1)} %pad_add_fusion.place, f32[4,8,8,128]{3,2,1,0:T(8,128)S(1)} %bitcast.8, f32[8,256]{1,0:T(8,128)S(1)} %get-tuple-element.23.params, bf16[4,28,16,256]{3,2,1,0:T(8,128)(2,1)S(1)} %get-tuple-element.19.feat, bf16[2,28,16,256]{3,2,1,0:T(8,128)(2,1)S(1)} %collective-permute-done.1.prev, ...), custom_call_target="tpu_custom_call" | custom-call | tf_op jit(solution)/shard_map/norm_conv_down/pallas_call | solution.py:302
  (1 shorter events, 0.0 us)
Async XLA Ops:
  0.0 14.2 %copy-start = (bf16[4,28,16,256]{3,2,1,0:T(8,128)(2,1)S(1)}, bf16[4,28,16,256]{3,2,1,0:T(8,128)(2,1)}, u32[]{:S(2)}) copy-start(bf16[4,28,16,256]{3,2,1,0:T(8,128)(2,1)} %feat.1) | copy-start | bytes 2752516
  0.0 14.2 %copy-start.3 = (s32[4]{0:T(128)S(1)}, s32[4]{0:T(128)}, u32[]{:S(2)}) copy-start(s32[4]{0:T(128)} %ids.1) | copy-start | bytes 52
  0.0 14.2 %copy-start.4 = (s32[4]{0:T(128)S(1)}, s32[4]{0:T(128)}, u32[]{:S(2)}) copy-start(s32[4]{0:T(128)} %valid.1) | copy-start | bytes 52
  0.0 14.2 %copy-start.1 = (f32[256]{0:T(256)S(1)}, f32[256]{0:T(256)}, u32[]{:S(2)}) copy-start(f32[256]{0:T(256)} %param.10) | copy-start | bytes 3076
  0.0 14.2 %copy-start.2 = (f32[256]{0:T(256)S(1)}, f32[256]{0:T(256)}, u32[]{:S(2)}) copy-start(f32[256]{0:T(256)} %param.11) | copy-start | bytes 3076
  1.2 22.5 %collective-permute-start = (bf16[36,32,256]{2,1,0:T(8,128)(2,1)S(1)}, bf16[36,32,256]{2,1,0:T(8,128)(2,1)S(1)}, u32[]{:S(2)}, u32[]{:S(2)}) collective-permute-start(bf16[36,32,256]{2,1,0:T(8,128)(2,1)S(1)} %pad_maximum_fusion.plain.rest_1_), channel_id=1, source_target_pairs={{6,0},{3,1},{0,2},{5,3},{2,4},{7,5},{4,6},{1,7},{14,8},{11,9},{8,1... | collective-permute-start | bytes 1769480 | tf_op jit(solution)/shard_map/ppermute | solution.py:33
  6.5 17.3 %collective-permute-start.4 = (bf16[36,32,256]{2,1,0:T(8,128)(2,1)S(1)}, bf16[36,32,256]{2,1,0:T(8,128)(2,1)S(1)}, u32[]{:S(2)}, u32[]{:S(2)}) collective-permute-start(bf16[36,32,256]{2,1,0:T(8,128)(2,1)S(1)} %pad_maximum_fusion.plain.rest_1_), channel_id=1, source_target_pairs={{7,0},{2,1},{1,2},{4,3},{3,4},{6,5},{5,6},{0,7},{15,8},{10,9},{9,1... | collective-permute-start | bytes 1769480 | tf_op jit(solution)/shard_map/ppermute | solution.py:33
  11.0 12.8 %collective-permute-start.1 = (bf16[2,28,16,256]{3,2,1,0:T(8,128)(2,1)}, bf16[2,28,16,256]{3,2,1,0:T(8,128)(2,1)S(1)}, u32[]{:S(2)}, u32[]{:S(2)}) collective-permute-start(bf16[2,28,16,256]{3,2,1,0:T(8,128)(2,1)} %slice.3), channel_id=1, source_target_pairs={{0,8},{8,16},{16,24},{24,32},{32,40},{40,48},{48,56},{56,64},{64,7... | collective-permute-start | bytes 1376264 | tf_op jit(solution)/shard_map/ppermute | solution.py:19
  15.3 4.8 %collective-permute-start.2 = (f32[8,128]{1,0:T(8,128)S(1)}, f32[8,128]{1,0:T(8,128)S(1)}, u32[]{:S(2)}, u32[]{:S(2)}) collective-permute-start(f32[8,128]{1,0:T(8,128)S(1)} %get-tuple-element.16), channel_id=1, source_target_pairs={{16,48},{24,56},{32,0},{40,8},{48,80},{56,88},{64,32},{72,40},{80,... | collective-permute-start | bytes 12296 | tf_op jit(solution)/shard_map/ppermute | solution.py:348
  25.7 26.2 %collective-permute-start.6 = (bf16[114,32,256]{2,1,0:T(8,128)(2,1)}, bf16[114,32,256]{2,1,0:T(8,128)(2,1)}, u32[]{:S(2)}, u32[]{:S(2)}) collective-permute-start(bf16[114,32,256]{2,1,0:T(8,128)(2,1)} %get-tuple-element.25), channel_id=1, source_target_pairs={{0,1},{1,0},{2,3},{3,2},{4,5},{5,4},{6,7},{7,6},{8,9},{9,8},{10,11... | collective-permute-start | bytes 5603336 | tf_op jit(solution)/shard_map/ppermute | solution.py:23
  31.3 16.5 %collective-permute-start.3 = (bf16[36,32,256]{2,1,0:T(8,128)(2,1)S(1)}, bf16[36,32,256]{2,1,0:T(8,128)(2,1)}, u32[]{:S(2)}, u32[]{:S(2)}) collective-permute-start(bf16[36,32,256]{2,1,0:T(8,128)(2,1)S(1)} %collective-permute-done.near.rest_2_), channel_id=1, source_target_pairs={{6,0},{3,1},{0,2},{5,3},{2,4},{7,5},{4,6},{1,7},{14,8},{11,9},{8,1... | collective-permute-start | bytes 1769480 | tf_op jit(solution)/shard_map/ppermute | solution.py:33
  35.1 12.6 %all-to-all-start = ((f32[32,8,128]{2,1,0:T(8,128)}), f32[32,8,128]{2,1,0:T(8,128)S(1)}, u32[]{:S(2)}, u32[]{:S(2)}) async-start(f32[32,8,128]{2,1,0:T(8,128)} %broadcast_in_dim.2), calls=%async_computation | async-start | bytes 262144 | tf_op jit(solution)/shard_map/all_to_all | solution.py:360
  40.1 6.2 %collective-permute-start.5 = (bf16[6,32,256]{2,1,0:T(8,128)(2,1)S(1)}, bf16[6,32,256]{2,1,0:T(8,128)(2,1)S(1)}, u32[]{:S(2)}, u32[]{:S(2)}) collective-permute-start(bf16[6,32,256]{2,1,0:T(8,128)(2,1)S(1)} %get-tuple-element.21), channel_id=1, source_target_pairs={{7,0},{2,1},{1,2},{4,3},{3,4},{6,5},{5,6},{0,7},{15,8},{10,9},{9,1... | collective-permute-start | bytes 294920 | tf_op jit(solution)/shard_map/ppermute | solution.py:33
  47.7 4.1 %collective-permute-start.7 = (bf16[36,32,256]{2,1,0:T(8,128)(2,1)}, bf16[36,32,256]{2,1,0:T(8,128)(2,1)S(1)}, u32[]{:S(2)}, u32[]{:S(2)}) collective-permute-start(bf16[36,32,256]{2,1,0:T(8,128)(2,1)} %collective-permute-done.3.rest_4_), channel_id=1, source_target_pairs={{0,1},{1,0},{2,3},{3,2},{4,5},{5,4},{6,7},{7,6},{8,9},{9,8},{10,11... | collective-permute-start | bytes 1769480 | tf_op jit(solution)/shard_map/ppermute | solution.py:23

commit v4 on v3

--- a/solution.py
+++ b/solution.py
@@ -23,14 +23,28 @@
     return lax.ppermute(value, axis, [(i, i ^ bits) for i in range(lax.axis_size(axis))])
 
 
-def ring_move(value, axis, cross):
-    chips = lax.axis_size(axis) // 2
+def ring_pairs(bands, cross):
+    chips = bands // 2
     pairs = []
     for chip in range(chips):
         for core in range(2):
             source_chip = (chip + (-1 if core == 0 else 1)) % chips
             pairs.append((2 * source_chip + (core ^ cross), 2 * chip + core))
-    return lax.ppermute(value, axis, pairs)
+    return pairs
+
+
+def ring_move(value, cross):
+    return lax.ppermute(value, "rows", ring_pairs(lax.axis_size("rows"), cross))
+
+
+def diagonal_move(value, band_pairs):
+    bands, times = lax.axis_size("rows"), lax.axis_size("tm")
+    pairs = [
+        ((at - 1) * bands + source, at * bands + target)
+        for at in range(1, times)
+        for source, target in band_pairs
+    ]
+    return lax.ppermute(value, ("tm", "rows"), pairs)
 
 
 def group_lanes(channels, first):
@@ -49,11 +63,23 @@
     )
 
 
-def pack_kernel(ids, valid, feat, gain, bias, table, params, kept):
+def pack_kernel(
+    place, feat, norm, table, params, kept, tail, chip_edge, core_edge, chip_last, core_last
+):
     frames, height, across, channels = feat.shape
     kept[...] = feat[...]
-    params[0:1, :] = gain[...]
-    params[1:2, :] = bias[...]
+    tail[...] = feat[frames - 2 :]
+    for core in range(2):
+
+        @pl.when(place[0] % 2 == core)
+        def _(core=core):
+            sides = ((chip_edge, chip_last, core), (core_edge, core_last, 1 - core))
+            for target, last, side in sides:
+                row = side * (height - 2)
+                target[...] = feat[:, row : row + 2].reshape(target.shape)
+                last[...] = feat[frames - 2 :, row : row + 2].reshape(last.shape)
+
+    params[0:2, :] = norm[...]
 
     first, second = [], []
     for f in range(frames):
@@ -65,14 +91,14 @@
     ) + exact_dot(jnp.concatenate(second + second, axis=0), group_lanes(channels, GROUPS))
     lane = lax.broadcasted_iota(jnp.int32, (1, 128), 1)
     for at in range(2 * frames):
-        weight = valid[at % frames].astype(F32)
+        weight = place[2 + frames + at % frames].astype(F32)
         row = rows[at : at + 1, :] * weight
-        row = jnp.where(lane == ID_LANE, ids[at % frames].astype(F32) + 1.0, row)
+        row = jnp.where(lane == ID_LANE, place[2 + at % frames].astype(F32) + 1.0, row)
         table[at : at + 1, :] = jnp.where(lane == VALID_LANE, weight, row)
 
 
-def pack_call(clip_ids, frame_valid, features, gain, bias):
-    frames, channels = features.shape[0], features.shape[-1]
+def pack_call(place, features, norm):
+    frames, height, across, channels = features.shape
     vmem = pl.BlockSpec(memory_space=pltpu.VMEM)
     return pl.pallas_call(
         pack_kernel,
@@ -80,46 +106,38 @@
             jax.ShapeDtypeStruct((2 * frames, 128), F32),
             jax.ShapeDtypeStruct((8, channels), F32),
             jax.ShapeDtypeStruct(features.shape, BF16),
+            jax.ShapeDtypeStruct((2, height, across, channels), BF16),
+            jax.ShapeDtypeStruct((frames, 2 * across, channels), BF16),
+            jax.ShapeDtypeStruct((frames, 2 * across, channels), BF16),
+            jax.ShapeDtypeStruct((2, 2 * across, channels), BF16),
+            jax.ShapeDtypeStruct((2, 2 * across, channels), BF16),
         ),
-        in_specs=[pl.BlockSpec(memory_space=pltpu.SMEM)] * 2 + [vmem] * 3,
-        out_specs=(vmem,) * 3,
-        compiler_params=pltpu.CompilerParams(vmem_limit_bytes=10 << 20),
+        in_specs=[pl.BlockSpec(memory_space=pltpu.SMEM)] + [vmem] * 2,
+        out_specs=(vmem,) * 8,
+        compiler_params=pltpu.CompilerParams(vmem_limit_bytes=12 << 20),
         name="frame_sums",
-    )(clip_ids, frame_valid, features, gain, bias)
-
-
-def swap_kernel(place, feat, prev, plain, near, near_cross, swap, edge):
-    frames, height, across, channels = feat.shape
-    taps, slice_in, _ = plain.shape
+    )(place, features, norm)
+
+
+def swap_kernel(core_edge, plain, near, near_cross, swap):
+    taps = plain.shape[0]
     for at, piece in enumerate((plain, near, near_cross)):
         swap[at * taps : (at + 1) * taps] = piece[...]
-    for core in range(2):
-
-        @pl.when(place[0] % 2 == core)
-        def _(core=core):
-            for source, first, count in ((prev, 0, 2), (feat, 2, frames)):
-                first_rows = source[:, 0:2].reshape(count, slice_in, channels)
-                last_rows = source[:, height - 2 :].reshape(count, slice_in, channels)
-                edge[first : first + count] = last_rows if core else first_rows
-                to_core = first_rows if core else last_rows
-                swap[3 * taps + first : 3 * taps + first + count] = to_core
-
-
-def swap_call(place, feat, prev, plain, near, near_cross):
-    frames, height, across, channels = feat.shape
-    taps, slice_in, _ = plain.shape
+    swap[3 * taps :] = core_edge[...]
+
+
+def swap_call(core_edge, plain, near, near_cross):
+    frames = core_edge.shape[0]
+    taps, slice_in, channels = plain.shape
     vmem = pl.BlockSpec(memory_space=pltpu.VMEM)
     return pl.pallas_call(
         swap_kernel,
-        out_shape=(
-            jax.ShapeDtypeStruct((3 * taps + frames + 2, slice_in, channels), BF16),
-            jax.ShapeDtypeStruct((frames + 2, slice_in, channels), BF16),
-        ),
-        in_specs=[pl.BlockSpec(memory_space=pltpu.SMEM)] + [vmem] * 5,
-        out_specs=(vmem,) * 2,
+        out_shape=jax.ShapeDtypeStruct((3 * taps + frames, slice_in, channels), BF16),
+        in_specs=[vmem] * 4,
+        out_specs=vmem,
         compiler_params=pltpu.CompilerParams(vmem_limit_bytes=10 << 20),
         name="swap_message",
-    )(place, feat, prev, plain, near, near_cross)
+    )(core_edge, plain, near, near_cross)
 
 
 def held_places(band):
@@ -129,7 +147,7 @@
     return [band, 2 * near_chip + core, 2 * near_chip + 1 - core, 2 * far_chip + core]
 
 
-def main_kernel(place, block, params, feat, prev, edge, *rest):
+def main_kernel(place, block, params, feat, prev, edges, far_chip, far_core, *rest):
     swap, pieces = rest[0], rest[1:6]
     out, w_all, hcol, mixed_all, top, bottom, sems = rest[6:]
     frames, height, across, channels = feat.shape
@@ -138,7 +156,7 @@
 
     band = place[0]
     places = held_places(band) + held_places(band + 1 - 2 * (band % 2))
-    sources = list(pieces[:4])
+    sources = [piece.at[0:taps] for piece in pieces[:4]]
     sources += [swap.at[at * taps : (at + 1) * taps] for at in range(3)] + [pieces[4]]
     copies = []
     for at in range(8):
@@ -152,10 +170,16 @@
 
         @pl.when(band % 2 == core)
         def _(core=core):
-            swap_rows = swap[3 * taps :].reshape(frames + 2, 2, across, channels)
-            edge_rows = edge[...].reshape(frames + 2, 2, across, channels)
-            top[...] = (swap_rows if core else edge_rows)[:, 1:2]
-            bottom[...] = edge_rows if core else swap_rows
+            swap_rows = swap[3 * taps :].reshape(frames, 2, across, channels)
+            chip_rows = edges[...].reshape(frames, 2, across, channels)
+            swap_prev = far_core[...].reshape(2, 2, across, channels)
+            chip_prev = far_chip[...].reshape(2, 2, across, channels)
+            above, below = (swap_rows, chip_rows) if core else (chip_rows, swap_rows)
+            above_prev, below_prev = (swap_prev, chip_prev) if core else (chip_prev, swap_prev)
+            top[0:2] = above_prev[:, 1:2]
+            top[2:] = above[:, 1:2]
+            bottom[0:2] = below_prev
+            bottom[2:] = below
 
     bands = block.shape[1]
     here = place[1] % BLOCK
@@ -235,24 +259,18 @@
 
     out_rows = height + 1
     lane_parts = channels // 128
-    ids_all = [before_ids[f : f + 1] for f in range(2)]
-    ids_all = ids_all + [own_ids[f : f + 1] for f in range(frames)]
+    hcol[frames + 2] = jnp.zeros(hcol.shape[1:], BF16)
+    ids_all = [before_ids[f, 0] for f in range(2)] + [own_ids[f, 0] for f in range(frames)]
     for t in range(frames):
         total = None
-        for dt in (2, 1, 0):
-            lhs = jnp.concatenate(
-                [
-                    hcol[t + dt, dr : dr + out_rows].reshape(out_rows * across, 3 * channels)
-                    for dr in range(3)
-                ],
-                axis=1,
-            )
-            rhs = w_all[dt * 9 : dt * 9 + 9].reshape(9 * channels, channels)
-            part = jnp.dot(lhs, rhs, preferred_element_type=F32)
-            if dt == 2:
-                total = part
-            else:
-                total = total + jnp.where(ids_all[t + dt] == ids_all[t + 2], part, 0.0)
+        for dt in range(3):
+            at = jnp.where(ids_all[t + dt] == ids_all[t + 2], t + dt, frames + 2)
+            for dr in range(3):
+                lhs = hcol[at, dr : dr + out_rows].reshape(out_rows * across, 3 * channels)
+                tap = (dt * 3 + dr) * 3
+                rhs = w_all[tap : tap + 3].reshape(3 * channels, channels)
+                product = jnp.dot(lhs, rhs, preferred_element_type=F32)
+                total = product if total is None else total + product
         weight = own_valid[t : t + 1]
         body_rows = height * across
         main_rows = feat[t].astype(F32).reshape(body_rows, channels) + total[:body_rows]
@@ -294,7 +312,7 @@
     out[...] = reduced.astype(BF16)
 
 
-def main_call(place, block, params, feat, prev, edge, swap, pieces):
+def main_call(place, block, params, feat, prev, edges, swap, pieces):
     frames, height, across, channels = feat.shape
     taps = pieces[0].shape[0]
     points = frames * (height // 2) * (across // 2)
@@ -303,11 +321,11 @@
         main_kernel,
         out_shape=jax.ShapeDtypeStruct((points, channels), BF16),
         in_specs=[pl.BlockSpec(memory_space=pltpu.SMEM)]
-        + [vmem] * 11,
+        + [vmem] * 13,
         out_specs=vmem,
         scratch_shapes=[
             pltpu.VMEM((taps, channels, channels), BF16),
-            pltpu.VMEM((frames + 2, height + 3, across, 3 * channels), BF16),
+            pltpu.VMEM((frames + 3, height + 3, across, 3 * channels), BF16),
             pltpu.VMEM((channels // 128, frames, height // 2 + 1, 2, across, 128), F32),
             pltpu.VMEM((frames + 2, 1, across, channels), BF16),
             pltpu.VMEM((frames + 2, 2, across, channels), BF16),
@@ -315,17 +333,17 @@
         ],
         compiler_params=pltpu.CompilerParams(vmem_limit_bytes=24 << 20),
         name="norm_conv_down",
-    )(place, block, params, feat, prev, edge, swap, *pieces)
+    )(place, block, params, feat, prev, *edges, swap, *pieces)
 
 
 def body(features, clip_ids, frame_valid, norm_gain, norm_bias, conv_weight, down_weight):
     frames, height, across, channels = features.shape
     slice_in = conv_weight.shape[3]
-    place = jnp.stack([lax.axis_index("rows"), lax.axis_index("tm")]).astype(jnp.int32)
-
+    where = jnp.stack([lax.axis_index("rows"), lax.axis_index("tm")]).astype(jnp.int32)
+    place = jnp.concatenate([where, clip_ids, frame_valid])
+    norm = jnp.stack([norm_gain, norm_bias])
     bands, times = lax.axis_size("rows"), lax.axis_size("tm")
 
-    prev = shifted(features[frames - 2 :], "tm", 1)
     plain = jnp.concatenate(
         [
             conv_weight.reshape(27, slice_in, channels),
@@ -333,15 +351,17 @@
         ],
         axis=0,
     )
-    near = ring_move(plain, "rows", 0)
-    table, params, feat = pack_call(
-        clip_ids,
-        frame_valid,
-        features,
-        norm_gain.reshape(1, channels),
-        norm_bias.reshape(1, channels),
+    near = ring_move(plain, 0)
+    table, params, feat, tail, chip_edge, core_edge, chip_last, core_last = pack_call(
+        place, features, norm
     )
-    near_cross = ring_move(plain, "rows", 1)
+    prev = shifted(tail, "tm", 1)
+    near_cross = ring_move(plain, 1)
+    edges = [
+        ring_move(chip_edge, 1),
+        diagonal_move(chip_last, ring_pairs(bands, 1)),
+        diagonal_move(core_last, [(at ^ 1, at) for at in range(bands)]),
+    ]
 
     half = BLOCK // 2
     pairs = [(at, at + (BLOCK if at % BLOCK >= half else -BLOCK)) for at in range(times)]
@@ -349,11 +369,9 @@
     row = lax.broadcasted_iota(jnp.int32, table.shape, 0)
     rows = jnp.where(row < frames, table, sent)
 
-    near, prev, rows = lax.optimization_barrier((near, prev, rows))
-    far = ring_move(near, "rows", 0)
-    swap, edge = swap_call(place, feat, prev, plain, near, near_cross)
-    swap = swapped(swap, "rows", 1)
-    edge = ring_move(edge, "rows", 1)
+    near, prev, edges, rows = lax.optimization_barrier((near, prev, edges, rows))
+    far = ring_move(near, 0)
+    swap = swapped(swap_call(core_edge, plain, near, near_cross), "rows", 1)
 
     size = BLOCK * bands
     groups = [[first + at for at in range(size)] for first in range(0, bands * times, size)]
@@ -366,10 +384,10 @@
         tiled=True,
     ).reshape(BLOCK, bands, *rows.shape)
 
-    far, block, edge = lax.optimization_barrier((far, block, edge))
+    far, block = lax.optimization_barrier((far, block))
     pieces = [plain, near, near_cross, far, swapped(far, "rows", 1)]
 
-    out = main_call(place, block, params, feat, prev, edge, swap, pieces)
+    out = main_call(place, block, params, feat, prev, edges, swap, pieces)
     return out.reshape(frames, height // 2, across // 2, channels)
 
 

time: 65.9 us -> 72.6 us (1.10)
  the two profiles are of different devices: /device:TPU:1 before, /device:TPU:257 now
where the time goes in v4:
time: 72.6 us; the launch traced here: 72.1 us
  starting transfers between devices  27.8 us (38%)
  waiting for transfers between devices  16.1 us (22%)
  Pallas kernels  13.6 us (19%)
  blocking collectives  11.7 us (16%)
  other arithmetic  2.75 us (4%)
    ppermute x2, waiting for transfers between devices, diagonal_move(): return lax.ppermute(value, ('tm', 'rows'), pairs)  14.4 us
    pallas_call x1, Pallas kernels, main_call(): pl.pallas_call(main_kernel, out_shape=jax.ShapeDtypeStruct((points, chann...  12.5 us
    ppermute x4, starting transfers between devices, ring_move(): return lax.ppermute(value, 'rows', ring_pairs(lax.axis_size('rows'), cross))  11.9 us
    all_to_all x1, blocking collectives, body(): lax.all_to_all(jnp.broadcast_to(rows[None], (size, *rows.shape)), ('tm',...  11.7 us
    ppermute x2, starting transfers between devices, diagonal_move(): return lax.ppermute(value, ('tm', 'rows'), pairs)  6.17 us
    ppermute x2, starting transfers between devices, swapped(): lax.ppermute(value, axis, [(i, i ^ bits) for i in range(lax.axis_size(axi...  4.61 us
    ppermute x1, starting transfers between devices, shifted(): lax.ppermute(value, axis, [(source, source + steps) for source in range(f...  3.21 us
    ppermute x1, starting transfers between devices, body(): lax.ppermute(table, 'tm', [pair for pair in pairs if 0 <= pair[1] < times])  1.92 us
  transfers between devices with their start and end apart: 10, of which 3 were waited for; matrix products, arithmetic and copies ran while one was open for 2% of the time, Pallas kernels for 1%

profile of v4, /device:TPU:257, one launch (start us, length us, event | category | flops | bytes accessed | tf_op | source)
XLA Modules:
  0.0 72.1 jit_solution(18246274100740276743)
XLA Ops:
  0.0 0.0 copy-start
  0.0 1.2 %pad_maximum_fusion.plain.rest_1_ = bf16[36,32,256]{2,1,0:T(8,128)(2,1)S(1)} fusion(bf16[9,32,256]{2,1,0:T(8,128)(2,1)} %bitcast.10, bf16[27,32,256]{2,1,0:T(8,128)(2,1)} %bitcast.9), kind=kLoop, calls=%fused_computation | loop fusion | flops 294912 | bytes 1179648 | tf_op jit(solution)/shard_map/concatenate | solution.py:347
  1.2 4.4 %collective-permute-start = (bf16[36,32,256]{2,1,0:T(8,128)(2,1)S(1)}, bf16[36,32,256]{2,1,0:T(8,128)(2,1)S(1)}, u32[]{:S(2)}, u32[]{:S(2)}) collective-permute-start(bf16[36,32,256]{2,1,0:T(8,128)(2,1)S(1)} %pad_maximum_fusion.plain.rest_1_), channel_id=1, source_target_pairs={{6,0},{3,1},{0,2},{5,3},{2,4},{7,5},{4,6},{1,7},{14,8},{11,9},{8,1... | collective-permute-start | bytes 1769480 | tf_op jit(solution)/shard_map/ppermute | solution.py:37
  5.6 2.7 %collective-permute-start.7 = (bf16[36,32,256]{2,1,0:T(8,128)(2,1)S(1)}, bf16[36,32,256]{2,1,0:T(8,128)(2,1)S(1)}, u32[]{:S(2)}, u32[]{:S(2)}) collective-permute-start(bf16[36,32,256]{2,1,0:T(8,128)(2,1)S(1)} %pad_maximum_fusion.plain.rest_1_), channel_id=1, source_target_pairs={{7,0},{2,1},{1,2},{4,3},{3,4},{6,5},{5,6},{0,7},{15,8},{10,9},{9,1... | collective-permute-start | bytes 1769480 | tf_op jit(solution)/shard_map/ppermute | solution.py:37
  8.3 0.8 %pad_add_fusion.place = s32[10]{0:T(128)S(1)} fusion(s32[4]{0:T(128)} %param.9, s32[4]{0:T(128)} %param.8, s32[1]{0:T(128)} %bitcast.1, s32[1]{0:T(128)} %bitcast), kind=kLoop, calls=%fused_computation.3 | loop fusion | flops 30 | bytes 80 | tf_op jit(solution)/shard_map/concatenate | solution.py:343
  9.1 0.7 pad_maximum_fusion.1.norm
  9.8 0.0 copy-done
  9.8 1.1 %frame_sums.1 = (f32[8,128]{1,0:T(8,128)S(1)}, f32[8,256]{1,0:T(8,128)S(1)}, bf16[4,28,16,256]{3,2,1,0:T(8,128)(2,1)S(1)}, bf16[2,28,16,256]{3,2,1,0:T(8,128)(2,...) custom-call(s32[10]{0:T(128)S(1)} %pad_add_fusion.place, ...), custom_call_target="tpu_custom_call" | custom-call | tf_op jit(solution)/shard_map/frame_sums/pallas_call | solution.py:103
  10.9 3.2 %collective-permute-start.1 = (bf16[2,28,16,256]{3,2,1,0:T(8,128)(2,1)S(1)}, bf16[2,28,16,256]{3,2,1,0:T(8,128)(2,1)S(1)}, u32[]{:S(2)}, u32[]{:S(2)}) collective-permute-start(bf16[2,28,16,256]{3,2,1,0:T(8,128)(2,1)S(1)} %get-tuple-element.21), channel_id=1, source_target_pairs={{0,8},{8,16},{16,24},{24,32},{32,40},{40,48},{48,56},{56,64},{64,7... | collective-permute-start | bytes 1376264 | tf_op jit(solution)/shard_map/ppermute | solution.py:19
  14.1 1.9 %collective-permute-start.5 = (f32[8,128]{1,0:T(8,128)S(1)}, f32[8,128]{1,0:T(8,128)S(1)}, u32[]{:S(2)}, u32[]{:S(2)}) collective-permute-start(f32[8,128]{1,0:T(8,128)S(1)} %get-tuple-element.25), channel_id=1, source_target_pairs={{16,48},{24,56},{32,0},{40,8},{48,80},{56,88},{64,32},{72,40},{80,... | collective-permute-start | bytes 12296 | tf_op jit(solution)/shard_map/ppermute | solution.py:368
  16.0 4.3 %collective-permute-start.3 = (bf16[2,32,256]{2,1,0:T(8,128)(2,1)S(1)}, bf16[2,32,256]{2,1,0:T(8,128)(2,1)S(1)}, u32[]{:S(2)}, u32[]{:S(2)}) collective-permute-start(bf16[2,32,256]{2,1,0:T(8,128)(2,1)S(1)} %get-tuple-element.23), channel_id=1, source_target_pairs={{7,8},{2,9},{1,10},{4,11},{3,12},{6,13},{5,14},{0,15},{15,16},{10,... | collective-permute-start | bytes 98312 | tf_op jit(solution)/shard_map/ppermute | solution.py:47
  20.3 0.0 collective-permute-done.5
  20.3 2.4 %collective-permute-start.2 = (bf16[4,32,256]{2,1,0:T(8,128)(2,1)S(1)}, bf16[4,32,256]{2,1,0:T(8,128)(2,1)S(1)}, u32[]{:S(2)}, u32[]{:S(2)}) collective-permute-start(bf16[4,32,256]{2,1,0:T(8,128)(2,1)S(1)} %get-tuple-element.22), channel_id=1, source_target_pairs={{7,0},{2,1},{1,2},{4,3},{3,4},{6,5},{5,6},{0,7},{15,8},{10,9},{9,1... | collective-permute-start | bytes 196616 | tf_op jit(solution)/shard_map/ppermute | solution.py:37
  22.7 7.3 %collective-permute-done.3.far_chip = bf16[2,32,256]{2,1,0:T(8,128)(2,1)S(1)} collective-permute-done((bf16[2,32,256]{2,1,0:T(8,128)(2,1)S(1)}, bf16[2,32,256]{2,1,0:T(8,128)(2,1)S(1)}, u32[]{:S(2)}, u32[]{:S(2)}) %collective-permute-start.3) | collective-permute-done | bytes 32800 | tf_op jit(solution)/shard_map/ppermute | solution.py:47
  30.0 1.9 %collective-permute-start.4 = (bf16[2,32,256]{2,1,0:T(8,128)(2,1)S(1)}, bf16[2,32,256]{2,1,0:T(8,128)(2,1)S(1)}, u32[]{:S(2)}, u32[]{:S(2)}) collective-permute-start(bf16[2,32,256]{2,1,0:T(8,128)(2,1)S(1)} %get-tuple-element.24), channel_id=1, source_target_pairs={{1,8},{0,9},{3,10},{2,11},{5,12},{4,13},{7,14},{6,15},{9,16},{8,17... | collective-permute-start | bytes 98312 | tf_op jit(solution)/shard_map/ppermute | solution.py:47
  32.0 0.1 broadcast_select_fusion
  32.0 7.1 %collective-permute-done.4.far_core = bf16[2,32,256]{2,1,0:T(8,128)(2,1)S(1)} collective-permute-done((bf16[2,32,256]{2,1,0:T(8,128)(2,1)S(1)}, bf16[2,32,256]{2,1,0:T(8,128)(2,1)S(1)}, u32[]{:S(2)}, u32[]{:S(2)}) %collective-permute-start.4) | collective-permute-done | bytes 32800 | tf_op jit(solution)/shard_map/ppermute | solution.py:47
  39.1 0.0 collective-permute-done.2.edges
  39.1 0.0 collective-permute-done.1.prev
  39.2 0.0 collective-permute-done.near.rest_2_
  39.2 0.0 collective-permute-done.7.near_cross.rest_3_
  39.2 0.1 swap_message.1
  39.3 2.3 %collective-permute-start.8 = (bf16[112,32,256]{2,1,0:T(8,128)(2,1)S(1)}, bf16[112,32,256]{2,1,0:T(8,128)(2,1)S(1)}, u32[]{:S(2)}, u32[]{:S(2)}) collective-permute-start(bf16[112,32,256]{2,1,0:T(8,128)(2,1)S(1)} %swap_message.1), channel_id=1, source_target_pairs={{0,1},{1,0},{2,3},{3,2},{4,5},{5,4},{6,7},{7,6},{8,9},{9,8},{10,11... | collective-permute-start | bytes 5505032 | tf_op jit(solution)/shard_map/ppermute | solution.py:23
  41.6 2.4 %collective-permute-start.6 = (bf16[36,32,256]{2,1,0:T(8,128)(2,1)S(1)}, bf16[36,32,256]{2,1,0:T(8,128)(2,1)S(1)}, u32[]{:S(2)}, u32[]{:S(2)}) collective-permute-start(bf16[36,32,256]{2,1,0:T(8,128)(2,1)S(1)} %collective-permute-done.near.rest_2_), channel_id=1, source_target_pairs={{6,0},{3,1},{0,2},{5,3},{2,4},{7,5},{4,6},{1,7},{14,8},{11,9},{8,1... | collective-permute-start | bytes 1769480 | tf_op jit(solution)/shard_map/ppermute | solution.py:37
  44.1 11.7 %all_to_all.5 = f32[32,8,128]{2,1,0:T(8,128)S(1)} all-to-all(f32[32,8,128]{2,1,0:T(8,128)S(1)} %broadcast_in_dim.2), channel_id=1, replica_groups={{0,1,2,3,4,5,6,7,8,9,10,11,12,13,14,15,16,17,18,19,20,21,22,23,24,25,26..., dimensions={0} | all-to-all | bytes 262144 | tf_op jit(solution)/shard_map/all_to_all | solution.py:378
  55.8 0.0 collective-permute-done.6.rest_4_
  55.8 2.3 %collective-permute-start.9 = (bf16[36,32,256]{2,1,0:T(8,128)(2,1)S(1)}, bf16[36,32,256]{2,1,0:T(8,128)(2,1)S(1)}, u32[]{:S(2)}, u32[]{:S(2)}) collective-permute-start(bf16[36,32,256]{2,1,0:T(8,128)(2,1)S(1)} %collective-permute-done.6.rest_4_), channel_id=1, source_target_pairs={{0,1},{1,0},{2,3},{3,2},{4,5},{5,4},{6,7},{7,6},{8,9},{9,8},{10,11... | collective-permute-start | bytes 1769480 | tf_op jit(solution)/shard_map/ppermute | solution.py:23
  58.1 1.6 %collective-permute-done.9.rest_5_ = bf16[36,32,256]{2,1,0:T(8,128)(2,1)S(1)} collective-permute-done((bf16[36,32,256]{2,1,0:T(8,128)(2,1)S(1)}, bf16[36,32,256]{2,1,0:T(8,128)(2,1)S(1)}, u32[]{:S(2)}, u32[]{:S(2)}) %collective-permute-start.9) | collective-permute-done | bytes 589856 | tf_op jit(solution)/shard_map/ppermute | solution.py:23
  59.7 0.0 collective-permute-done.8.rest_0_
  59.7 12.5 %norm_conv_down.1 = bf16[448,256]{1,0:T(8,128)(2,1)} custom-call(s32[10]{0:T(128)S(1)} %pad_add_fusion.place, f32[4,8,8,128]{3,2,1,0:T(8,128)S(1)} %bitcast.8, f32[8,256]{1,0:T(8,128)S(1)} %get-tuple-element.29.params, bf16[4,28,16,256]{3,2,1,0:T(8,128)(2,1)S(1)} %get-tuple-element.30.feat, bf16[2,28,16,256]{3,2,1,0:T(8,128)(2,1)S(1)} %collective-permute-done.1.prev, ...), custom_call_target="tpu_custom_call" | custom-call | tf_op jit(solution)/shard_map/norm_conv_down/pallas_call | solution.py:320
  (2 shorter events, 0.0 us)
Async XLA Ops:
  0.0 9.8 %copy-start = (bf16[4,28,16,256]{3,2,1,0:T(8,128)(2,1)S(1)}, bf16[4,28,16,256]{3,2,1,0:T(8,128)(2,1)}, u32[]{:S(2)}) copy-start(bf16[4,28,16,256]{3,2,1,0:T(8,128)(2,1)} %feat.1) | copy-start | bytes 2752516
  1.2 37.9 %collective-permute-start = (bf16[36,32,256]{2,1,0:T(8,128)(2,1)S(1)}, bf16[36,32,256]{2,1,0:T(8,128)(2,1)S(1)}, u32[]{:S(2)}, u32[]{:S(2)}) collective-permute-start(bf16[36,32,256]{2,1,0:T(8,128)(2,1)S(1)} %pad_maximum_fusion.plain.rest_1_), channel_id=1, source_target_pairs={{6,0},{3,1},{0,2},{5,3},{2,4},{7,5},{4,6},{1,7},{14,8},{11,9},{8,1... | collective-permute-start | bytes 1769480 | tf_op jit(solution)/shard_map/ppermute | solution.py:37
  5.6 33.5 %collective-permute-start.7 = (bf16[36,32,256]{2,1,0:T(8,128)(2,1)S(1)}, bf16[36,32,256]{2,1,0:T(8,128)(2,1)S(1)}, u32[]{:S(2)}, u32[]{:S(2)}) collective-permute-start(bf16[36,32,256]{2,1,0:T(8,128)(2,1)S(1)} %pad_maximum_fusion.plain.rest_1_), channel_id=1, source_target_pairs={{7,0},{2,1},{1,2},{4,3},{3,4},{6,5},{5,6},{0,7},{15,8},{10,9},{9,1... | collective-permute-start | bytes 1769480 | tf_op jit(solution)/shard_map/ppermute | solution.py:37
  10.9 28.3 %collective-permute-start.1 = (bf16[2,28,16,256]{3,2,1,0:T(8,128)(2,1)S(1)}, bf16[2,28,16,256]{3,2,1,0:T(8,128)(2,1)S(1)}, u32[]{:S(2)}, u32[]{:S(2)}) collective-permute-start(bf16[2,28,16,256]{3,2,1,0:T(8,128)(2,1)S(1)} %get-tuple-element.21), channel_id=1, source_target_pairs={{0,8},{8,16},{16,24},{24,32},{32,40},{40,48},{48,56},{56,64},{64,7... | collective-permute-start | bytes 1376264 | tf_op jit(solution)/shard_map/ppermute | solution.py:19
  14.1 6.2 %collective-permute-start.5 = (f32[8,128]{1,0:T(8,128)S(1)}, f32[8,128]{1,0:T(8,128)S(1)}, u32[]{:S(2)}, u32[]{:S(2)}) collective-permute-start(f32[8,128]{1,0:T(8,128)S(1)} %get-tuple-element.25), channel_id=1, source_target_pairs={{16,48},{24,56},{32,0},{40,8},{48,80},{56,88},{64,32},{72,40},{80,... | collective-permute-start | bytes 12296 | tf_op jit(solution)/shard_map/ppermute | solution.py:368
  16.0 14.1 %collective-permute-start.3 = (bf16[2,32,256]{2,1,0:T(8,128)(2,1)S(1)}, bf16[2,32,256]{2,1,0:T(8,128)(2,1)S(1)}, u32[]{:S(2)}, u32[]{:S(2)}) collective-permute-start(bf16[2,32,256]{2,1,0:T(8,128)(2,1)S(1)} %get-tuple-element.23), channel_id=1, source_target_pairs={{7,8},{2,9},{1,10},{4,11},{3,12},{6,13},{5,14},{0,15},{15,16},{10,... | collective-permute-start | bytes 98312 | tf_op jit(solution)/shard_map/ppermute | solution.py:47
  20.3 18.9 %collective-permute-start.2 = (bf16[4,32,256]{2,1,0:T(8,128)(2,1)S(1)}, bf16[4,32,256]{2,1,0:T(8,128)(2,1)S(1)}, u32[]{:S(2)}, u32[]{:S(2)}) collective-permute-start(bf16[4,32,256]{2,1,0:T(8,128)(2,1)S(1)} %get-tuple-element.22), channel_id=1, source_target_pairs={{7,0},{2,1},{1,2},{4,3},{3,4},{6,5},{5,6},{0,7},{15,8},{10,9},{9,1... | collective-permute-start | bytes 196616 | tf_op jit(solution)/shard_map/ppermute | solution.py:37
  30.0 9.1 %collective-permute-start.4 = (bf16[2,32,256]{2,1,0:T(8,128)(2,1)S(1)}, bf16[2,32,256]{2,1,0:T(8,128)(2,1)S(1)}, u32[]{:S(2)}, u32[]{:S(2)}) collective-permute-start(bf16[2,32,256]{2,1,0:T(8,128)(2,1)S(1)} %get-tuple-element.24), channel_id=1, source_target_pairs={{1,8},{0,9},{3,10},{2,11},{5,12},{4,13},{7,14},{6,15},{9,16},{8,17... | collective-permute-start | bytes 98312 | tf_op jit(solution)/shard_map/ppermute | solution.py:47
  39.3 20.4 %collective-permute-start.8 = (bf16[112,32,256]{2,1,0:T(8,128)(2,1)S(1)}, bf16[112,32,256]{2,1,0:T(8,128)(2,1)S(1)}, u32[]{:S(2)}, u32[]{:S(2)}) collective-permute-start(bf16[112,32,256]{2,1,0:T(8,128)(2,1)S(1)} %swap_message.1), channel_id=1, source_target_pairs={{0,1},{1,0},{2,3},{3,2},{4,5},{5,4},{6,7},{7,6},{8,9},{9,8},{10,11... | collective-permute-start | bytes 5505032 | tf_op jit(solution)/shard_map/ppermute | solution.py:23
  41.6 14.1 %collective-permute-start.6 = (bf16[36,32,256]{2,1,0:T(8,128)(2,1)S(1)}, bf16[36,32,256]{2,1,0:T(8,128)(2,1)S(1)}, u32[]{:S(2)}, u32[]{:S(2)}) collective-permute-start(bf16[36,32,256]{2,1,0:T(8,128)(2,1)S(1)} %collective-permute-done.near.rest_2_), channel_id=1, source_target_pairs={{6,0},{3,1},{0,2},{5,3},{2,4},{7,5},{4,6},{1,7},{14,8},{11,9},{8,1... | collective-permute-start | bytes 1769480 | tf_op jit(solution)/shard_map/ppermute | solution.py:37
  55.8 3.9 %collective-permute-start.9 = (bf16[36,32,256]{2,1,0:T(8,128)(2,1)S(1)}, bf16[36,32,256]{2,1,0:T(8,128)(2,1)S(1)}, u32[]{:S(2)}, u32[]{:S(2)}) collective-permute-start(bf16[36,32,256]{2,1,0:T(8,128)(2,1)S(1)} %collective-permute-done.6.rest_4_), channel_id=1, source_target_pairs={{0,1},{1,0},{2,3},{3,2},{4,5},{5,4},{6,7},{7,6},{8,9},{9,8},{10,11... | collective-permute-start | bytes 1769480 | tf_op jit(solution)/shard_map/ppermute | solution.py:23

commit v5 on v3

--- a/solution.py
+++ b/solution.py
@@ -49,9 +49,10 @@
     )
 
 
-def pack_kernel(ids, valid, feat, gain, bias, table, params, kept):
+def pack_kernel(ids, valid, feat, gain, bias, table, params, kept, tail):
     frames, height, across, channels = feat.shape
     kept[...] = feat[...]
+    tail[...] = feat[frames - 2 :]
     params[0:1, :] = gain[...]
     params[1:2, :] = bias[...]
 
@@ -80,9 +81,10 @@
             jax.ShapeDtypeStruct((2 * frames, 128), F32),
             jax.ShapeDtypeStruct((8, channels), F32),
             jax.ShapeDtypeStruct(features.shape, BF16),
+            jax.ShapeDtypeStruct((2, *features.shape[1:]), BF16),
         ),
         in_specs=[pl.BlockSpec(memory_space=pltpu.SMEM)] * 2 + [vmem] * 3,
-        out_specs=(vmem,) * 3,
+        out_specs=(vmem,) * 4,
         compiler_params=pltpu.CompilerParams(vmem_limit_bytes=10 << 20),
         name="frame_sums",
     )(clip_ids, frame_valid, features, gain, bias)
@@ -235,24 +237,18 @@
 
     out_rows = height + 1
     lane_parts = channels // 128
-    ids_all = [before_ids[f : f + 1] for f in range(2)]
-    ids_all = ids_all + [own_ids[f : f + 1] for f in range(frames)]
+    hcol[frames + 2] = jnp.zeros(hcol.shape[1:], BF16)
+    ids_all = [before_ids[f, 0] for f in range(2)] + [own_ids[f, 0] for f in range(frames)]
     for t in range(frames):
         total = None
-        for dt in (2, 1, 0):
-            lhs = jnp.concatenate(
-                [
-                    hcol[t + dt, dr : dr + out_rows].reshape(out_rows * across, 3 * channels)
-                    for dr in range(3)
-                ],
-                axis=1,
-            )
-            rhs = w_all[dt * 9 : dt * 9 + 9].reshape(9 * channels, channels)
-            part = jnp.dot(lhs, rhs, preferred_element_type=F32)
-            if dt == 2:
-                total = part
-            else:
-                total = total + jnp.where(ids_all[t + dt] == ids_all[t + 2], part, 0.0)
+        for dt in range(3):
+            at = jnp.where(ids_all[t + dt] == ids_all[t + 2], t + dt, frames + 2)
+            for dr in range(3):
+                lhs = hcol[at, dr : dr + out_rows].reshape(out_rows * across, 3 * channels)
+                tap = (dt * 3 + dr) * 3
+                rhs = w_all[tap : tap + 3].reshape(3 * channels, channels)
+                product = jnp.dot(lhs, rhs, preferred_element_type=F32)
+                total = product if total is None else total + product
         weight = own_valid[t : t + 1]
         body_rows = height * across
         main_rows = feat[t].astype(F32).reshape(body_rows, channels) + total[:body_rows]
@@ -307,7 +303,7 @@
         out_specs=vmem,
         scratch_shapes=[
             pltpu.VMEM((taps, channels, channels), BF16),
-            pltpu.VMEM((frames + 2, height + 3, across, 3 * channels), BF16),
+            pltpu.VMEM((frames + 3, height + 3, across, 3 * channels), BF16),
             pltpu.VMEM((channels // 128, frames, height // 2 + 1, 2, across, 128), F32),
             pltpu.VMEM((frames + 2, 1, across, channels), BF16),
             pltpu.VMEM((frames + 2, 2, across, channels), BF16),
@@ -325,7 +321,6 @@
 
     bands, times = lax.axis_size("rows"), lax.axis_size("tm")
 
-    prev = shifted(features[frames - 2 :], "tm", 1)
     plain = jnp.concatenate(
         [
             conv_weight.reshape(27, slice_in, channels),
@@ -334,13 +329,14 @@
         axis=0,
     )
     near = ring_move(plain, "rows", 0)
-    table, params, feat = pack_call(
+    table, params, feat, tail = pack_call(
         clip_ids,
         frame_valid,
         features,
         norm_gain.reshape(1, channels),
         norm_bias.reshape(1, channels),
     )
+    prev = shifted(tail, "tm", 1)
     near_cross = ring_move(plain, "rows", 1)
 
     half = BLOCK // 2
@@ -348,13 +344,8 @@
     sent = lax.ppermute(table, "tm", [pair for pair in pairs if 0 <= pair[1] < times])
     row = lax.broadcasted_iota(jnp.int32, table.shape, 0)
     rows = jnp.where(row < frames, table, sent)
-
-    near, prev, rows = lax.optimization_barrier((near, prev, rows))
+    near, rows = lax.optimization_barrier((near, rows))
     far = ring_move(near, "rows", 0)
-    swap, edge = swap_call(place, feat, prev, plain, near, near_cross)
-    swap = swapped(swap, "rows", 1)
-    edge = ring_move(edge, "rows", 1)
-
     size = BLOCK * bands
     groups = [[first + at for at in range(size)] for first in range(0, bands * times, size)]
     block = lax.all_to_all(
@@ -366,7 +357,10 @@
         tiled=True,
     ).reshape(BLOCK, bands, *rows.shape)
 
-    far, block, edge = lax.optimization_barrier((far, block, edge))
+    prev, near_cross, far, block = lax.optimization_barrier((prev, near_cross, far, block))
+    swap, edge = swap_call(place, feat, prev, plain, near, near_cross)
+    swap = swapped(swap, "rows", 1)
+    edge = ring_move(edge, "rows", 1)
     pieces = [plain, near, near_cross, far, swapped(far, "rows", 1)]
 
     out = main_call(place, block, params, feat, prev, edge, swap, pieces)

time: 65.9 us -> 67.9 us (1.030)
  local copies, waits for them, and re-layouts: 2.51 us -> 4.51 us
  waiting for transfers between devices: 12.9 us -> 14.8 us
  Pallas kernels: 16.5 us -> 15.4 us
  starting transfers between devices: 32 us -> 31.3 us
    all_to_all x1, waiting for transfers between devices: 1.4 us -> 6.61 us  [body(): lax.all_to_all(jnp.broadcast_to(rows[None], (size, *rows.shape)), ('tm',...]
    unnamed x10, local copies, waits for them, and re-layouts: 0.02 us -> 3.84 us
    ppermute x2, starting transfers between devices: 7.86 us -> 4.33 us  [swapped(): lax.ppermute(value, axis, [(i, i ^ bits) for i in range(lax.axis_size(axi...]
    ppermute x1, waiting for transfers between devices: 3.6 us -> 0.93 us  [shifted(): lax.ppermute(value, axis, [(source, source + steps) for source in range(f...]
    ppermute x4, starting transfers between devices: 14.6 us -> 17.2 us  [ring_move(): return lax.ppermute(value, axis, pairs)]
    all_to_all x1, starting transfers between devices: 5 us -> 7.16 us  [body(): lax.all_to_all(jnp.broadcast_to(rows[None], (size, *rows.shape)), ('tm',...]
    ppermute x1, starting transfers between devices: 3.22 us -> 1.32 us  [shifted(): lax.ppermute(value, axis, [(source, source + steps) for source in range(f...]
    slice x1 -> x0, local copies, waits for them, and re-layouts: 1.83 us -> none  [body(): prev = shifted(features[frames - 2:], 'tm', 1)]
  transfers between devices with their start and end apart: 9 -> 9, of which waited for: 5 -> 4; matrix products, arithmetic and copies ran while one was open for 4% -> 1% of each run, Pallas kernels for 2% -> 3%
where the time goes in v5:
time: 67.9 us; the launch traced here: 67.4 us
  starting transfers between devices  31.3 us (46%)
  Pallas kernels  15.4 us (23%)
  waiting for transfers between devices  14.8 us (22%)
  local copies, waits for them, and re-layouts  4.51 us (7%)
  other arithmetic  1.3 us (2%)
    ppermute x4, starting transfers between devices, ring_move(): return lax.ppermute(value, axis, pairs)  17.2 us
    pallas_call x1, Pallas kernels, main_call(): pl.pallas_call(main_kernel, out_shape=jax.ShapeDtypeStruct((points, chann...  13 us
    all_to_all x1, starting transfers between devices, body(): lax.all_to_all(jnp.broadcast_to(rows[None], (size, *rows.shape)), ('tm',...  7.16 us
    all_to_all x1, waiting for transfers between devices, body(): lax.all_to_all(jnp.broadcast_to(rows[None], (size, *rows.shape)), ('tm',...  6.61 us
    ppermute x2, starting transfers between devices, swapped(): lax.ppermute(value, axis, [(i, i ^ bits) for i in range(lax.axis_size(axi...  4.33 us
    unnamed x10, local copies, waits for them, and re-layouts  3.84 us
    ppermute x4, waiting for transfers between devices, ring_move(): return lax.ppermute(value, axis, pairs)  3.69 us
    ppermute x1, waiting for transfers between devices, body(): lax.ppermute(table, 'tm', [pair for pair in pairs if 0 <= pair[1] < times])  3.52 us
  transfers between devices with their start and end apart: 9, of which 4 were waited for; matrix products, arithmetic and copies ran while one was open for 1% of the time, Pallas kernels for 3%

profile of v5, /device:TPU:1, one launch (start us, length us, event | category | flops | bytes accessed | tf_op | source)
XLA Modules:
  0.0 67.4 jit_solution(10203824171303193499)
XLA Ops:
  0.0 1.1 %pad_maximum_fusion.plain.rest_1_ = bf16[36,32,256]{2,1,0:T(8,128)(2,1)S(1)} fusion(bf16[9,32,256]{2,1,0:T(8,128)(2,1)} %bitcast.12, bf16[27,32,256]{2,1,0:T(8,128)(2,1)} %bitcast.11), kind=kLoop, calls=%fused_computation | loop fusion | flops 294912 | bytes 1179648 | tf_op jit(solution)/shard_map/concatenate | solution.py:324
  1.2 5.2 %collective-permute-start.2 = (bf16[36,32,256]{2,1,0:T(8,128)(2,1)S(1)}, bf16[36,32,256]{2,1,0:T(8,128)(2,1)S(1)}, u32[]{:S(2)}, u32[]{:S(2)}) collective-permute-start(bf16[36,32,256]{2,1,0:T(8,128)(2,1)S(1)} %pad_maximum_fusion.plain.rest_1_), channel_id=1, source_target_pairs={{6,0},{3,1},{0,2},{5,3},{2,4},{7,5},{4,6},{1,7},{14,8},{11,9},{8,1... | collective-permute-start | bytes 1769480 | tf_op jit(solution)/shard_map/ppermute | solution.py:33
  6.4 2.7 %collective-permute-start.1 = (bf16[36,32,256]{2,1,0:T(8,128)(2,1)S(1)}, bf16[36,32,256]{2,1,0:T(8,128)(2,1)S(1)}, u32[]{:S(2)}, u32[]{:S(2)}) collective-permute-start(bf16[36,32,256]{2,1,0:T(8,128)(2,1)S(1)} %pad_maximum_fusion.plain.rest_1_), channel_id=1, source_target_pairs={{7,0},{2,1},{1,2},{4,3},{3,4},{6,5},{5,6},{0,7},{15,8},{10,9},{9,1... | collective-permute-start | bytes 1769480 | tf_op jit(solution)/shard_map/ppermute | solution.py:33
  9.1 0.0 copy-start
  9.1 1.2 %copy-done = bf16[4,28,16,256]{3,2,1,0:T(8,128)(2,1)S(1)} copy-done((bf16[4,28,16,256]{3,2,1,0:T(8,128)(2,1)S(1)}, bf16[4,28,16,256]{3,2,1,0:T(8,128)(2,1)}, u32[]{:S(2)}) %copy-start) | copy-done | bytes 917528
  10.3 0.0 copy-start.1
  10.3 0.7 %copy-done.1 = f32[256]{0:T(256)S(1)} copy-done((f32[256]{0:T(256)S(1)}, f32[256]{0:T(256)}, u32[]{:S(2)}) %copy-start.1) | copy-done | bytes 1048
  10.9 0.0 copy-start.2
  10.9 0.7 %copy-done.2 = f32[256]{0:T(256)S(1)} copy-done((f32[256]{0:T(256)S(1)}, f32[256]{0:T(256)}, u32[]{:S(2)}) %copy-start.2) | copy-done | bytes 1048
  11.6 0.0 copy-start.3
  11.6 0.7 copy-done.3
  12.3 0.0 copy-start.4
  12.3 0.7 copy-done.4
  12.9 1.7 %frame_sums.1 = (f32[8,128]{1,0:T(8,128)S(1)}, f32[8,256]{1,0:T(8,128)S(1)}, bf16[4,28,16,256]{3,2,1,0:T(8,128)(2,1)S(1)}, bf16[2,28,16,256]{3,2,1,0:T(8,128)(2,1)}) custom-call(s32[4]{0:T(128)S(1)} %copy-done.3, s32[4]{0:T(128)S(1)} %copy-done.4, bf16[4,28,16,256]{3,2,1,0:T(8,128)(2,1)S(1)} %copy-done, f32[1,256]{1,0:T(1,128)S(1)} %bitcast.9, ...), custom_call_target="tpu_custom_call" | custom-call | tf_op jit(solution)/shard_map/frame_sums/pallas_call | solution.py:78
  14.7 1.3 %collective-permute-start.3 = (f32[8,128]{1,0:T(8,128)S(1)}, f32[8,128]{1,0:T(8,128)S(1)}, u32[]{:S(2)}, u32[]{:S(2)}) collective-permute-start(f32[8,128]{1,0:T(8,128)S(1)} %get-tuple-element.18), channel_id=1, source_target_pairs={{16,48},{24,56},{32,0},{40,8},{48,80},{56,88},{64,32},{72,40},{80,... | collective-permute-start | bytes 12296 | tf_op jit(solution)/shard_map/ppermute | solution.py:344
  16.0 3.5 %collective-permute-done.3 = f32[8,128]{1,0:T(8,128)S(1)} collective-permute-done((f32[8,128]{1,0:T(8,128)S(1)}, f32[8,128]{1,0:T(8,128)S(1)}, u32[]{:S(2)}, u32[]{:S(2)}) %collective-permute-start.3) | collective-permute-done | bytes 4128 | tf_op jit(solution)/shard_map/ppermute | solution.py:344
  19.5 0.1 broadcast_select_fusion
  19.5 0.0 collective-permute-done.2.near.rest_2_
  19.6 6.8 %collective-permute-start.4 = (bf16[36,32,256]{2,1,0:T(8,128)(2,1)S(1)}, bf16[36,32,256]{2,1,0:T(8,128)(2,1)}, u32[]{:S(2)}, u32[]{:S(2)}) collective-permute-start(bf16[36,32,256]{2,1,0:T(8,128)(2,1)S(1)} %collective-permute-done.2.near.rest_2_), channel_id=1, source_target_pairs={{6,0},{3,1},{0,2},{5,3},{2,4},{7,5},{4,6},{1,7},{14,8},{11,9},{8,1... | collective-permute-start | bytes 1769480 | tf_op jit(solution)/shard_map/ppermute | solution.py:33
  26.3 1.3 %collective-permute-start = (bf16[2,28,16,256]{3,2,1,0:T(8,128)(2,1)}, bf16[2,28,16,256]{3,2,1,0:T(8,128)(2,1)S(1)}, u32[]{:S(2)}, u32[]{:S(2)}) collective-permute-start(bf16[2,28,16,256]{3,2,1,0:T(8,128)(2,1)} %get-tuple-element.17), channel_id=1, source_target_pairs={{0,8},{8,16},{16,24},{24,32},{32,40},{40,48},{48,56},{56,64},{64,7... | collective-permute-start | bytes 1376264 | tf_op jit(solution)/shard_map/ppermute | solution.py:19
  27.7 0.7 broadcast_in_dim.2
  28.3 7.2 %all-to-all-start = ((f32[32,8,128]{2,1,0:T(8,128)}), f32[32,8,128]{2,1,0:T(8,128)S(1)}, u32[]{:S(2)}, u32[]{:S(2)}) async-start(f32[32,8,128]{2,1,0:T(8,128)} %broadcast_in_dim.2), calls=%async_computation | async-start | bytes 262144 | tf_op jit(solution)/shard_map/all_to_all | solution.py:351
  35.5 0.1 pad_add_fusion.place
  35.6 0.9 %collective-permute-done.prev = bf16[2,28,16,256]{3,2,1,0:T(8,128)(2,1)S(1)} collective-permute-done((bf16[2,28,16,256]{3,2,1,0:T(8,128)(2,1)}, bf16[2,28,16,256]{3,2,1,0:T(8,128)(2,1)S(1)}, u32[]{:S(2)}, u32[]{:S(2)}) %collective-permute-start) | collective-permute-done | bytes 458784 | tf_op jit(solution)/shard_map/ppermute | solution.py:19
  36.5 0.0 collective-permute-done.1.near_cross.rest_3_
  36.5 6.6 %all-to-all-done = f32[32,8,128]{2,1,0:T(8,128)S(1)} async-done(((f32[32,8,128]{2,1,0:T(8,128)}), f32[32,8,128]{2,1,0:T(8,128)S(1)}, u32[]{:S(2)}, u32[]{:S(2)}) %all-to-all-start) | async-done | bytes 131104 | tf_op jit(solution)/shard_map/all_to_all | solution.py:351
  43.1 0.0 collective-permute-done.4.rest_4_
  43.1 0.7 %swap_message.1 = (bf16[114,32,256]{2,1,0:T(8,128)(2,1)S(1)}, bf16[6,32,256]{2,1,0:T(8,128)(2,1)S(1)}) custom-call(s32[2]{0:T(128)S(1)} %pad_add_fusion.place, bf16[4,28,16,256]{3,2,1,0:T(8,128)(2,1)S(1)} %get-tuple-element.23.feat, bf16[2,28,16,256]{3,2,1,0:T(8,128)(2,1)S(1)} %collective-permute-done.prev, ...), custom_call_target="tpu_custom_call" | custom-call | tf_op jit(solution)/shard_map/swap_message/pallas_call | solution.py:114
  43.8 2.3 %collective-permute-start.6 = (bf16[114,32,256]{2,1,0:T(8,128)(2,1)S(1)}, bf16[114,32,256]{2,1,0:T(8,128)(2,1)S(1)}, u32[]{:S(2)}, u32[]{:S(2)}) collective-permute-start(bf16[114,32,256]{2,1,0:T(8,128)(2,1)S(1)} %get-tuple-element.27), channel_id=1, source_target_pairs={{0,1},{1,0},{2,3},{3,2},{4,5},{5,4},{6,7},{7,6},{8,9},{9,8},{10,11... | collective-permute-start | bytes 5603336 | tf_op jit(solution)/shard_map/ppermute | solution.py:23
  46.1 2.0 %collective-permute-start.7 = (bf16[36,32,256]{2,1,0:T(8,128)(2,1)}, bf16[36,32,256]{2,1,0:T(8,128)(2,1)S(1)}, u32[]{:S(2)}, u32[]{:S(2)}) collective-permute-start(bf16[36,32,256]{2,1,0:T(8,128)(2,1)} %collective-permute-done.4.rest_4_), channel_id=1, source_target_pairs={{0,1},{1,0},{2,3},{3,2},{4,5},{5,4},{6,7},{7,6},{8,9},{9,8},{10,11... | collective-permute-start | bytes 1769480 | tf_op jit(solution)/shard_map/ppermute | solution.py:23
  48.2 2.5 %collective-permute-start.5 = (bf16[6,32,256]{2,1,0:T(8,128)(2,1)S(1)}, bf16[6,32,256]{2,1,0:T(8,128)(2,1)S(1)}, u32[]{:S(2)}, u32[]{:S(2)}) collective-permute-start(bf16[6,32,256]{2,1,0:T(8,128)(2,1)S(1)} %get-tuple-element.26), channel_id=1, source_target_pairs={{7,0},{2,1},{1,2},{4,3},{3,4},{6,5},{5,6},{0,7},{15,8},{10,9},{9,1... | collective-permute-start | bytes 294920 | tf_op jit(solution)/shard_map/ppermute | solution.py:33
  50.7 3.7 %collective-permute-done.5.edge = bf16[6,32,256]{2,1,0:T(8,128)(2,1)S(1)} collective-permute-done((bf16[6,32,256]{2,1,0:T(8,128)(2,1)S(1)}, bf16[6,32,256]{2,1,0:T(8,128)(2,1)S(1)}, u32[]{:S(2)}, u32[]{:S(2)}) %collective-permute-start.5) | collective-permute-done | bytes 98336 | tf_op jit(solution)/shard_map/ppermute | solution.py:33
  54.4 0.0 collective-permute-done.7.rest_5_
  54.4 0.0 collective-permute-done.6.rest_0_
  54.4 13.0 %norm_conv_down.1 = bf16[448,256]{1,0:T(8,128)(2,1)} custom-call(s32[2]{0:T(128)S(1)} %pad_add_fusion.place, f32[4,8,8,128]{3,2,1,0:T(8,128)S(1)} %bitcast.8, f32[8,256]{1,0:T(8,128)S(1)} %get-tuple-element.22.params, bf16[4,28,16,256]{3,2,1,0:T(8,128)(2,1)S(1)} %get-tuple-element.23.feat, bf16[2,28,16,256]{3,2,1,0:T(8,128)(2,1)S(1)} %collective-permute-done.prev, ...), custom_call_target="tpu_custom_call" | custom-call | tf_op jit(solution)/shard_map/norm_conv_down/pallas_call | solution.py:298
  (1 shorter events, 0.0 us)
Async XLA Ops:
  1.2 18.4 %collective-permute-start.2 = (bf16[36,32,256]{2,1,0:T(8,128)(2,1)S(1)}, bf16[36,32,256]{2,1,0:T(8,128)(2,1)S(1)}, u32[]{:S(2)}, u32[]{:S(2)}) collective-permute-start(bf16[36,32,256]{2,1,0:T(8,128)(2,1)S(1)} %pad_maximum_fusion.plain.rest_1_), channel_id=1, source_target_pairs={{6,0},{3,1},{0,2},{5,3},{2,4},{7,5},{4,6},{1,7},{14,8},{11,9},{8,1... | collective-permute-start | bytes 1769480 | tf_op jit(solution)/shard_map/ppermute | solution.py:33
  6.4 30.1 %collective-permute-start.1 = (bf16[36,32,256]{2,1,0:T(8,128)(2,1)S(1)}, bf16[36,32,256]{2,1,0:T(8,128)(2,1)S(1)}, u32[]{:S(2)}, u32[]{:S(2)}) collective-permute-start(bf16[36,32,256]{2,1,0:T(8,128)(2,1)S(1)} %pad_maximum_fusion.plain.rest_1_), channel_id=1, source_target_pairs={{7,0},{2,1},{1,2},{4,3},{3,4},{6,5},{5,6},{0,7},{15,8},{10,9},{9,1... | collective-permute-start | bytes 1769480 | tf_op jit(solution)/shard_map/ppermute | solution.py:33
  9.1 1.2 %copy-start = (bf16[4,28,16,256]{3,2,1,0:T(8,128)(2,1)S(1)}, bf16[4,28,16,256]{3,2,1,0:T(8,128)(2,1)}, u32[]{:S(2)}) copy-start(bf16[4,28,16,256]{3,2,1,0:T(8,128)(2,1)} %feat.1) | copy-start | bytes 2752516
  10.3 0.7 %copy-start.1 = (f32[256]{0:T(256)S(1)}, f32[256]{0:T(256)}, u32[]{:S(2)}) copy-start(f32[256]{0:T(256)} %param.10) | copy-start | bytes 3076
  10.9 0.7 %copy-start.2 = (f32[256]{0:T(256)S(1)}, f32[256]{0:T(256)}, u32[]{:S(2)}) copy-start(f32[256]{0:T(256)} %param.11) | copy-start | bytes 3076
  11.6 0.7 copy-start.3
  12.3 0.7 copy-start.4
  14.7 4.8 %collective-permute-start.3 = (f32[8,128]{1,0:T(8,128)S(1)}, f32[8,128]{1,0:T(8,128)S(1)}, u32[]{:S(2)}, u32[]{:S(2)}) collective-permute-start(f32[8,128]{1,0:T(8,128)S(1)} %get-tuple-element.18), channel_id=1, source_target_pairs={{16,48},{24,56},{32,0},{40,8},{48,80},{56,88},{64,32},{72,40},{80,... | collective-permute-start | bytes 12296 | tf_op jit(solution)/shard_map/ppermute | solution.py:344
  19.6 23.6 %collective-permute-start.4 = (bf16[36,32,256]{2,1,0:T(8,128)(2,1)S(1)}, bf16[36,32,256]{2,1,0:T(8,128)(2,1)}, u32[]{:S(2)}, u32[]{:S(2)}) collective-permute-start(bf16[36,32,256]{2,1,0:T(8,128)(2,1)S(1)} %collective-permute-done.2.near.rest_2_), channel_id=1, source_target_pairs={{6,0},{3,1},{0,2},{5,3},{2,4},{7,5},{4,6},{1,7},{14,8},{11,9},{8,1... | collective-permute-start | bytes 1769480 | tf_op jit(solution)/shard_map/ppermute | solution.py:33
  26.3 10.2 %collective-permute-start = (bf16[2,28,16,256]{3,2,1,0:T(8,128)(2,1)}, bf16[2,28,16,256]{3,2,1,0:T(8,128)(2,1)S(1)}, u32[]{:S(2)}, u32[]{:S(2)}) collective-permute-start(bf16[2,28,16,256]{3,2,1,0:T(8,128)(2,1)} %get-tuple-element.17), channel_id=1, source_target_pairs={{0,8},{8,16},{16,24},{24,32},{32,40},{40,48},{48,56},{56,64},{64,7... | collective-permute-start | bytes 1376264 | tf_op jit(solution)/shard_map/ppermute | solution.py:19
  28.3 14.8 %all-to-all-start = ((f32[32,8,128]{2,1,0:T(8,128)}), f32[32,8,128]{2,1,0:T(8,128)S(1)}, u32[]{:S(2)}, u32[]{:S(2)}) async-start(f32[32,8,128]{2,1,0:T(8,128)} %broadcast_in_dim.2), calls=%async_computation | async-start | bytes 262144 | tf_op jit(solution)/shard_map/all_to_all | solution.py:351
  43.8 10.6 %collective-permute-start.6 = (bf16[114,32,256]{2,1,0:T(8,128)(2,1)S(1)}, bf16[114,32,256]{2,1,0:T(8,128)(2,1)S(1)}, u32[]{:S(2)}, u32[]{:S(2)}) collective-permute-start(bf16[114,32,256]{2,1,0:T(8,128)(2,1)S(1)} %get-tuple-element.27), channel_id=1, source_target_pairs={{0,1},{1,0},{2,3},{3,2},{4,5},{5,4},{6,7},{7,6},{8,9},{9,8},{10,11... | collective-permute-start | bytes 5603336 | tf_op jit(solution)/shard_map/ppermute | solution.py:23
  46.1 8.2 %collective-permute-start.7 = (bf16[36,32,256]{2,1,0:T(8,128)(2,1)}, bf16[36,32,256]{2,1,0:T(8,128)(2,1)S(1)}, u32[]{:S(2)}, u32[]{:S(2)}) collective-permute-start(bf16[36,32,256]{2,1,0:T(8,128)(2,1)} %collective-permute-done.4.rest_4_), channel_id=1, source_target_pairs={{0,1},{1,0},{2,3},{3,2},{4,5},{5,4},{6,7},{7,6},{8,9},{9,8},{10,11... | collective-permute-start | bytes 1769480 | tf_op jit(solution)/shard_map/ppermute | solution.py:23
  48.2 6.2 %collective-permute-start.5 = (bf16[6,32,256]{2,1,0:T(8,128)(2,1)S(1)}, bf16[6,32,256]{2,1,0:T(8,128)(2,1)S(1)}, u32[]{:S(2)}, u32[]{:S(2)}) collective-permute-start(bf16[6,32,256]{2,1,0:T(8,128)(2,1)S(1)} %get-tuple-element.26), channel_id=1, source_target_pairs={{7,0},{2,1},{1,2},{4,3},{3,4},{6,5},{5,6},{0,7},{15,8},{10,9},{9,1... | collective-permute-start | bytes 294920 | tf_op jit(solution)/shard_map/ppermute | solution.py:33

commit v6 on v5

--- a/solution.py
+++ b/solution.py
@@ -49,10 +49,9 @@
     )
 
 
-def pack_kernel(ids, valid, feat, gain, bias, table, params, kept, tail):
+def pack_kernel(ids, valid, feat, gain, bias, table, params, kept):
     frames, height, across, channels = feat.shape
     kept[...] = feat[...]
-    tail[...] = feat[frames - 2 :]
     params[0:1, :] = gain[...]
     params[1:2, :] = bias[...]
 
@@ -81,47 +80,59 @@
             jax.ShapeDtypeStruct((2 * frames, 128), F32),
             jax.ShapeDtypeStruct((8, channels), F32),
             jax.ShapeDtypeStruct(features.shape, BF16),
-            jax.ShapeDtypeStruct((2, *features.shape[1:]), BF16),
         ),
         in_specs=[pl.BlockSpec(memory_space=pltpu.SMEM)] * 2 + [vmem] * 3,
-        out_specs=(vmem,) * 4,
+        out_specs=(vmem,) * 3,
         compiler_params=pltpu.CompilerParams(vmem_limit_bytes=10 << 20),
         name="frame_sums",
     )(clip_ids, frame_valid, features, gain, bias)
 
 
-def swap_kernel(place, feat, prev, plain, near, near_cross, swap, edge):
+def edges_kernel(place, feat, prev, chip_edge, core_edge):
     frames, height, across, channels = feat.shape
-    taps, slice_in, _ = plain.shape
-    for at, piece in enumerate((plain, near, near_cross)):
-        swap[at * taps : (at + 1) * taps] = piece[...]
     for core in range(2):
 
         @pl.when(place[0] % 2 == core)
         def _(core=core):
-            for source, first, count in ((prev, 0, 2), (feat, 2, frames)):
-                first_rows = source[:, 0:2].reshape(count, slice_in, channels)
-                last_rows = source[:, height - 2 :].reshape(count, slice_in, channels)
-                edge[first : first + count] = last_rows if core else first_rows
-                to_core = first_rows if core else last_rows
-                swap[3 * taps + first : 3 * taps + first + count] = to_core
-
-
-def swap_call(place, feat, prev, plain, near, near_cross):
+            for target, side in ((chip_edge, core), (core_edge, 1 - core)):
+                row = side * (height - 2)
+                for source, first, count in ((prev, 0, 2), (feat, 2, frames)):
+                    rows = source[:, row : row + 2].reshape(count, 2 * across, channels)
+                    target[first : first + count] = rows
+
+
+def edges_call(place, feat, prev):
     frames, height, across, channels = feat.shape
-    taps, slice_in, _ = plain.shape
+    vmem = pl.BlockSpec(memory_space=pltpu.VMEM)
+    return pl.pallas_call(
+        edges_kernel,
+        out_shape=(jax.ShapeDtypeStruct((frames + 2, 2 * across, channels), BF16),) * 2,
+        in_specs=[pl.BlockSpec(memory_space=pltpu.SMEM)] + [vmem] * 2,
+        out_specs=(vmem,) * 2,
+        compiler_params=pltpu.CompilerParams(vmem_limit_bytes=8 << 20),
+        name="edge_rows",
+    )(place, feat, prev)
+
+
+def swap_kernel(core_edge, plain, near, swap):
+    taps = plain.shape[0]
+    for at, piece in enumerate((plain, near)):
+        swap[at * taps : (at + 1) * taps] = piece[...]
+    swap[2 * taps :] = core_edge[...]
+
+
+def swap_call(core_edge, plain, near):
+    rows = core_edge.shape[0]
+    taps, slice_in, channels = plain.shape
     vmem = pl.BlockSpec(memory_space=pltpu.VMEM)
     return pl.pallas_call(
         swap_kernel,
-        out_shape=(
-            jax.ShapeDtypeStruct((3 * taps + frames + 2, slice_in, channels), BF16),
-            jax.ShapeDtypeStruct((frames + 2, slice_in, channels), BF16),
-        ),
-        in_specs=[pl.BlockSpec(memory_space=pltpu.SMEM)] + [vmem] * 5,
-        out_specs=(vmem,) * 2,
-        compiler_params=pltpu.CompilerParams(vmem_limit_bytes=10 << 20),
+        out_shape=jax.ShapeDtypeStruct((2 * taps + rows, slice_in, channels), BF16),
+        in_specs=[vmem] * 3,
+        out_specs=vmem,
+        compiler_params=pltpu.CompilerParams(vmem_limit_bytes=8 << 20),
         name="swap_message",
-    )(place, feat, prev, plain, near, near_cross)
+    )(core_edge, plain, near)
 
 
 def held_places(band):
@@ -132,8 +143,8 @@
 
 
 def main_kernel(place, block, params, feat, prev, edge, *rest):
-    swap, pieces = rest[0], rest[1:6]
-    out, w_all, hcol, mixed_all, top, bottom, sems = rest[6:]
+    swap, pieces = rest[0], rest[1:7]
+    out, w_all, hcol, mixed_all, top, bottom, sems = rest[7:]
     frames, height, across, channels = feat.shape
     taps, slice_in = pieces[0].shape[:2]
     taps_conv = 27
@@ -141,7 +152,7 @@
     band = place[0]
     places = held_places(band) + held_places(band + 1 - 2 * (band % 2))
     sources = list(pieces[:4])
-    sources += [swap.at[at * taps : (at + 1) * taps] for at in range(3)] + [pieces[4]]
+    sources += [swap.at[at * taps : (at + 1) * taps] for at in range(2)] + list(pieces[4:])
     copies = []
     for at in range(8):
         start = pl.multiple_of(places[at] * slice_in, slice_in)
@@ -154,7 +165,7 @@
 
         @pl.when(band % 2 == core)
         def _(core=core):
-            swap_rows = swap[3 * taps :].reshape(frames + 2, 2, across, channels)
+            swap_rows = swap[2 * taps :].reshape(frames + 2, 2, across, channels)
             edge_rows = edge[...].reshape(frames + 2, 2, across, channels)
             top[...] = (swap_rows if core else edge_rows)[:, 1:2]
             bottom[...] = edge_rows if core else swap_rows
@@ -299,7 +310,7 @@
         main_kernel,
         out_shape=jax.ShapeDtypeStruct((points, channels), BF16),
         in_specs=[pl.BlockSpec(memory_space=pltpu.SMEM)]
-        + [vmem] * 11,
+        + [vmem] * 12,
         out_specs=vmem,
         scratch_shapes=[
             pltpu.VMEM((taps, channels, channels), BF16),
@@ -321,6 +332,7 @@
 
     bands, times = lax.axis_size("rows"), lax.axis_size("tm")
 
+    prev = shifted(features[frames - 2 :], "tm", 1)
     plain = jnp.concatenate(
         [
             conv_weight.reshape(27, slice_in, channels),
@@ -329,14 +341,13 @@
         axis=0,
     )
     near = ring_move(plain, "rows", 0)
-    table, params, feat, tail = pack_call(
+    table, params, feat = pack_call(
         clip_ids,
         frame_valid,
         features,
         norm_gain.reshape(1, channels),
         norm_bias.reshape(1, channels),
     )
-    prev = shifted(tail, "tm", 1)
     near_cross = ring_move(plain, "rows", 1)
 
     half = BLOCK // 2
@@ -344,8 +355,17 @@
     sent = lax.ppermute(table, "tm", [pair for pair in pairs if 0 <= pair[1] < times])
     row = lax.broadcasted_iota(jnp.int32, table.shape, 0)
     rows = jnp.where(row < frames, table, sent)
-    near, rows = lax.optimization_barrier((near, rows))
+
+    near, prev, rows = lax.optimization_barrier((near, prev, rows))
+    chip_edge, core_edge = edges_call(place, feat, prev)
+    edge = ring_move(chip_edge, "rows", 1)
+    message = swap_call(core_edge, plain, near)
+    near, near_cross, message, edge, rows = lax.optimization_barrier(
+        (near, near_cross, message, edge, rows)
+    )
     far = ring_move(near, "rows", 0)
+    swap = swapped(message, "rows", 1)
+    cross_swapped = swapped(near_cross, "rows", 1)
     size = BLOCK * bands
     groups = [[first + at for at in range(size)] for first in range(0, bands * times, size)]
     block = lax.all_to_all(
@@ -357,11 +377,8 @@
         tiled=True,
     ).reshape(BLOCK, bands, *rows.shape)
 
-    prev, near_cross, far, block = lax.optimization_barrier((prev, near_cross, far, block))
-    swap, edge = swap_call(place, feat, prev, plain, near, near_cross)
-    swap = swapped(swap, "rows", 1)
-    edge = ring_move(edge, "rows", 1)
-    pieces = [plain, near, near_cross, far, swapped(far, "rows", 1)]
+    far, block = lax.optimization_barrier((far, block))
+    pieces = [plain, near, near_cross, far, cross_swapped, swapped(far, "rows", 1)]
 
     out = main_call(place, block, params, feat, prev, edge, swap, pieces)
     return out.reshape(frames, height // 2, across // 2, channels)

time: 67.9 us -> 70.3 us (1.035)
  starting transfers between devices: 31.3 us -> 35.1 us
  local copies, waits for them, and re-layouts: 4.51 us -> 1.49 us
  Pallas kernels: 15.4 us -> 16.2 us
    ppermute x2 -> x3, starting transfers between devices: 4.33 us -> 10.3 us  [swapped(): lax.ppermute(value, axis, [(i, i ^ bits) for i in range(lax.axis_size(axi...]
    unnamed x10, local copies, waits for them, and re-layouts: 3.84 us -> 0.02 us
    ppermute x1, waiting for transfers between devices: 0.93 us -> 3.61 us  [shifted(): lax.ppermute(value, axis, [(source, source + steps) for source in range(f...]
    ppermute x4, waiting for transfers between devices: 3.69 us -> 1.14 us  [ring_move(): return lax.ppermute(value, axis, pairs)]
    ppermute x4, starting transfers between devices: 17.2 us -> 14.7 us  [ring_move(): return lax.ppermute(value, axis, pairs)]
    ppermute x1, starting transfers between devices: 1.32 us -> 3.22 us  [shifted(): lax.ppermute(value, axis, [(source, source + steps) for source in range(f...]
    ppermute x2 -> x3, waiting for transfers between devices: 0.01 us -> 1.81 us  [swapped(): lax.ppermute(value, axis, [(i, i ^ bits) for i in range(lax.axis_size(axi...]
    all_to_all x1, starting transfers between devices: 7.16 us -> 5.57 us  [body(): lax.all_to_all(jnp.broadcast_to(rows[None], (size, *rows.shape)), ('tm',...]
  transfers between devices with their start and end apart: 9 -> 10, of which waited for: 4 -> 5; matrix products, arithmetic and copies ran while one was open for 1% -> 2% of each run, Pallas kernels for 3% -> 4%
where the time goes in v6:
time: 70.3 us; the launch traced here: 69.8 us
  starting transfers between devices  35.1 us (50%)
  Pallas kernels  16.2 us (23%)
  waiting for transfers between devices  15.5 us (22%)
  local copies, waits for them, and re-layouts  1.49 us (2%)
  other arithmetic  1.37 us (2%)
    ppermute x4, starting transfers between devices, ring_move(): return lax.ppermute(value, axis, pairs)  14.7 us
    pallas_call x1, Pallas kernels, main_call(): pl.pallas_call(main_kernel, out_shape=jax.ShapeDtypeStruct((points, chann...  13.5 us
    ppermute x3, starting transfers between devices, swapped(): lax.ppermute(value, axis, [(i, i ^ bits) for i in range(lax.axis_size(axi...  10.3 us
    all_to_all x1, starting transfers between devices, body(): lax.all_to_all(jnp.broadcast_to(rows[None], (size, *rows.shape)), ('tm',...  5.57 us
    all_to_all x1, waiting for transfers between devices, body(): lax.all_to_all(jnp.broadcast_to(rows[None], (size, *rows.shape)), ('tm',...  5.47 us
    ppermute x1, waiting for transfers between devices, shifted(): lax.ppermute(value, axis, [(source, source + steps) for source in range(f...  3.61 us
    ppermute x1, waiting for transfers between devices, body(): lax.ppermute(table, 'tm', [pair for pair in pairs if 0 <= pair[1] < times])  3.41 us
    ppermute x1, starting transfers between devices, shifted(): lax.ppermute(value, axis, [(source, source + steps) for source in range(f...  3.22 us
  transfers between devices with their start and end apart: 10, of which 5 were waited for; matrix products, arithmetic and copies ran while one was open for 2% of the time, Pallas kernels for 4%

profile of v6, /device:TPU:1, one launch (start us, length us, event | category | flops | bytes accessed | tf_op | source)
XLA Modules:
  0.0 69.8 jit_solution(12815963092536171313)
XLA Ops:
  0.0 0.0 copy-start
  0.0 0.0 copy-start.3
  0.0 0.0 copy-start.4
  0.0 0.0 copy-start.1
  0.0 0.0 copy-start.2
  0.0 1.2 %pad_maximum_fusion.plain.rest_1_ = bf16[36,32,256]{2,1,0:T(8,128)(2,1)S(1)} fusion(bf16[9,32,256]{2,1,0:T(8,128)(2,1)} %bitcast.12, bf16[27,32,256]{2,1,0:T(8,128)(2,1)} %bitcast.11), kind=kLoop, calls=%fused_computation | loop fusion | flops 294912 | bytes 1179648 | tf_op jit(solution)/shard_map/concatenate | solution.py:336
  1.2 5.2 %collective-permute-start = (bf16[36,32,256]{2,1,0:T(8,128)(2,1)S(1)}, bf16[36,32,256]{2,1,0:T(8,128)(2,1)S(1)}, u32[]{:S(2)}, u32[]{:S(2)}) collective-permute-start(bf16[36,32,256]{2,1,0:T(8,128)(2,1)S(1)} %pad_maximum_fusion.plain.rest_1_), channel_id=1, source_target_pairs={{6,0},{3,1},{0,2},{5,3},{2,4},{7,5},{4,6},{1,7},{14,8},{11,9},{8,1... | collective-permute-start | bytes 1769480 | tf_op jit(solution)/shard_map/ppermute | solution.py:33
  6.5 2.7 %collective-permute-start.3 = (bf16[36,32,256]{2,1,0:T(8,128)(2,1)S(1)}, bf16[36,32,256]{2,1,0:T(8,128)(2,1)S(1)}, u32[]{:S(2)}, u32[]{:S(2)}) collective-permute-start(bf16[36,32,256]{2,1,0:T(8,128)(2,1)S(1)} %pad_maximum_fusion.plain.rest_1_), channel_id=1, source_target_pairs={{7,0},{2,1},{1,2},{4,3},{3,4},{6,5},{5,6},{0,7},{15,8},{10,9},{9,1... | collective-permute-start | bytes 1769480 | tf_op jit(solution)/shard_map/ppermute | solution.py:33
  9.2 0.0 copy-done
  9.2 0.8 %slice.3 = bf16[2,28,16,256]{3,2,1,0:T(8,128)(2,1)} slice(bf16[4,28,16,256]{3,2,1,0:T(8,128)(2,1)S(1)} %copy-done), slice={[2:4], [0:28], [0:16], [0:256]} | slice | bytes 917504 | tf_op jit(solution)/shard_map/slice | solution.py:335
  10.0 3.2 %collective-permute-start.1 = (bf16[2,28,16,256]{3,2,1,0:T(8,128)(2,1)}, bf16[2,28,16,256]{3,2,1,0:T(8,128)(2,1)S(1)}, u32[]{:S(2)}, u32[]{:S(2)}) collective-permute-start(bf16[2,28,16,256]{3,2,1,0:T(8,128)(2,1)} %slice.3), channel_id=1, source_target_pairs={{0,8},{8,16},{16,24},{24,32},{32,40},{40,48},{48,56},{56,64},{64,7... | collective-permute-start | bytes 1376264 | tf_op jit(solution)/shard_map/ppermute | solution.py:19
  13.2 0.0 copy-done.3
  13.2 0.0 copy-done.4
  13.2 0.0 copy-done.1
  13.2 0.0 copy-done.2
  13.2 1.0 %frame_sums.1 = (f32[8,128]{1,0:T(8,128)S(1)}, f32[8,256]{1,0:T(8,128)S(1)}, bf16[4,28,16,256]{3,2,1,0:T(8,128)(2,1)S(1)}) custom-call(s32[4]{0:T(128)S(1)} %copy-done.3, s32[4]{0:T(128)S(1)} %copy-done.4, bf16[4,28,16,256]{3,2,1,0:T(8,128)(2,1)S(1)} %copy-done, f32[1,256]{1,0:T(1,128)S(1)} %bitcast.9, f32[1,256]{1,0:T(1,128)S(1)} %bitcast.10), custom_call_target="tpu_custom_call" | custom-call | tf_op jit(solution)/shard_map/frame_sums/pallas_call | solution.py:77
  14.2 1.3 %collective-permute-start.2 = (f32[8,128]{1,0:T(8,128)S(1)}, f32[8,128]{1,0:T(8,128)S(1)}, u32[]{:S(2)}, u32[]{:S(2)}) collective-permute-start(f32[8,128]{1,0:T(8,128)S(1)} %get-tuple-element.20), channel_id=1, source_target_pairs={{16,48},{24,56},{32,0},{40,8},{48,80},{56,88},{64,32},{72,40},{80,... | collective-permute-start | bytes 12296 | tf_op jit(solution)/shard_map/ppermute | solution.py:355
  15.6 0.1 pad_add_fusion.place
  15.6 3.4 %collective-permute-done.2 = f32[8,128]{1,0:T(8,128)S(1)} collective-permute-done((f32[8,128]{1,0:T(8,128)S(1)}, f32[8,128]{1,0:T(8,128)S(1)}, u32[]{:S(2)}, u32[]{:S(2)}) %collective-permute-start.2) | collective-permute-done | bytes 4128 | tf_op jit(solution)/shard_map/ppermute | solution.py:355
  19.1 0.1 broadcast_select_fusion
  19.1 3.6 %collective-permute-done.1.prev = bf16[2,28,16,256]{3,2,1,0:T(8,128)(2,1)S(1)} collective-permute-done((bf16[2,28,16,256]{3,2,1,0:T(8,128)(2,1)}, bf16[2,28,16,256]{3,2,1,0:T(8,128)(2,1)S(1)}, u32[]{:S(2)}, u32[]{:S(2)}) %collective-permute-start.1) | collective-permute-done | bytes 458784 | tf_op jit(solution)/shard_map/ppermute | solution.py:19
  22.7 0.0 collective-permute-done.near.rest_2_
  22.7 0.6 edge_rows.1
  23.3 4.2 %collective-permute-start.4 = (bf16[6,32,256]{2,1,0:T(8,128)(2,1)S(1)}, bf16[6,32,256]{2,1,0:T(8,128)(2,1)S(1)}, u32[]{:S(2)}, u32[]{:S(2)}) collective-permute-start(bf16[6,32,256]{2,1,0:T(8,128)(2,1)S(1)} %get-tuple-element.25), channel_id=1, source_target_pairs={{7,0},{2,1},{1,2},{4,3},{3,4},{6,5},{5,6},{0,7},{15,8},{10,9},{9,1... | collective-permute-start | bytes 294920 | tf_op jit(solution)/shard_map/ppermute | solution.py:33
  27.5 1.1 %swap_message.1 = bf16[78,32,256]{2,1,0:T(8,128)(2,1)} custom-call(bf16[6,32,256]{2,1,0:T(8,128)(2,1)S(1)} %get-tuple-element.24.core_edge, bf16[36,32,256]{2,1,0:T(8,128)(2,1)S(1)} %pad_maximum_fusion.plain.rest_1_, bf16[36,32,256]{2,1,0:T(8,128)(2,1)S(1)} %collective-permute-done.near.rest_2_), custom_call_target="tpu_custom_call" | custom-call | tf_op jit(solution)/shard_map/swap_message/pallas_call | solution.py:128
  28.7 0.0 collective-permute-done.3.rest_3_
  28.7 1.1 %collective-permute-done.4.edge = bf16[6,32,256]{2,1,0:T(8,128)(2,1)S(1)} collective-permute-done((bf16[6,32,256]{2,1,0:T(8,128)(2,1)S(1)}, bf16[6,32,256]{2,1,0:T(8,128)(2,1)S(1)}, u32[]{:S(2)}, u32[]{:S(2)}) %collective-permute-start.4) | collective-permute-done | bytes 98336 | tf_op jit(solution)/shard_map/ppermute | solution.py:33
  29.8 5.8 %collective-permute-start.6 = (bf16[78,32,256]{2,1,0:T(8,128)(2,1)}, bf16[78,32,256]{2,1,0:T(8,128)(2,1)}, u32[]{:S(2)}, u32[]{:S(2)}) collective-permute-start(bf16[78,32,256]{2,1,0:T(8,128)(2,1)} %swap_message.1), channel_id=1, source_target_pairs={{0,1},{1,0},{2,3},{3,2},{4,5},{5,4},{6,7},{7,6},{8,9},{9,8},{10,11... | collective-permute-start | bytes 3833864 | tf_op jit(solution)/shard_map/ppermute | solution.py:23
  35.6 2.6 %collective-permute-start.5 = (bf16[36,32,256]{2,1,0:T(8,128)(2,1)S(1)}, bf16[36,32,256]{2,1,0:T(8,128)(2,1)}, u32[]{:S(2)}, u32[]{:S(2)}) collective-permute-start(bf16[36,32,256]{2,1,0:T(8,128)(2,1)S(1)} %collective-permute-done.near.rest_2_), channel_id=1, source_target_pairs={{6,0},{3,1},{0,2},{5,3},{2,4},{7,5},{4,6},{1,7},{14,8},{11,9},{8,1... | collective-permute-start | bytes 1769480 | tf_op jit(solution)/shard_map/ppermute | solution.py:33
  38.3 0.7 broadcast_in_dim.2
  39.0 5.6 %all-to-all-start = ((f32[32,8,128]{2,1,0:T(8,128)}), f32[32,8,128]{2,1,0:T(8,128)S(1)}, u32[]{:S(2)}, u32[]{:S(2)}) async-start(f32[32,8,128]{2,1,0:T(8,128)} %broadcast_in_dim.2), calls=%async_computation | async-start | bytes 262144 | tf_op jit(solution)/shard_map/all_to_all | solution.py:371
  44.5 2.1 %collective-permute-start.7 = (bf16[36,32,256]{2,1,0:T(8,128)(2,1)S(1)}, bf16[36,32,256]{2,1,0:T(8,128)(2,1)}, u32[]{:S(2)}, u32[]{:S(2)}) collective-permute-start(bf16[36,32,256]{2,1,0:T(8,128)(2,1)S(1)} %collective-permute-done.3.rest_3_), channel_id=1, source_target_pairs={{0,1},{1,0},{2,3},{3,2},{4,5},{5,4},{6,7},{7,6},{8,9},{9,8},{10,11... | collective-permute-start | bytes 1769480 | tf_op jit(solution)/shard_map/ppermute | solution.py:23
  46.7 5.5 %all-to-all-done = f32[32,8,128]{2,1,0:T(8,128)S(1)} async-done(((f32[32,8,128]{2,1,0:T(8,128)}), f32[32,8,128]{2,1,0:T(8,128)S(1)}, u32[]{:S(2)}, u32[]{:S(2)}) %all-to-all-start) | async-done | bytes 131104 | tf_op jit(solution)/shard_map/all_to_all | solution.py:371
  52.2 0.0 collective-permute-done.5.rest_4_
  52.2 2.3 %collective-permute-start.8 = (bf16[36,32,256]{2,1,0:T(8,128)(2,1)}, bf16[36,32,256]{2,1,0:T(8,128)(2,1)S(1)}, u32[]{:S(2)}, u32[]{:S(2)}) collective-permute-start(bf16[36,32,256]{2,1,0:T(8,128)(2,1)} %collective-permute-done.5.rest_4_), channel_id=1, source_target_pairs={{0,1},{1,0},{2,3},{3,2},{4,5},{5,4},{6,7},{7,6},{8,9},{9,8},{10,11... | collective-permute-start | bytes 1769480 | tf_op jit(solution)/shard_map/ppermute | solution.py:23
  54.5 0.0 collective-permute-done.7.rest_5_
  54.5 1.8 %collective-permute-done.8.rest_6_ = bf16[36,32,256]{2,1,0:T(8,128)(2,1)S(1)} collective-permute-done((bf16[36,32,256]{2,1,0:T(8,128)(2,1)}, bf16[36,32,256]{2,1,0:T(8,128)(2,1)S(1)}, u32[]{:S(2)}, u32[]{:S(2)}) %collective-permute-start.8) | collective-permute-done | bytes 589856 | tf_op jit(solution)/shard_map/ppermute | solution.py:23
  56.3 0.0 collective-permute-done.6.rest_0_
  56.3 13.5 %norm_conv_down.1 = bf16[448,256]{1,0:T(8,128)(2,1)} custom-call(s32[2]{0:T(128)S(1)} %pad_add_fusion.place, f32[4,8,8,128]{3,2,1,0:T(8,128)S(1)} %bitcast.8, f32[8,256]{1,0:T(8,128)S(1)} %get-tuple-element.30.params, bf16[4,28,16,256]{3,2,1,0:T(8,128)(2,1)S(1)} %get-tuple-element.22.feat, bf16[2,28,16,256]{3,2,1,0:T(8,128)(2,1)S(1)} %collective-permute-done.1.prev, ...), custom_call_target="tpu_custom_call" | custom-call | tf_op jit(solution)/shard_map/norm_conv_down/pallas_call | solution.py:309
  (1 shorter events, 0.0 us)
Async XLA Ops:
  0.0 9.2 %copy-start = (bf16[4,28,16,256]{3,2,1,0:T(8,128)(2,1)S(1)}, bf16[4,28,16,256]{3,2,1,0:T(8,128)(2,1)}, u32[]{:S(2)}) copy-start(bf16[4,28,16,256]{3,2,1,0:T(8,128)(2,1)} %feat.1) | copy-start | bytes 2752516
  0.0 13.2 %copy-start.3 = (s32[4]{0:T(128)S(1)}, s32[4]{0:T(128)}, u32[]{:S(2)}) copy-start(s32[4]{0:T(128)} %ids.1) | copy-start | bytes 52
  0.0 13.2 %copy-start.4 = (s32[4]{0:T(128)S(1)}, s32[4]{0:T(128)}, u32[]{:S(2)}) copy-start(s32[4]{0:T(128)} %valid.1) | copy-start | bytes 52
  0.0 13.2 %copy-start.1 = (f32[256]{0:T(256)S(1)}, f32[256]{0:T(256)}, u32[]{:S(2)}) copy-start(f32[256]{0:T(256)} %param.10) | copy-start | bytes 3076
  0.0 13.2 %copy-start.2 = (f32[256]{0:T(256)S(1)}, f32[256]{0:T(256)}, u32[]{:S(2)}) copy-start(f32[256]{0:T(256)} %param.11) | copy-start | bytes 3076
  1.2 21.5 %collective-permute-start = (bf16[36,32,256]{2,1,0:T(8,128)(2,1)S(1)}, bf16[36,32,256]{2,1,0:T(8,128)(2,1)S(1)}, u32[]{:S(2)}, u32[]{:S(2)}) collective-permute-start(bf16[36,32,256]{2,1,0:T(8,128)(2,1)S(1)} %pad_maximum_fusion.plain.rest_1_), channel_id=1, source_target_pairs={{6,0},{3,1},{0,2},{5,3},{2,4},{7,5},{4,6},{1,7},{14,8},{11,9},{8,1... | collective-permute-start | bytes 1769480 | tf_op jit(solution)/shard_map/ppermute | solution.py:33
  6.5 22.2 %collective-permute-start.3 = (bf16[36,32,256]{2,1,0:T(8,128)(2,1)S(1)}, bf16[36,32,256]{2,1,0:T(8,128)(2,1)S(1)}, u32[]{:S(2)}, u32[]{:S(2)}) collective-permute-start(bf16[36,32,256]{2,1,0:T(8,128)(2,1)S(1)} %pad_maximum_fusion.plain.rest_1_), channel_id=1, source_target_pairs={{7,0},{2,1},{1,2},{4,3},{3,4},{6,5},{5,6},{0,7},{15,8},{10,9},{9,1... | collective-permute-start | bytes 1769480 | tf_op jit(solution)/shard_map/ppermute | solution.py:33
  10.0 12.8 %collective-permute-start.1 = (bf16[2,28,16,256]{3,2,1,0:T(8,128)(2,1)}, bf16[2,28,16,256]{3,2,1,0:T(8,128)(2,1)S(1)}, u32[]{:S(2)}, u32[]{:S(2)}) collective-permute-start(bf16[2,28,16,256]{3,2,1,0:T(8,128)(2,1)} %slice.3), channel_id=1, source_target_pairs={{0,8},{8,16},{16,24},{24,32},{32,40},{40,48},{48,56},{56,64},{64,7... | collective-permute-start | bytes 1376264 | tf_op jit(solution)/shard_map/ppermute | solution.py:19
  14.2 4.8 %collective-permute-start.2 = (f32[8,128]{1,0:T(8,128)S(1)}, f32[8,128]{1,0:T(8,128)S(1)}, u32[]{:S(2)}, u32[]{:S(2)}) collective-permute-start(f32[8,128]{1,0:T(8,128)S(1)} %get-tuple-element.20), channel_id=1, source_target_pairs={{16,48},{24,56},{32,0},{40,8},{48,80},{56,88},{64,32},{72,40},{80,... | collective-permute-start | bytes 12296 | tf_op jit(solution)/shard_map/ppermute | solution.py:355
  23.3 6.5 %collective-permute-start.4 = (bf16[6,32,256]{2,1,0:T(8,128)(2,1)S(1)}, bf16[6,32,256]{2,1,0:T(8,128)(2,1)S(1)}, u32[]{:S(2)}, u32[]{:S(2)}) collective-permute-start(bf16[6,32,256]{2,1,0:T(8,128)(2,1)S(1)} %get-tuple-element.25), channel_id=1, source_target_pairs={{7,0},{2,1},{1,2},{4,3},{3,4},{6,5},{5,6},{0,7},{15,8},{10,9},{9,1... | collective-permute-start | bytes 294920 | tf_op jit(solution)/shard_map/ppermute | solution.py:33
  29.8 26.5 %collective-permute-start.6 = (bf16[78,32,256]{2,1,0:T(8,128)(2,1)}, bf16[78,32,256]{2,1,0:T(8,128)(2,1)}, u32[]{:S(2)}, u32[]{:S(2)}) collective-permute-start(bf16[78,32,256]{2,1,0:T(8,128)(2,1)} %swap_message.1), channel_id=1, source_target_pairs={{0,1},{1,0},{2,3},{3,2},{4,5},{5,4},{6,7},{7,6},{8,9},{9,8},{10,11... | collective-permute-start | bytes 3833864 | tf_op jit(solution)/shard_map/ppermute | solution.py:23
  35.6 16.5 %collective-permute-start.5 = (bf16[36,32,256]{2,1,0:T(8,128)(2,1)S(1)}, bf16[36,32,256]{2,1,0:T(8,128)(2,1)}, u32[]{:S(2)}, u32[]{:S(2)}) collective-permute-start(bf16[36,32,256]{2,1,0:T(8,128)(2,1)S(1)} %collective-permute-done.near.rest_2_), channel_id=1, source_target_pairs={{6,0},{3,1},{0,2},{5,3},{2,4},{7,5},{4,6},{1,7},{14,8},{11,9},{8,1... | collective-permute-start | bytes 1769480 | tf_op jit(solution)/shard_map/ppermute | solution.py:33
  39.0 13.2 %all-to-all-start = ((f32[32,8,128]{2,1,0:T(8,128)}), f32[32,8,128]{2,1,0:T(8,128)S(1)}, u32[]{:S(2)}, u32[]{:S(2)}) async-start(f32[32,8,128]{2,1,0:T(8,128)} %broadcast_in_dim.2), calls=%async_computation | async-start | bytes 262144 | tf_op jit(solution)/shard_map/all_to_all | solution.py:371
  44.5 9.9 %collective-permute-start.7 = (bf16[36,32,256]{2,1,0:T(8,128)(2,1)S(1)}, bf16[36,32,256]{2,1,0:T(8,128)(2,1)}, u32[]{:S(2)}, u32[]{:S(2)}) collective-permute-start(bf16[36,32,256]{2,1,0:T(8,128)(2,1)S(1)} %collective-permute-done.3.rest_3_), channel_id=1, source_target_pairs={{0,1},{1,0},{2,3},{3,2},{4,5},{5,4},{6,7},{7,6},{8,9},{9,8},{10,11... | collective-permute-start | bytes 1769480 | tf_op jit(solution)/shard_map/ppermute | solution.py:23
  52.2 4.1 %collective-permute-start.8 = (bf16[36,32,256]{2,1,0:T(8,128)(2,1)}, bf16[36,32,256]{2,1,0:T(8,128)(2,1)S(1)}, u32[]{:S(2)}, u32[]{:S(2)}) collective-permute-start(bf16[36,32,256]{2,1,0:T(8,128)(2,1)} %collective-permute-done.5.rest_4_), channel_id=1, source_target_pairs={{0,1},{1,0},{2,3},{3,2},{4,5},{5,4},{6,7},{7,6},{8,9},{9,8},{10,11... | collective-permute-start | bytes 1769480 | tf_op jit(solution)/shard_map/ppermute | solution.py:23

commit v7 on v2

--- a/solution.py
+++ b/solution.py
@@ -83,7 +83,7 @@
         ),
         in_specs=[pl.BlockSpec(memory_space=pltpu.SMEM)] * 2 + [vmem] * 3,
         out_specs=(vmem,) * 3,
-        compiler_params=pltpu.CompilerParams(vmem_limit_bytes=24 << 20),
+        compiler_params=pltpu.CompilerParams(vmem_limit_bytes=10 << 20),
         name="frame_sums",
     )(clip_ids, frame_valid, features, gain, bias)
 
@@ -115,7 +115,7 @@
         ),
         in_specs=[pl.BlockSpec(memory_space=pltpu.SMEM)] + [vmem] * 3,
         out_specs=(vmem,) * 2,
-        compiler_params=pltpu.CompilerParams(vmem_limit_bytes=16 << 20),
+        compiler_params=pltpu.CompilerParams(vmem_limit_bytes=8 << 20),
         name="edge_rows",
     )(place, feat, prev, plain)
 
@@ -307,7 +307,7 @@
             pltpu.VMEM((frames + 2, 2, across, channels), BF16),
             pltpu.SemaphoreType.DMA((8,)),
         ],
-        compiler_params=pltpu.CompilerParams(vmem_limit_bytes=28 << 20),
+        compiler_params=pltpu.CompilerParams(vmem_limit_bytes=24 << 20),
         name="norm_conv_down",
     )(place, block, params, feat, prev, edge, *pieces)
 
@@ -347,8 +347,9 @@
     far = ring_move(near, "rows", 0)
     near_swapped = swapped(near, "rows", 1)
     swap, edge = edges_call(place, feat, prev, plain)
+    edge = ring_move(edge, "rows", 1)
+    swap, edge = lax.optimization_barrier((swap, edge))
     other = swapped(swap, "rows", 1)
-    edge = ring_move(edge, "rows", 1)
     near_cross, rows = lax.optimization_barrier((near_cross, rows))
     cross_swapped = swapped(near_cross, "rows", 1)
 

time: 63.8 us -> 63.3 us (level)
  Pallas kernels: 15.8 us -> 14.9 us
  local copies, waits for them, and re-layouts: 2.48 us -> 3.35 us
    ppermute x4, waiting for transfers between devices: 2.69 us -> 0.01 us  [ring_move(): return lax.ppermute(value, axis, pairs)]
    ppermute x4, waiting for transfers between devices: 0.01 us -> 1.8 us  [swapped(): lax.ppermute(value, axis, [(i, i ^ bits) for i in range(lax.axis_size(axi...]
    all_to_all x1, waiting for transfers between devices: 0.01 us -> 1.11 us  [body(): lax.all_to_all(jnp.broadcast_to(rows[None], (size, *rows.shape)), ('tm',...]
    pallas_call x1, Pallas kernels: 1.48 us -> 0.6 us  [edges_call(): pl.pallas_call(edges_kernel, out_shape=(jax.ShapeDtypeStruct((taps + fram...]
    unnamed x14 -> x16, local copies, waits for them, and re-layouts: 1.73 us -> 2.6 us
    ppermute x4, starting transfers between devices: 16.6 us -> 15.9 us  [ring_move(): return lax.ppermute(value, axis, pairs)]
  transfers between devices with their start and end apart: 11 -> 11, of which waited for: 2 -> 3; matrix products, arithmetic and copies ran while one was open for 1% -> 1% of each run, Pallas kernels for 4% -> 3%
where the time goes in v7:
time: 63.3 us; the launch traced here: 62.7 us
  starting transfers between devices  36.4 us (58%)
  Pallas kernels  14.9 us (24%)
  waiting for transfers between devices  6.41 us (10%)
  local copies, waits for them, and re-layouts  3.35 us (5%)
  other arithmetic  1.37 us (2%)
    ppermute x4, starting transfers between devices, ring_move(): return lax.ppermute(value, axis, pairs)  15.9 us
    pallas_call x1, Pallas kernels, main_call(): pl.pallas_call(main_kernel, out_shape=jax.ShapeDtypeStruct((points, chann...  13.3 us
    ppermute x4, starting transfers between devices, swapped(): lax.ppermute(value, axis, [(i, i ^ bits) for i in range(lax.axis_size(axi...  8.78 us
    all_to_all x1, starting transfers between devices, body(): lax.all_to_all(jnp.broadcast_to(rows[None], (size, *rows.shape)), ('tm',...  7.21 us
    ppermute x1, waiting for transfers between devices, body(): lax.ppermute(table, 'tm', [pair for pair in pairs if 0 <= pair[1] < times])  3.49 us
    ppermute x1, starting transfers between devices, shifted(): lax.ppermute(value, axis, [(source, source + steps) for source in range(f...  3.23 us
    unnamed x16, local copies, waits for them, and re-layouts  2.6 us
    ppermute x4, waiting for transfers between devices, swapped(): lax.ppermute(value, axis, [(i, i ^ bits) for i in range(lax.axis_size(axi...  1.8 us
  transfers between devices with their start and end apart: 11, of which 3 were waited for; matrix products, arithmetic and copies ran while one was open for 1% of the time, Pallas kernels for 3%

profile of v7, /device:TPU:1, one launch (start us, length us, event | category | flops | bytes accessed | tf_op | source)
XLA Modules:
  0.0 62.7 jit_solution(11937874742110295572)
XLA Ops:
  0.0 0.0 copy-start
  0.0 1.2 %pad_maximum_fusion.plain.rest_0_ = bf16[36,32,256]{2,1,0:T(8,128)(2,1)S(1)} fusion(bf16[9,32,256]{2,1,0:T(8,128)(2,1)} %bitcast.12, bf16[27,32,256]{2,1,0:T(8,128)(2,1)} %bitcast.11), kind=kLoop, calls=%fused_computation | loop fusion | flops 294912 | bytes 1179648 | tf_op jit(solution)/shard_map/concatenate | solution.py:323
  1.2 5.2 %collective-permute-start = (bf16[36,32,256]{2,1,0:T(8,128)(2,1)S(1)}, bf16[36,32,256]{2,1,0:T(8,128)(2,1)S(1)}, u32[]{:S(2)}, u32[]{:S(2)}) collective-permute-start(bf16[36,32,256]{2,1,0:T(8,128)(2,1)S(1)} %pad_maximum_fusion.plain.rest_0_), channel_id=1, source_target_pairs={{6,0},{3,1},{0,2},{5,3},{2,4},{7,5},{4,6},{1,7},{14,8},{11,9},{8,1... | collective-permute-start | bytes 1769480 | tf_op jit(solution)/shard_map/ppermute | solution.py:33
  6.4 0.0 copy-done
  6.5 0.0 copy-start.4
  6.5 0.0 copy-start.6
  6.5 3.2 %collective-permute-start.1 = (bf16[2,28,16,256]{3,2,1,0:T(8,128)(2,1)S(1)}, bf16[2,28,16,256]{3,2,1,0:T(8,128)(2,1)S(1)}, u32[]{:S(2)}, u32[]{:S(2)}) collective-permute-start(bf16[2,28,16,256]{3,2,1,0:T(8,128)(2,1)S(1)} %slice.3), channel_id=1, source_target_pairs={{0,8},{8,16},{16,24},{24,32},{32,40},{40,48},{48,56},{56,64},{64,7... | collective-permute-start | bytes 1376264 | tf_op jit(solution)/shard_map/ppermute | solution.py:19
  9.8 3.0 %collective-permute-start.4 = (bf16[36,32,256]{2,1,0:T(8,128)(2,1)S(1)}, bf16[36,32,256]{2,1,0:T(8,128)(2,1)S(1)}, u32[]{:S(2)}, u32[]{:S(2)}) collective-permute-start(bf16[36,32,256]{2,1,0:T(8,128)(2,1)S(1)} %pad_maximum_fusion.plain.rest_0_), channel_id=1, source_target_pairs={{7,0},{2,1},{1,2},{4,3},{3,4},{6,5},{5,6},{0,7},{15,8},{10,9},{9,1... | collective-permute-start | bytes 1769480 | tf_op jit(solution)/shard_map/ppermute | solution.py:33
  12.7 0.0 copy-start.3
  12.8 0.0 copy-start.5
  12.8 0.0 copy-done.4
  12.8 0.0 copy-done.6
  12.8 0.6 %copy-done.3 = f32[256]{0:T(256)S(1)} copy-done((f32[256]{0:T(256)S(1)}, f32[256]{0:T(256)}, u32[]{:S(2)}) %copy-start.3) | copy-done | bytes 1048
  13.4 0.0 copy-done.5
  13.4 1.0 %frame_sums.1 = (f32[8,128]{1,0:T(8,128)S(1)}, f32[8,256]{1,0:T(8,128)S(1)}, bf16[4,28,16,256]{3,2,1,0:T(8,128)(2,1)S(1)}) custom-call(s32[4]{0:T(128)S(1)} %copy-done.5, s32[4]{0:T(128)S(1)} %copy-done.6, bf16[4,28,16,256]{3,2,1,0:T(8,128)(2,1)S(1)} %copy-done, f32[1,256]{1,0:T(1,128)S(1)} %bitcast.9, f32[1,256]{1,0:T(1,128)S(1)} %bitcast.10), custom_call_target="tpu_custom_call" | custom-call | tf_op jit(solution)/shard_map/frame_sums/pallas_call | solution.py:77
  14.4 1.3 %collective-permute-start.2 = (f32[8,128]{1,0:T(8,128)S(1)}, f32[8,128]{1,0:T(8,128)S(1)}, u32[]{:S(2)}, u32[]{:S(2)}) collective-permute-start(f32[8,128]{1,0:T(8,128)S(1)} %get-tuple-element.19), channel_id=1, source_target_pairs={{16,48},{24,56},{32,0},{40,8},{48,80},{56,88},{64,32},{72,40},{80,... | collective-permute-start | bytes 12296 | tf_op jit(solution)/shard_map/ppermute | solution.py:342
  15.7 3.5 %collective-permute-done.2 = f32[8,128]{1,0:T(8,128)S(1)} collective-permute-done((f32[8,128]{1,0:T(8,128)S(1)}, f32[8,128]{1,0:T(8,128)S(1)}, u32[]{:S(2)}, u32[]{:S(2)}) %collective-permute-start.2) | collective-permute-done | bytes 4128 | tf_op jit(solution)/shard_map/ppermute | solution.py:342
  19.2 0.1 broadcast_select_fusion
  19.3 0.0 collective-permute-done.1.prev
  19.3 0.0 collective-permute-done.rest_1_
  19.3 4.9 %collective-permute-start.3 = (bf16[36,32,256]{2,1,0:T(8,128)(2,1)S(1)}, bf16[36,32,256]{2,1,0:T(8,128)(2,1)}, u32[]{:S(2)}, u32[]{:S(2)}) collective-permute-start(bf16[36,32,256]{2,1,0:T(8,128)(2,1)S(1)} %collective-permute-done.rest_1_), channel_id=1, source_target_pairs={{6,0},{3,1},{0,2},{5,3},{2,4},{7,5},{4,6},{1,7},{14,8},{11,9},{8,1... | collective-permute-start | bytes 1769480 | tf_op jit(solution)/shard_map/ppermute | solution.py:33
  24.2 0.1 pad_add_fusion.place
  24.3 0.6 edge_rows.1
  24.9 0.0 copy-start.7
  24.9 0.9 %copy-done.7 = bf16[42,32,256]{2,1,0:T(8,128)(2,1)} copy-done((bf16[42,32,256]{2,1,0:T(8,128)(2,1)}, bf16[42,32,256]{2,1,0:T(8,128)(2,1)S(1)}, u32[]{:S(2)}) %copy-start.7) | copy-done | bytes 688152
  25.8 2.8 %collective-permute-start.5 = (bf16[6,32,256]{2,1,0:T(8,128)(2,1)S(1)}, bf16[6,32,256]{2,1,0:T(8,128)(2,1)S(1)}, u32[]{:S(2)}, u32[]{:S(2)}) collective-permute-start(bf16[6,32,256]{2,1,0:T(8,128)(2,1)S(1)} %get-tuple-element.28), channel_id=1, source_target_pairs={{7,0},{2,1},{1,2},{4,3},{3,4},{6,5},{5,6},{0,7},{15,8},{10,9},{9,1... | collective-permute-start | bytes 294920 | tf_op jit(solution)/shard_map/ppermute | solution.py:33
  28.6 0.0 collective-permute-done.4.rest_2_
  28.6 0.0 copy-start.1
  28.6 0.7 %broadcast_in_dim.2 = f32[32,8,128]{2,1,0:T(8,128)} broadcast(f32[8,128]{1,0:T(8,128)S(1)} %broadcast_select_fusion), dimensions={1,2} | broadcast | bytes 135168 | tf_op jit(solution)/shard_map/broadcast_in_dim | solution.py:359
  29.4 7.2 %all-to-all-start = ((f32[32,8,128]{2,1,0:T(8,128)}), f32[32,8,128]{2,1,0:T(8,128)S(1)}, u32[]{:S(2)}, u32[]{:S(2)}) async-start(f32[32,8,128]{2,1,0:T(8,128)} %broadcast_in_dim.2), calls=%async_computation | async-start | bytes 262144 | tf_op jit(solution)/shard_map/all_to_all | solution.py:358
  36.6 0.0 collective-permute-done.5.edge
  36.6 0.0 copy-done.1
  36.6 2.1 %collective-permute-start.6 = (bf16[42,32,256]{2,1,0:T(8,128)(2,1)}, bf16[42,32,256]{2,1,0:T(8,128)(2,1)S(1)}, u32[]{:S(2)}, u32[]{:S(2)}) collective-permute-start(bf16[42,32,256]{2,1,0:T(8,128)(2,1)} %copy-done.7), channel_id=1, source_target_pairs={{0,1},{1,0},{2,3},{3,2},{4,5},{5,4},{6,7},{7,6},{8,9},{9,8},{10,11... | collective-permute-start | bytes 2064392 | tf_op jit(solution)/shard_map/ppermute | solution.py:23
  38.7 2.2 %collective-permute-start.7 = (bf16[36,32,256]{2,1,0:T(8,128)(2,1)S(1)}, bf16[36,32,256]{2,1,0:T(8,128)(2,1)}, u32[]{:S(2)}, u32[]{:S(2)}) collective-permute-start(bf16[36,32,256]{2,1,0:T(8,128)(2,1)S(1)} %collective-permute-done.rest_1_), channel_id=1, source_target_pairs={{0,1},{1,0},{2,3},{3,2},{4,5},{5,4},{6,7},{7,6},{8,9},{9,8},{10,11... | collective-permute-start | bytes 1769480 | tf_op jit(solution)/shard_map/ppermute | solution.py:23
  40.9 2.1 %collective-permute-start.8 = (bf16[36,32,256]{2,1,0:T(8,128)(2,1)}, bf16[36,32,256]{2,1,0:T(8,128)(2,1)}, u32[]{:S(2)}, u32[]{:S(2)}) collective-permute-start(bf16[36,32,256]{2,1,0:T(8,128)(2,1)} %copy-done.1), channel_id=1, source_target_pairs={{0,1},{1,0},{2,3},{3,2},{4,5},{5,4},{6,7},{7,6},{8,9},{9,8},{10,11... | collective-permute-start | bytes 1769480 | tf_op jit(solution)/shard_map/ppermute | solution.py:23
  43.1 1.1 %all-to-all-done = f32[32,8,128]{2,1,0:T(8,128)S(1)} async-done(((f32[32,8,128]{2,1,0:T(8,128)}), f32[32,8,128]{2,1,0:T(8,128)S(1)}, u32[]{:S(2)}, u32[]{:S(2)}) %all-to-all-start) | async-done | bytes 131104 | tf_op jit(solution)/shard_map/all_to_all | solution.py:358
  44.2 0.0 collective-permute-done.3.rest_3_
  44.2 2.3 %collective-permute-start.9 = (bf16[36,32,256]{2,1,0:T(8,128)(2,1)}, bf16[36,32,256]{2,1,0:T(8,128)(2,1)S(1)}, u32[]{:S(2)}, u32[]{:S(2)}) collective-permute-start(bf16[36,32,256]{2,1,0:T(8,128)(2,1)} %collective-permute-done.3.rest_3_), channel_id=1, source_target_pairs={{0,1},{1,0},{2,3},{3,2},{4,5},{5,4},{6,7},{7,6},{8,9},{9,8},{10,11... | collective-permute-start | bytes 1769480 | tf_op jit(solution)/shard_map/ppermute | solution.py:23
  46.5 0.0 collective-permute-done.8.rest_6_
  46.5 0.0 collective-permute-done.7.rest_5_
  46.5 0.0 collective-permute-done.6.rest_4_
  46.5 1.8 %collective-permute-done.9.rest_7_ = bf16[36,32,256]{2,1,0:T(8,128)(2,1)S(1)} collective-permute-done((bf16[36,32,256]{2,1,0:T(8,128)(2,1)}, bf16[36,32,256]{2,1,0:T(8,128)(2,1)S(1)}, u32[]{:S(2)}, u32[]{:S(2)}) %collective-permute-start.9) | collective-permute-done | bytes 589856 | tf_op jit(solution)/shard_map/ppermute | solution.py:23
  48.3 0.0 copy-start.2
  48.3 1.1 %copy-done.2 = bf16[36,32,256]{2,1,0:T(8,128)(2,1)S(1)} copy-done((bf16[36,32,256]{2,1,0:T(8,128)(2,1)S(1)}, bf16[36,32,256]{2,1,0:T(8,128)(2,1)}, u32[]{:S(2)}) %copy-start.2) | copy-done | bytes 589848
  49.4 13.3 %norm_conv_down.1 = bf16[448,256]{1,0:T(8,128)(2,1)} custom-call(s32[2]{0:T(128)S(1)} %pad_add_fusion.place, f32[4,8,8,128]{3,2,1,0:T(8,128)S(1)} %bitcast.8, f32[8,256]{1,0:T(8,128)S(1)} %get-tuple-element.24.params, bf16[4,28,16,256]{3,2,1,0:T(8,128)(2,1)S(1)} %get-tuple-element.25.feat, bf16[2,28,16,256]{3,2,1,0:T(8,128)(2,1)S(1)} %collective-permute-done.1.prev, ...), custom_call_target="tpu_custom_call" | custom-call | tf_op jit(solution)/shard_map/norm_conv_down/pallas_call | solution.py:296
  (2 shorter events, 0.0 us)
Async XLA Ops:
  0.0 6.4 %copy-start = (bf16[4,28,16,256]{3,2,1,0:T(8,128)(2,1)S(1)}, bf16[4,28,16,256]{3,2,1,0:T(8,128)(2,1)}, u32[]{:S(2)}) copy-start(bf16[4,28,16,256]{3,2,1,0:T(8,128)(2,1)} %feat.1) | copy-start | bytes 2752516
  1.2 18.1 %collective-permute-start = (bf16[36,32,256]{2,1,0:T(8,128)(2,1)S(1)}, bf16[36,32,256]{2,1,0:T(8,128)(2,1)S(1)}, u32[]{:S(2)}, u32[]{:S(2)}) collective-permute-start(bf16[36,32,256]{2,1,0:T(8,128)(2,1)S(1)} %pad_maximum_fusion.plain.rest_0_), channel_id=1, source_target_pairs={{6,0},{3,1},{0,2},{5,3},{2,4},{7,5},{4,6},{1,7},{14,8},{11,9},{8,1... | collective-permute-start | bytes 1769480 | tf_op jit(solution)/shard_map/ppermute | solution.py:33
  6.5 6.3 %copy-start.4 = (f32[256]{0:T(256)S(1)}, f32[256]{0:T(256)}, u32[]{:S(2)}) copy-start(f32[256]{0:T(256)} %param.11) | copy-start | bytes 3076
  6.5 6.3 %copy-start.6 = (s32[4]{0:T(128)S(1)}, s32[4]{0:T(128)}, u32[]{:S(2)}) copy-start(s32[4]{0:T(128)} %valid.1) | copy-start | bytes 52
  6.5 12.8 %collective-permute-start.1 = (bf16[2,28,16,256]{3,2,1,0:T(8,128)(2,1)S(1)}, bf16[2,28,16,256]{3,2,1,0:T(8,128)(2,1)S(1)}, u32[]{:S(2)}, u32[]{:S(2)}) collective-permute-start(bf16[2,28,16,256]{3,2,1,0:T(8,128)(2,1)S(1)} %slice.3), channel_id=1, source_target_pairs={{0,8},{8,16},{16,24},{24,32},{32,40},{40,48},{48,56},{56,64},{64,7... | collective-permute-start | bytes 1376264 | tf_op jit(solution)/shard_map/ppermute | solution.py:19
  9.8 18.9 %collective-permute-start.4 = (bf16[36,32,256]{2,1,0:T(8,128)(2,1)S(1)}, bf16[36,32,256]{2,1,0:T(8,128)(2,1)S(1)}, u32[]{:S(2)}, u32[]{:S(2)}) collective-permute-start(bf16[36,32,256]{2,1,0:T(8,128)(2,1)S(1)} %pad_maximum_fusion.plain.rest_0_), channel_id=1, source_target_pairs={{7,0},{2,1},{1,2},{4,3},{3,4},{6,5},{5,6},{0,7},{15,8},{10,9},{9,1... | collective-permute-start | bytes 1769480 | tf_op jit(solution)/shard_map/ppermute | solution.py:33
  12.7 0.7 %copy-start.3 = (f32[256]{0:T(256)S(1)}, f32[256]{0:T(256)}, u32[]{:S(2)}) copy-start(f32[256]{0:T(256)} %param.10) | copy-start | bytes 3076
  12.8 0.7 %copy-start.5 = (s32[4]{0:T(128)S(1)}, s32[4]{0:T(128)}, u32[]{:S(2)}) copy-start(s32[4]{0:T(128)} %ids.1) | copy-start | bytes 52
  14.4 4.8 %collective-permute-start.2 = (f32[8,128]{1,0:T(8,128)S(1)}, f32[8,128]{1,0:T(8,128)S(1)}, u32[]{:S(2)}, u32[]{:S(2)}) collective-permute-start(f32[8,128]{1,0:T(8,128)S(1)} %get-tuple-element.19), channel_id=1, source_target_pairs={{16,48},{24,56},{32,0},{40,8},{48,80},{56,88},{64,32},{72,40},{80,... | collective-permute-start | bytes 12296 | tf_op jit(solution)/shard_map/ppermute | solution.py:342
  19.3 24.9 %collective-permute-start.3 = (bf16[36,32,256]{2,1,0:T(8,128)(2,1)S(1)}, bf16[36,32,256]{2,1,0:T(8,128)(2,1)}, u32[]{:S(2)}, u32[]{:S(2)}) collective-permute-start(bf16[36,32,256]{2,1,0:T(8,128)(2,1)S(1)} %collective-permute-done.rest_1_), channel_id=1, source_target_pairs={{6,0},{3,1},{0,2},{5,3},{2,4},{7,5},{4,6},{1,7},{14,8},{11,9},{8,1... | collective-permute-start | bytes 1769480 | tf_op jit(solution)/shard_map/ppermute | solution.py:33
  24.9 0.9 %copy-start.7 = (bf16[42,32,256]{2,1,0:T(8,128)(2,1)}, bf16[42,32,256]{2,1,0:T(8,128)(2,1)S(1)}, u32[]{:S(2)}) copy-start(bf16[42,32,256]{2,1,0:T(8,128)(2,1)S(1)} %get-tuple-element.32) | copy-start | bytes 2064388
  25.8 10.8 %collective-permute-start.5 = (bf16[6,32,256]{2,1,0:T(8,128)(2,1)S(1)}, bf16[6,32,256]{2,1,0:T(8,128)(2,1)S(1)}, u32[]{:S(2)}, u32[]{:S(2)}) collective-permute-start(bf16[6,32,256]{2,1,0:T(8,128)(2,1)S(1)} %get-tuple-element.28), channel_id=1, source_target_pairs={{7,0},{2,1},{1,2},{4,3},{3,4},{6,5},{5,6},{0,7},{15,8},{10,9},{9,1... | collective-permute-start | bytes 294920 | tf_op jit(solution)/shard_map/ppermute | solution.py:33
  28.6 8.0 %copy-start.1 = (bf16[36,32,256]{2,1,0:T(8,128)(2,1)}, bf16[36,32,256]{2,1,0:T(8,128)(2,1)S(1)}, u32[]{:S(2)}) copy-start(bf16[36,32,256]{2,1,0:T(8,128)(2,1)S(1)} %collective-permute-done.4.rest_2_) | copy-start | bytes 1769476
  29.4 14.8 %all-to-all-start = ((f32[32,8,128]{2,1,0:T(8,128)}), f32[32,8,128]{2,1,0:T(8,128)S(1)}, u32[]{:S(2)}, u32[]{:S(2)}) async-start(f32[32,8,128]{2,1,0:T(8,128)} %broadcast_in_dim.2), calls=%async_computation | async-start | bytes 262144 | tf_op jit(solution)/shard_map/all_to_all | solution.py:358
  36.6 9.9 %collective-permute-start.6 = (bf16[42,32,256]{2,1,0:T(8,128)(2,1)}, bf16[42,32,256]{2,1,0:T(8,128)(2,1)S(1)}, u32[]{:S(2)}, u32[]{:S(2)}) collective-permute-start(bf16[42,32,256]{2,1,0:T(8,128)(2,1)} %copy-done.7), channel_id=1, source_target_pairs={{0,1},{1,0},{2,3},{3,2},{4,5},{5,4},{6,7},{7,6},{8,9},{9,8},{10,11... | collective-permute-start | bytes 2064392 | tf_op jit(solution)/shard_map/ppermute | solution.py:23
  38.7 7.8 %collective-permute-start.7 = (bf16[36,32,256]{2,1,0:T(8,128)(2,1)S(1)}, bf16[36,32,256]{2,1,0:T(8,128)(2,1)}, u32[]{:S(2)}, u32[]{:S(2)}) collective-permute-start(bf16[36,32,256]{2,1,0:T(8,128)(2,1)S(1)} %collective-permute-done.rest_1_), channel_id=1, source_target_pairs={{0,1},{1,0},{2,3},{3,2},{4,5},{5,4},{6,7},{7,6},{8,9},{9,8},{10,11... | collective-permute-start | bytes 1769480 | tf_op jit(solution)/shard_map/ppermute | solution.py:23
  40.9 5.6 %collective-permute-start.8 = (bf16[36,32,256]{2,1,0:T(8,128)(2,1)}, bf16[36,32,256]{2,1,0:T(8,128)(2,1)}, u32[]{:S(2)}, u32[]{:S(2)}) collective-permute-start(bf16[36,32,256]{2,1,0:T(8,128)(2,1)} %copy-done.1), channel_id=1, source_target_pairs={{0,1},{1,0},{2,3},{3,2},{4,5},{5,4},{6,7},{7,6},{8,9},{9,8},{10,11... | collective-permute-start | bytes 1769480 | tf_op jit(solution)/shard_map/ppermute | solution.py:23
  44.2 4.1 %collective-permute-start.9 = (bf16[36,32,256]{2,1,0:T(8,128)(2,1)}, bf16[36,32,256]{2,1,0:T(8,128)(2,1)S(1)}, u32[]{:S(2)}, u32[]{:S(2)}) collective-permute-start(bf16[36,32,256]{2,1,0:T(8,128)(2,1)} %collective-permute-done.3.rest_3_), channel_id=1, source_target_pairs={{0,1},{1,0},{2,3},{3,2},{4,5},{5,4},{6,7},{7,6},{8,9},{9,8},{10,11... | collective-permute-start | bytes 1769480 | tf_op jit(solution)/shard_map/ppermute | solution.py:23
  48.3 1.1 %copy-start.2 = (bf16[36,32,256]{2,1,0:T(8,128)(2,1)S(1)}, bf16[36,32,256]{2,1,0:T(8,128)(2,1)}, u32[]{:S(2)}) copy-start(bf16[36,32,256]{2,1,0:T(8,128)(2,1)} %copy-done.1) | copy-start | bytes 1769476

commit v8 on v7

--- a/solution.py
+++ b/solution.py
@@ -231,22 +231,18 @@
 
     out_rows = height + 1
     lane_parts = channels // 128
-    ids_all = [before_ids[f : f + 1] for f in range(2)]
-    ids_all = ids_all + [own_ids[f : f + 1] for f in range(frames)]
+    hcol[frames + 2] = jnp.zeros(hcol.shape[1:], BF16)
+    ids_all = [before_ids[f, 0] for f in range(2)] + [own_ids[f, 0] for f in range(frames)]
     for t in range(frames):
         total = None
-        for dt in (2, 1, 0):
-            part = None
+        for dt in range(3):
+            at = jnp.where(ids_all[t + dt] == ids_all[t + 2], t + dt, frames + 2)
             for dr in range(3):
-                lhs = hcol[t + dt, dr : dr + out_rows].reshape(out_rows * across, 3 * channels)
+                lhs = hcol[at, dr : dr + out_rows].reshape(out_rows * across, 3 * channels)
                 tap = (dt * 3 + dr) * 3
                 rhs = w_all[tap : tap + 3].reshape(3 * channels, channels)
                 product = jnp.dot(lhs, rhs, preferred_element_type=F32)
-                part = product if part is None else part + product
-            if dt == 2:
-                total = part
-            else:
-                total = total + jnp.where(ids_all[t + dt] == ids_all[t + 2], part, 0.0)
+                total = product if total is None else total + product
         weight = own_valid[t : t + 1]
         body_rows = height * across
         main_rows = feat[t].astype(F32).reshape(body_rows, channels) + total[:body_rows]
@@ -301,13 +297,13 @@
         out_specs=vmem,
         scratch_shapes=[
             pltpu.VMEM((taps, channels, channels), BF16),
-            pltpu.VMEM((frames + 2, height + 3, across, 3 * channels), BF16),
+            pltpu.VMEM((frames + 3, height + 3, across, 3 * channels), BF16),
             pltpu.VMEM((channels // 128, frames, height // 2 + 1, 2, across, 128), F32),
             pltpu.VMEM((frames + 2, 1, across, channels), BF16),
             pltpu.VMEM((frames + 2, 2, across, channels), BF16),
             pltpu.SemaphoreType.DMA((8,)),
         ],
-        compiler_params=pltpu.CompilerParams(vmem_limit_bytes=24 << 20),
+        compiler_params=pltpu.CompilerParams(vmem_limit_bytes=20 << 20),
         name="norm_conv_down",
     )(place, block, params, feat, prev, edge, *pieces)
 

time: 63.3 us -> 63.2 us (level)
  no operation moved by 1% of the time
where the time goes in v8:
time: 63.2 us; the launch traced here: 62.7 us
  starting transfers between devices  36.4 us (58%)
  Pallas kernels  14.9 us (24%)
  waiting for transfers between devices  6.41 us (10%)
  local copies, waits for them, and re-layouts  3.35 us (5%)
  other arithmetic  1.37 us (2%)
    ppermute x4, starting transfers between devices, ring_move(): return lax.ppermute(value, axis, pairs)  15.9 us
    pallas_call x1, Pallas kernels, main_call(): pl.pallas_call(main_kernel, out_shape=jax.ShapeDtypeStruct((points, chann...  13.3 us
    ppermute x4, starting transfers between devices, swapped(): lax.ppermute(value, axis, [(i, i ^ bits) for i in range(lax.axis_size(axi...  8.78 us
    all_to_all x1, starting transfers between devices, body(): lax.all_to_all(jnp.broadcast_to(rows[None], (size, *rows.shape)), ('tm',...  7.21 us
    ppermute x1, waiting for transfers between devices, body(): lax.ppermute(table, 'tm', [pair for pair in pairs if 0 <= pair[1] < times])  3.49 us
    ppermute x1, starting transfers between devices, shifted(): lax.ppermute(value, axis, [(source, source + steps) for source in range(f...  3.23 us
    unnamed x16, local copies, waits for them, and re-layouts  2.6 us
    ppermute x4, waiting for transfers between devices, swapped(): lax.ppermute(value, axis, [(i, i ^ bits) for i in range(lax.axis_size(axi...  1.8 us
  transfers between devices with their start and end apart: 11, of which 3 were waited for; matrix products, arithmetic and copies ran while one was open for 1% of the time, Pallas kernels for 3%

profile of v8, /device:TPU:1, one launch (start us, length us, event | category | flops | bytes accessed | tf_op | source)
XLA Modules:
  0.0 62.7 jit_solution(6258277579495571362)
XLA Ops:
  0.0 0.0 copy-start
  0.0 1.2 %pad_maximum_fusion.plain.rest_0_ = bf16[36,32,256]{2,1,0:T(8,128)(2,1)S(1)} fusion(bf16[9,32,256]{2,1,0:T(8,128)(2,1)} %bitcast.12, bf16[27,32,256]{2,1,0:T(8,128)(2,1)} %bitcast.11), kind=kLoop, calls=%fused_computation | loop fusion | flops 294912 | bytes 1179648 | tf_op jit(solution)/shard_map/concatenate | solution.py:319
  1.2 5.2 %collective-permute-start = (bf16[36,32,256]{2,1,0:T(8,128)(2,1)S(1)}, bf16[36,32,256]{2,1,0:T(8,128)(2,1)S(1)}, u32[]{:S(2)}, u32[]{:S(2)}) collective-permute-start(bf16[36,32,256]{2,1,0:T(8,128)(2,1)S(1)} %pad_maximum_fusion.plain.rest_0_), channel_id=1, source_target_pairs={{6,0},{3,1},{0,2},{5,3},{2,4},{7,5},{4,6},{1,7},{14,8},{11,9},{8,1... | collective-permute-start | bytes 1769480 | tf_op jit(solution)/shard_map/ppermute | solution.py:33
  6.4 0.0 copy-done
  6.5 0.0 copy-start.4
  6.5 0.0 copy-start.6
  6.5 3.2 %collective-permute-start.1 = (bf16[2,28,16,256]{3,2,1,0:T(8,128)(2,1)S(1)}, bf16[2,28,16,256]{3,2,1,0:T(8,128)(2,1)S(1)}, u32[]{:S(2)}, u32[]{:S(2)}) collective-permute-start(bf16[2,28,16,256]{3,2,1,0:T(8,128)(2,1)S(1)} %slice.3), channel_id=1, source_target_pairs={{0,8},{8,16},{16,24},{24,32},{32,40},{40,48},{48,56},{56,64},{64,7... | collective-permute-start | bytes 1376264 | tf_op jit(solution)/shard_map/ppermute | solution.py:19
  9.8 3.0 %collective-permute-start.4 = (bf16[36,32,256]{2,1,0:T(8,128)(2,1)S(1)}, bf16[36,32,256]{2,1,0:T(8,128)(2,1)S(1)}, u32[]{:S(2)}, u32[]{:S(2)}) collective-permute-start(bf16[36,32,256]{2,1,0:T(8,128)(2,1)S(1)} %pad_maximum_fusion.plain.rest_0_), channel_id=1, source_target_pairs={{7,0},{2,1},{1,2},{4,3},{3,4},{6,5},{5,6},{0,7},{15,8},{10,9},{9,1... | collective-permute-start | bytes 1769480 | tf_op jit(solution)/shard_map/ppermute | solution.py:33
  12.7 0.0 copy-start.3
  12.8 0.0 copy-start.5
  12.8 0.0 copy-done.4
  12.8 0.0 copy-done.6
  12.8 0.6 %copy-done.3 = f32[256]{0:T(256)S(1)} copy-done((f32[256]{0:T(256)S(1)}, f32[256]{0:T(256)}, u32[]{:S(2)}) %copy-start.3) | copy-done | bytes 1048
  13.4 0.0 copy-done.5
  13.4 1.0 %frame_sums.1 = (f32[8,128]{1,0:T(8,128)S(1)}, f32[8,256]{1,0:T(8,128)S(1)}, bf16[4,28,16,256]{3,2,1,0:T(8,128)(2,1)S(1)}) custom-call(s32[4]{0:T(128)S(1)} %copy-done.5, s32[4]{0:T(128)S(1)} %copy-done.6, bf16[4,28,16,256]{3,2,1,0:T(8,128)(2,1)S(1)} %copy-done, f32[1,256]{1,0:T(1,128)S(1)} %bitcast.9, f32[1,256]{1,0:T(1,128)S(1)} %bitcast.10), custom_call_target="tpu_custom_call" | custom-call | tf_op jit(solution)/shard_map/frame_sums/pallas_call | solution.py:77
  14.4 1.3 %collective-permute-start.2 = (f32[8,128]{1,0:T(8,128)S(1)}, f32[8,128]{1,0:T(8,128)S(1)}, u32[]{:S(2)}, u32[]{:S(2)}) collective-permute-start(f32[8,128]{1,0:T(8,128)S(1)} %get-tuple-element.19), channel_id=1, source_target_pairs={{16,48},{24,56},{32,0},{40,8},{48,80},{56,88},{64,32},{72,40},{80,... | collective-permute-start | bytes 12296 | tf_op jit(solution)/shard_map/ppermute | solution.py:338
  15.7 3.5 %collective-permute-done.2 = f32[8,128]{1,0:T(8,128)S(1)} collective-permute-done((f32[8,128]{1,0:T(8,128)S(1)}, f32[8,128]{1,0:T(8,128)S(1)}, u32[]{:S(2)}, u32[]{:S(2)}) %collective-permute-start.2) | collective-permute-done | bytes 4128 | tf_op jit(solution)/shard_map/ppermute | solution.py:338
  19.2 0.1 broadcast_select_fusion
  19.3 0.0 collective-permute-done.1.prev
  19.3 0.0 collective-permute-done.rest_1_
  19.3 4.9 %collective-permute-start.3 = (bf16[36,32,256]{2,1,0:T(8,128)(2,1)S(1)}, bf16[36,32,256]{2,1,0:T(8,128)(2,1)}, u32[]{:S(2)}, u32[]{:S(2)}) collective-permute-start(bf16[36,32,256]{2,1,0:T(8,128)(2,1)S(1)} %collective-permute-done.rest_1_), channel_id=1, source_target_pairs={{6,0},{3,1},{0,2},{5,3},{2,4},{7,5},{4,6},{1,7},{14,8},{11,9},{8,1... | collective-permute-start | bytes 1769480 | tf_op jit(solution)/shard_map/ppermute | solution.py:33
  24.2 0.1 pad_add_fusion.place
  24.3 0.6 edge_rows.1
  24.9 0.0 copy-start.7
  24.9 0.9 %copy-done.7 = bf16[42,32,256]{2,1,0:T(8,128)(2,1)} copy-done((bf16[42,32,256]{2,1,0:T(8,128)(2,1)}, bf16[42,32,256]{2,1,0:T(8,128)(2,1)S(1)}, u32[]{:S(2)}) %copy-start.7) | copy-done | bytes 688152
  25.8 2.8 %collective-permute-start.5 = (bf16[6,32,256]{2,1,0:T(8,128)(2,1)S(1)}, bf16[6,32,256]{2,1,0:T(8,128)(2,1)S(1)}, u32[]{:S(2)}, u32[]{:S(2)}) collective-permute-start(bf16[6,32,256]{2,1,0:T(8,128)(2,1)S(1)} %get-tuple-element.28), channel_id=1, source_target_pairs={{7,0},{2,1},{1,2},{4,3},{3,4},{6,5},{5,6},{0,7},{15,8},{10,9},{9,1... | collective-permute-start | bytes 294920 | tf_op jit(solution)/shard_map/ppermute | solution.py:33
  28.6 0.0 collective-permute-done.4.rest_2_
  28.6 0.0 copy-start.1
  28.6 0.7 %broadcast_in_dim.2 = f32[32,8,128]{2,1,0:T(8,128)} broadcast(f32[8,128]{1,0:T(8,128)S(1)} %broadcast_select_fusion), dimensions={1,2} | broadcast | bytes 135168 | tf_op jit(solution)/shard_map/broadcast_in_dim | solution.py:355
  29.4 7.2 %all-to-all-start = ((f32[32,8,128]{2,1,0:T(8,128)}), f32[32,8,128]{2,1,0:T(8,128)S(1)}, u32[]{:S(2)}, u32[]{:S(2)}) async-start(f32[32,8,128]{2,1,0:T(8,128)} %broadcast_in_dim.2), calls=%async_computation | async-start | bytes 262144 | tf_op jit(solution)/shard_map/all_to_all | solution.py:354
  36.6 0.0 collective-permute-done.5.edge
  36.6 0.0 copy-done.1
  36.6 2.1 %collective-permute-start.6 = (bf16[42,32,256]{2,1,0:T(8,128)(2,1)}, bf16[42,32,256]{2,1,0:T(8,128)(2,1)S(1)}, u32[]{:S(2)}, u32[]{:S(2)}) collective-permute-start(bf16[42,32,256]{2,1,0:T(8,128)(2,1)} %copy-done.7), channel_id=1, source_target_pairs={{0,1},{1,0},{2,3},{3,2},{4,5},{5,4},{6,7},{7,6},{8,9},{9,8},{10,11... | collective-permute-start | bytes 2064392 | tf_op jit(solution)/shard_map/ppermute | solution.py:23
  38.7 2.2 %collective-permute-start.7 = (bf16[36,32,256]{2,1,0:T(8,128)(2,1)S(1)}, bf16[36,32,256]{2,1,0:T(8,128)(2,1)}, u32[]{:S(2)}, u32[]{:S(2)}) collective-permute-start(bf16[36,32,256]{2,1,0:T(8,128)(2,1)S(1)} %collective-permute-done.rest_1_), channel_id=1, source_target_pairs={{0,1},{1,0},{2,3},{3,2},{4,5},{5,4},{6,7},{7,6},{8,9},{9,8},{10,11... | collective-permute-start | bytes 1769480 | tf_op jit(solution)/shard_map/ppermute | solution.py:23
  40.9 2.1 %collective-permute-start.8 = (bf16[36,32,256]{2,1,0:T(8,128)(2,1)}, bf16[36,32,256]{2,1,0:T(8,128)(2,1)}, u32[]{:S(2)}, u32[]{:S(2)}) collective-permute-start(bf16[36,32,256]{2,1,0:T(8,128)(2,1)} %copy-done.1), channel_id=1, source_target_pairs={{0,1},{1,0},{2,3},{3,2},{4,5},{5,4},{6,7},{7,6},{8,9},{9,8},{10,11... | collective-permute-start | bytes 1769480 | tf_op jit(solution)/shard_map/ppermute | solution.py:23
  43.1 1.1 %all-to-all-done = f32[32,8,128]{2,1,0:T(8,128)S(1)} async-done(((f32[32,8,128]{2,1,0:T(8,128)}), f32[32,8,128]{2,1,0:T(8,128)S(1)}, u32[]{:S(2)}, u32[]{:S(2)}) %all-to-all-start) | async-done | bytes 131104 | tf_op jit(solution)/shard_map/all_to_all | solution.py:354
  44.2 0.0 collective-permute-done.3.rest_3_
  44.2 2.3 %collective-permute-start.9 = (bf16[36,32,256]{2,1,0:T(8,128)(2,1)}, bf16[36,32,256]{2,1,0:T(8,128)(2,1)S(1)}, u32[]{:S(2)}, u32[]{:S(2)}) collective-permute-start(bf16[36,32,256]{2,1,0:T(8,128)(2,1)} %collective-permute-done.3.rest_3_), channel_id=1, source_target_pairs={{0,1},{1,0},{2,3},{3,2},{4,5},{5,4},{6,7},{7,6},{8,9},{9,8},{10,11... | collective-permute-start | bytes 1769480 | tf_op jit(solution)/shard_map/ppermute | solution.py:23
  46.5 0.0 collective-permute-done.8.rest_6_
  46.5 0.0 collective-permute-done.7.rest_5_
  46.5 0.0 collective-permute-done.6.rest_4_
  46.5 1.8 %collective-permute-done.9.rest_7_ = bf16[36,32,256]{2,1,0:T(8,128)(2,1)S(1)} collective-permute-done((bf16[36,32,256]{2,1,0:T(8,128)(2,1)}, bf16[36,32,256]{2,1,0:T(8,128)(2,1)S(1)}, u32[]{:S(2)}, u32[]{:S(2)}) %collective-permute-start.9) | collective-permute-done | bytes 589856 | tf_op jit(solution)/shard_map/ppermute | solution.py:23
  48.3 0.0 copy-start.2
  48.3 1.1 %copy-done.2 = bf16[36,32,256]{2,1,0:T(8,128)(2,1)S(1)} copy-done((bf16[36,32,256]{2,1,0:T(8,128)(2,1)S(1)}, bf16[36,32,256]{2,1,0:T(8,128)(2,1)}, u32[]{:S(2)}) %copy-start.2) | copy-done | bytes 589848
  49.4 13.3 %norm_conv_down.1 = bf16[448,256]{1,0:T(8,128)(2,1)} custom-call(s32[2]{0:T(128)S(1)} %pad_add_fusion.place, f32[4,8,8,128]{3,2,1,0:T(8,128)S(1)} %bitcast.8, f32[8,256]{1,0:T(8,128)S(1)} %get-tuple-element.24.params, bf16[4,28,16,256]{3,2,1,0:T(8,128)(2,1)S(1)} %get-tuple-element.25.feat, bf16[2,28,16,256]{3,2,1,0:T(8,128)(2,1)S(1)} %collective-permute-done.1.prev, ...), custom_call_target="tpu_custom_call" | custom-call | tf_op jit(solution)/shard_map/norm_conv_down/pallas_call | solution.py:292
  (2 shorter events, 0.0 us)
Async XLA Ops:
  0.0 6.4 %copy-start = (bf16[4,28,16,256]{3,2,1,0:T(8,128)(2,1)S(1)}, bf16[4,28,16,256]{3,2,1,0:T(8,128)(2,1)}, u32[]{:S(2)}) copy-start(bf16[4,28,16,256]{3,2,1,0:T(8,128)(2,1)} %feat.1) | copy-start | bytes 2752516
  1.2 18.1 %collective-permute-start = (bf16[36,32,256]{2,1,0:T(8,128)(2,1)S(1)}, bf16[36,32,256]{2,1,0:T(8,128)(2,1)S(1)}, u32[]{:S(2)}, u32[]{:S(2)}) collective-permute-start(bf16[36,32,256]{2,1,0:T(8,128)(2,1)S(1)} %pad_maximum_fusion.plain.rest_0_), channel_id=1, source_target_pairs={{6,0},{3,1},{0,2},{5,3},{2,4},{7,5},{4,6},{1,7},{14,8},{11,9},{8,1... | collective-permute-start | bytes 1769480 | tf_op jit(solution)/shard_map/ppermute | solution.py:33
  6.5 6.3 %copy-start.4 = (f32[256]{0:T(256)S(1)}, f32[256]{0:T(256)}, u32[]{:S(2)}) copy-start(f32[256]{0:T(256)} %param.11) | copy-start | bytes 3076
  6.5 6.3 %copy-start.6 = (s32[4]{0:T(128)S(1)}, s32[4]{0:T(128)}, u32[]{:S(2)}) copy-start(s32[4]{0:T(128)} %valid.1) | copy-start | bytes 52
  6.5 12.8 %collective-permute-start.1 = (bf16[2,28,16,256]{3,2,1,0:T(8,128)(2,1)S(1)}, bf16[2,28,16,256]{3,2,1,0:T(8,128)(2,1)S(1)}, u32[]{:S(2)}, u32[]{:S(2)}) collective-permute-start(bf16[2,28,16,256]{3,2,1,0:T(8,128)(2,1)S(1)} %slice.3), channel_id=1, source_target_pairs={{0,8},{8,16},{16,24},{24,32},{32,40},{40,48},{48,56},{56,64},{64,7... | collective-permute-start | bytes 1376264 | tf_op jit(solution)/shard_map/ppermute | solution.py:19
  9.8 18.9 %collective-permute-start.4 = (bf16[36,32,256]{2,1,0:T(8,128)(2,1)S(1)}, bf16[36,32,256]{2,1,0:T(8,128)(2,1)S(1)}, u32[]{:S(2)}, u32[]{:S(2)}) collective-permute-start(bf16[36,32,256]{2,1,0:T(8,128)(2,1)S(1)} %pad_maximum_fusion.plain.rest_0_), channel_id=1, source_target_pairs={{7,0},{2,1},{1,2},{4,3},{3,4},{6,5},{5,6},{0,7},{15,8},{10,9},{9,1... | collective-permute-start | bytes 1769480 | tf_op jit(solution)/shard_map/ppermute | solution.py:33
  12.7 0.7 %copy-start.3 = (f32[256]{0:T(256)S(1)}, f32[256]{0:T(256)}, u32[]{:S(2)}) copy-start(f32[256]{0:T(256)} %param.10) | copy-start | bytes 3076
  12.8 0.7 %copy-start.5 = (s32[4]{0:T(128)S(1)}, s32[4]{0:T(128)}, u32[]{:S(2)}) copy-start(s32[4]{0:T(128)} %ids.1) | copy-start | bytes 52
  14.4 4.8 %collective-permute-start.2 = (f32[8,128]{1,0:T(8,128)S(1)}, f32[8,128]{1,0:T(8,128)S(1)}, u32[]{:S(2)}, u32[]{:S(2)}) collective-permute-start(f32[8,128]{1,0:T(8,128)S(1)} %get-tuple-element.19), channel_id=1, source_target_pairs={{16,48},{24,56},{32,0},{40,8},{48,80},{56,88},{64,32},{72,40},{80,... | collective-permute-start | bytes 12296 | tf_op jit(solution)/shard_map/ppermute | solution.py:338
  19.3 24.9 %collective-permute-start.3 = (bf16[36,32,256]{2,1,0:T(8,128)(2,1)S(1)}, bf16[36,32,256]{2,1,0:T(8,128)(2,1)}, u32[]{:S(2)}, u32[]{:S(2)}) collective-permute-start(bf16[36,32,256]{2,1,0:T(8,128)(2,1)S(1)} %collective-permute-done.rest_1_), channel_id=1, source_target_pairs={{6,0},{3,1},{0,2},{5,3},{2,4},{7,5},{4,6},{1,7},{14,8},{11,9},{8,1... | collective-permute-start | bytes 1769480 | tf_op jit(solution)/shard_map/ppermute | solution.py:33
  24.9 0.9 %copy-start.7 = (bf16[42,32,256]{2,1,0:T(8,128)(2,1)}, bf16[42,32,256]{2,1,0:T(8,128)(2,1)S(1)}, u32[]{:S(2)}) copy-start(bf16[42,32,256]{2,1,0:T(8,128)(2,1)S(1)} %get-tuple-element.32) | copy-start | bytes 2064388
  25.8 10.8 %collective-permute-start.5 = (bf16[6,32,256]{2,1,0:T(8,128)(2,1)S(1)}, bf16[6,32,256]{2,1,0:T(8,128)(2,1)S(1)}, u32[]{:S(2)}, u32[]{:S(2)}) collective-permute-start(bf16[6,32,256]{2,1,0:T(8,128)(2,1)S(1)} %get-tuple-element.28), channel_id=1, source_target_pairs={{7,0},{2,1},{1,2},{4,3},{3,4},{6,5},{5,6},{0,7},{15,8},{10,9},{9,1... | collective-permute-start | bytes 294920 | tf_op jit(solution)/shard_map/ppermute | solution.py:33
  28.6 8.0 %copy-start.1 = (bf16[36,32,256]{2,1,0:T(8,128)(2,1)}, bf16[36,32,256]{2,1,0:T(8,128)(2,1)S(1)}, u32[]{:S(2)}) copy-start(bf16[36,32,256]{2,1,0:T(8,128)(2,1)S(1)} %collective-permute-done.4.rest_2_) | copy-start | bytes 1769476
  29.4 14.8 %all-to-all-start = ((f32[32,8,128]{2,1,0:T(8,128)}), f32[32,8,128]{2,1,0:T(8,128)S(1)}, u32[]{:S(2)}, u32[]{:S(2)}) async-start(f32[32,8,128]{2,1,0:T(8,128)} %broadcast_in_dim.2), calls=%async_computation | async-start | bytes 262144 | tf_op jit(solution)/shard_map/all_to_all | solution.py:354
  36.6 9.9 %collective-permute-start.6 = (bf16[42,32,256]{2,1,0:T(8,128)(2,1)}, bf16[42,32,256]{2,1,0:T(8,128)(2,1)S(1)}, u32[]{:S(2)}, u32[]{:S(2)}) collective-permute-start(bf16[42,32,256]{2,1,0:T(8,128)(2,1)} %copy-done.7), channel_id=1, source_target_pairs={{0,1},{1,0},{2,3},{3,2},{4,5},{5,4},{6,7},{7,6},{8,9},{9,8},{10,11... | collective-permute-start | bytes 2064392 | tf_op jit(solution)/shard_map/ppermute | solution.py:23
  38.7 7.8 %collective-permute-start.7 = (bf16[36,32,256]{2,1,0:T(8,128)(2,1)S(1)}, bf16[36,32,256]{2,1,0:T(8,128)(2,1)}, u32[]{:S(2)}, u32[]{:S(2)}) collective-permute-start(bf16[36,32,256]{2,1,0:T(8,128)(2,1)S(1)} %collective-permute-done.rest_1_), channel_id=1, source_target_pairs={{0,1},{1,0},{2,3},{3,2},{4,5},{5,4},{6,7},{7,6},{8,9},{9,8},{10,11... | collective-permute-start | bytes 1769480 | tf_op jit(solution)/shard_map/ppermute | solution.py:23
  40.9 5.6 %collective-permute-start.8 = (bf16[36,32,256]{2,1,0:T(8,128)(2,1)}, bf16[36,32,256]{2,1,0:T(8,128)(2,1)}, u32[]{:S(2)}, u32[]{:S(2)}) collective-permute-start(bf16[36,32,256]{2,1,0:T(8,128)(2,1)} %copy-done.1), channel_id=1, source_target_pairs={{0,1},{1,0},{2,3},{3,2},{4,5},{5,4},{6,7},{7,6},{8,9},{9,8},{10,11... | collective-permute-start | bytes 1769480 | tf_op jit(solution)/shard_map/ppermute | solution.py:23
  44.2 4.1 %collective-permute-start.9 = (bf16[36,32,256]{2,1,0:T(8,128)(2,1)}, bf16[36,32,256]{2,1,0:T(8,128)(2,1)S(1)}, u32[]{:S(2)}, u32[]{:S(2)}) collective-permute-start(bf16[36,32,256]{2,1,0:T(8,128)(2,1)} %collective-permute-done.3.rest_3_), channel_id=1, source_target_pairs={{0,1},{1,0},{2,3},{3,2},{4,5},{5,4},{6,7},{7,6},{8,9},{9,8},{10,11... | collective-permute-start | bytes 1769480 | tf_op jit(solution)/shard_map/ppermute | solution.py:23
  48.3 1.1 %copy-start.2 = (bf16[36,32,256]{2,1,0:T(8,128)(2,1)S(1)}, bf16[36,32,256]{2,1,0:T(8,128)(2,1)}, u32[]{:S(2)}) copy-start(bf16[36,32,256]{2,1,0:T(8,128)(2,1)} %copy-done.1) | copy-start | bytes 1769476
